TPU v7x, 128 devices: a whole 4x4x4 slice. The times are simulated.
128 devices in a mesh: dp: 32 (over y, z, core), seq: 4 (over x).
Axes of the slice: x: 4, y: 4, z: 4, core: 2. Of those that a mesh axis runs over, the one named last changes fastest.
Arguments:
- layer_input: bfloat16 [32, 1024, 1152], P('dp', 'seq'), may hold values from -10 to 10
- out_grad: bfloat16 [32, 1024, 1152], P('dp', 'seq'), may hold values from -6 to 6
- segment_ids: int32 [32, 1024], P('dp'), may hold values from 0 to 254, as said below
- adapter_ids: int32 [32], P('dp'), may hold values from 0 to 7
- gain_attn_in: float32 [1152], replicated, may hold values from 0.25 to 1.75
- gain_attn_out: float32 [1152], replicated, may hold values from 0.25 to 1.75
- gain_mlp_in: float32 [1152], replicated, may hold values from 0.25 to 1.75
- gain_mlp_out: float32 [1152], replicated, may hold values from 0.25 to 1.75
- w_query: bfloat16 [1152, 1024], P(None, 'dp'), may hold values from -2 to 2
- w_key: bfloat16 [1152, 256], P(None, 'dp'), may hold values from -2 to 2
- w_value: bfloat16 [1152, 256], P(None, 'dp'), may hold values from -2 to 2
- w_out: bfloat16 [1024, 1152], P('dp'), may hold values from -0.1875 to 0.1875
- w_gate: bfloat16 [1152, 6912], P(None, 'dp'), may hold values from -0.1875 to 0.1875
- w_up: bfloat16 [1152, 6912], P(None, 'dp'), may hold values from -0.1875 to 0.1875
- w_down: bfloat16 [6912, 1152], P('dp'), may hold values from -0.078125 to 0.078125
- qkv_adapt_in: bfloat16 [8, 3, 16, 1152], replicated, may hold values from -0.1875 to 0.1875
- q_adapt_out: bfloat16 [8, 16, 1024], replicated, may hold values from -0.75 to 0.75
- kv_adapt_out: bfloat16 [8, 2, 16, 256], replicated, may hold values from -0.75 to 0.75
- o_adapt_in: bfloat16 [8, 16, 1024], replicated, may hold values from -0.1875 to 0.1875
- o_adapt_out: bfloat16 [8, 16, 1152], replicated, may hold values from -0.75 to 0.75
- mlp_adapt_in: bfloat16 [8, 2, 16, 1152], replicated, may hold values from -0.1875 to 0.1875
- mlp_adapt_out: bfloat16 [8, 2, 16, 6912], replicated, may hold values from -0.75 to 0.75
- down_adapt_in: bfloat16 [8, 16, 6912], replicated, may hold values from -0.078125 to 0.078125
- down_adapt_out: bfloat16 [8, 16, 1152], replicated, may hold values from -0.75 to 0.75
Outputs:
- layer_output: bfloat16 [32, 1024, 1152], P('dp', 'seq')
- input_grad: bfloat16 [32, 1024, 1152], P('dp', 'seq')
- grad_qkv_adapt_in: float32 [8, 3, 16, 1152], replicated
- grad_q_adapt_out: float32 [8, 16, 1024], replicated
- grad_kv_adapt_out: float32 [8, 2, 16, 256], replicated
- grad_o_adapt_in: float32 [8, 16, 1024], replicated
- grad_o_adapt_out: float32 [8, 16, 1152], replicated
- grad_mlp_adapt_in: float32 [8, 2, 16, 1152], replicated
- grad_mlp_adapt_out: float32 [8, 2, 16, 6912], replicated
- grad_down_adapt_in: float32 [8, 16, 6912], replicated
- grad_down_adapt_out: float32 [8, 16, 1152], replicated
Inputs may be any that keep to these rules, and one draw needn't show every extreme that they name: `segment_ids`: within each sequence the segment numbers start at 0, never fall and rise by at most one from token to token; each sequence holds one document of at least 770 tokens.
All inputs are finite; a program needn't handle non-finite values.
Results may differ from a plain program's by a relative error of at most 0.024.
Values may be sent and summed in bfloat16 or wider, within the bound.
A program may use at most 256 MiB of HBM per device.

v0:
```python
import jax
import jax.numpy as jnp
from jax import lax
from jax.sharding import PartitionSpec as P

epsilon = 1e-06
softcap = 50.0
masked_value = -1000000000.0
highest = lax.Precision.HIGHEST


def normed(values, gain_vector):
    return values * lax.rsqrt(jnp.mean(values * values, -1, keepdims=True) + epsilon) * gain_vector


def norm_back(values, gain_vector, cotangent):
    _, pull = jax.vjp(normed, values, gain_vector)
    return pull(cotangent)[0]


def geglu(gate_act, upward):
    return jax.nn.gelu(gate_act, approximate=True) * upward


def project(inputs, weight, down_sel, up_sel):
    latent = jnp.einsum(
        "sli,sri->slr", inputs, down_sel, preferred_element_type=jnp.float32
    ).astype(jnp.bfloat16)
    result = jnp.einsum("sli,io->slo", inputs, weight, preferred_element_type=jnp.float32)
    result = result + jnp.einsum("slr,sro->slo", latent, up_sel, preferred_element_type=jnp.float32)
    return (result, latent)


def project_back(grad_rows, weight, down_sel, up_sel, inputs, latent):
    latent_grad = jnp.einsum(
        "slo,sro->slr", grad_rows, up_sel, preferred_element_type=jnp.float32
    ).astype(jnp.bfloat16)
    input_cot = jnp.einsum("slo,io->sli", grad_rows, weight, preferred_element_type=jnp.float32)
    input_cot = input_cot + jnp.einsum(
        "slr,sri->sli", latent_grad, down_sel, preferred_element_type=jnp.float32
    )
    up_part = jnp.einsum("slr,slo->sro", latent, grad_rows, preferred_element_type=jnp.float32)
    down_part = jnp.einsum("slr,sli->sri", latent_grad, inputs, preferred_element_type=jnp.float32)
    return (input_cot, down_part, up_part)


def allowed_mask(segments, row_start, block_rows):
    length = segments.shape[0]
    query_seg = segments[row_start : row_start + block_rows]
    query_pos = row_start + jnp.arange(block_rows, dtype=jnp.int32)
    key_pos = jnp.arange(length, dtype=jnp.int32)
    return ((query_seg[:, None] == segments[None, :]) & (key_pos[None, :] <= query_pos[:, None]))[
        None
    ]


def capped_scores(query_block, key_rows, score_scale):
    raw_scores = jnp.einsum(
        "bhe,ke->hbk", query_block, key_rows, preferred_element_type=jnp.float32
    )
    bent_part = jnp.tanh(raw_scores * (score_scale / softcap))
    return (softcap * bent_part, bent_part)


def attend(queries, key_rows, value_rows, segment_rows, score_scale):
    members, length = (queries.shape[0], queries.shape[1])
    block_rows = min(512, length)
    outputs, log_totals = ([], [])
    out_blocks = []
    total_blocks = []
    for row_start in range(0, length, block_rows):
        query_block = queries[0, row_start : row_start + block_rows]
        capped, _ = capped_scores(query_block, key_rows[0], score_scale)
        allowed = allowed_mask(segment_rows[0], row_start, block_rows)
        shown_scores = jnp.where(allowed, capped, masked_value)
        row_peak = jnp.max(shown_scores, -1, keepdims=True)
        exponent = jnp.where(allowed, jnp.exp(shown_scores - row_peak), 0.0)
        row_total = jnp.sum(exponent, -1, keepdims=True)
        probabilities = (exponent / row_total).astype(jnp.bfloat16)
        out_blocks.append(
            jnp.einsum(
                "hbk,ke->bhe", probabilities, value_rows[0], preferred_element_type=jnp.float32
            ).astype(jnp.bfloat16)
        )
        total_blocks.append(row_peak + jnp.log(row_total))
    outputs.append(jnp.concatenate(out_blocks, 0))
    log_totals.append(jnp.concatenate(total_blocks, 1))
    return (jnp.stack(outputs), jnp.stack(log_totals))


def attend_back(queries, key_rows, value_rows, segment_rows, log_totals, head_grads, score_scale):
    members, length = (queries.shape[0], queries.shape[1])
    block_rows = min(512, length)
    query_grads, key_parts, value_parts = ([], [], [])
    query_blocks = []
    key_part = jnp.zeros(key_rows.shape[1:], jnp.float32)
    value_part = jnp.zeros(value_rows.shape[1:], jnp.float32)
    for row_start in range(0, length, block_rows):
        query_block = queries[0, row_start : row_start + block_rows]
        grad_block = head_grads[0, row_start : row_start + block_rows]
        capped, bent_part = capped_scores(query_block, key_rows[0], score_scale)
        allowed = allowed_mask(segment_rows[0], row_start, block_rows)
        shown_scores = jnp.where(allowed, capped, masked_value)
        block_totals = log_totals[0][:, row_start : row_start + block_rows]
        probabilities = jnp.where(allowed, jnp.exp(shown_scores - block_totals), 0.0)
        prob_grad = jnp.einsum(
            "bhe,ke->hbk", grad_block, value_rows[0], preferred_element_type=jnp.float32
        )
        centre = jnp.sum(probabilities * prob_grad, -1, keepdims=True)
        raw_grad = (
            probabilities * (prob_grad - centre) * (1.0 - bent_part * bent_part) * score_scale
        ).astype(jnp.bfloat16)
        query_blocks.append(
            jnp.einsum(
                "hbk,ke->bhe", raw_grad, key_rows[0], preferred_element_type=jnp.float32
            ).astype(jnp.bfloat16)
        )
        key_part = key_part + jnp.einsum(
            "hbk,bhe->ke", raw_grad, query_block, preferred_element_type=jnp.float32
        )
        value_part = value_part + jnp.einsum(
            "hbk,bhe->ke",
            probabilities.astype(jnp.bfloat16),
            grad_block,
            preferred_element_type=jnp.float32,
        )
    query_grads.append(jnp.concatenate(query_blocks, 0))
    key_parts.append(key_part)
    value_parts.append(value_part)
    return (jnp.stack(query_grads), jnp.stack(key_parts), jnp.stack(value_parts))


def body(
    layer_input,
    out_grad,
    segment_ids,
    adapter_ids,
    gain_attn_in,
    gain_attn_out,
    gain_mlp_in,
    gain_mlp_out,
    w_query,
    w_key,
    w_value,
    w_out,
    w_gate,
    w_up,
    w_down,
    qkv_adapt_in,
    q_adapt_out,
    kv_adapt_out,
    o_adapt_in,
    o_adapt_out,
    mlp_adapt_in,
    mlp_adapt_out,
    down_adapt_in,
    down_adapt_out,
):
    members, local_len = (layer_input.shape[0], layer_input.shape[1])
    query_full, key_full, value_full, out_full = (
        lax.all_gather(w_query, "dp", axis=1, tiled=True),
        lax.all_gather(w_key, "dp", axis=1, tiled=True),
        lax.all_gather(w_value, "dp", axis=1, tiled=True),
        lax.all_gather(w_out, "dp", axis=0, tiled=True),
    )
    gate_full, up_full, down_full = (
        lax.all_gather(w_gate, "dp", axis=1, tiled=True),
        lax.all_gather(w_up, "dp", axis=1, tiled=True),
        lax.all_gather(w_down, "dp", axis=0, tiled=True),
    )
    head_dim = key_full.shape[1]
    head_count = query_full.shape[1] // head_dim
    score_scale = head_dim ** (-0.5)
    tables = (
        qkv_adapt_in,
        q_adapt_out,
        kv_adapt_out,
        o_adapt_in,
        o_adapt_out,
        mlp_adapt_in,
        mlp_adapt_out,
        down_adapt_in,
        down_adapt_out,
    )
    adapter_count = qkv_adapt_in.shape[0]
    chooser = adapter_ids[:, None] == jnp.arange(adapter_count, dtype=jnp.int32)[None, :]
    pick_rows = chooser.astype(jnp.bfloat16)
    picked = [
        lax.dot_general(
            pick_rows, adapter_table, (((1,), (0,)), ((), ())), preferred_element_type=jnp.float32
        ).astype(jnp.bfloat16)
        for adapter_table in tables
    ]
    qkv_in, q_out, kv_out, o_in, o_out, mlp_in, mlp_out, down_in, down_out = picked
    input_rows = layer_input.astype(jnp.float32)
    first_norm = normed(input_rows, gain_attn_in).astype(jnp.bfloat16)
    query_proj, query_latent = project(first_norm, query_full, qkv_in[:, 0], q_out)
    key_proj, key_latent = project(first_norm, key_full, qkv_in[:, 1], kv_out[:, 0])
    value_proj, value_latent = project(first_norm, value_full, qkv_in[:, 2], kv_out[:, 1])
    query_rows = query_proj.astype(jnp.bfloat16).reshape(members, local_len, head_count, head_dim)
    head_queries = lax.all_to_all(query_rows, "seq", split_axis=2, concat_axis=1, tiled=True)
    all_keys, all_values = (
        lax.all_gather(key_proj.astype(jnp.bfloat16), "seq", axis=1, tiled=True),
        lax.all_gather(value_proj.astype(jnp.bfloat16), "seq", axis=1, tiled=True),
    )
    context, log_totals = attend(head_queries, all_keys, all_values, segment_ids, score_scale)
    context_rows = lax.all_to_all(context, "seq", split_axis=1, concat_axis=2, tiled=True).reshape(
        members, local_len, head_count * head_dim
    )
    attn_proj, out_latent = project(context_rows, out_full, o_in, o_out)
    mixed = input_rows + normed(attn_proj, gain_attn_out)
    second_norm = normed(mixed, gain_mlp_in).astype(jnp.bfloat16)
    gate_proj, gate_latent = project(second_norm, gate_full, mlp_in[:, 0], mlp_out[:, 0])
    up_proj, up_latent = project(second_norm, up_full, mlp_in[:, 1], mlp_out[:, 1])
    hidden = geglu(gate_proj, up_proj).astype(jnp.bfloat16)
    down_proj, down_latent = project(hidden, down_full, down_in, down_out)
    layer_output = (mixed + normed(down_proj, gain_mlp_out)).astype(jnp.bfloat16)
    query_back, key_back, value_back, out_back = (
        lax.all_gather(w_query, "dp", axis=1, tiled=True),
        lax.all_gather(w_key, "dp", axis=1, tiled=True),
        lax.all_gather(w_value, "dp", axis=1, tiled=True),
        lax.all_gather(w_out, "dp", axis=0, tiled=True),
    )
    gate_back, up_back, down_back = (
        lax.all_gather(w_gate, "dp", axis=1, tiled=True),
        lax.all_gather(w_up, "dp", axis=1, tiled=True),
        lax.all_gather(w_down, "dp", axis=0, tiled=True),
    )
    cotangent = out_grad.astype(jnp.float32)
    down_grad = norm_back(down_proj, gain_mlp_out, cotangent).astype(jnp.bfloat16)
    hidden_grad, down_in_grad, down_out_grad = project_back(
        down_grad, down_back, down_in, down_out, hidden, down_latent
    )
    _, geglu_pull = jax.vjp(geglu, gate_proj, up_proj)
    gate_grad, upward_grad = geglu_pull(hidden_grad)
    gate_cot, gate_in_grad, gate_out_grad = project_back(
        gate_grad.astype(jnp.bfloat16),
        gate_back,
        mlp_in[:, 0],
        mlp_out[:, 0],
        second_norm,
        gate_latent,
    )
    upward_cot, up_in_grad, up_out_grad = project_back(
        upward_grad.astype(jnp.bfloat16),
        up_back,
        mlp_in[:, 1],
        mlp_out[:, 1],
        second_norm,
        up_latent,
    )
    mixed_grad = cotangent + norm_back(mixed, gain_mlp_in, gate_cot + upward_cot)
    attn_grad = norm_back(attn_proj, gain_attn_out, mixed_grad).astype(jnp.bfloat16)
    context_cot, o_in_grad, o_out_grad = project_back(
        attn_grad, out_back, o_in, o_out, context_rows, out_latent
    )
    grad_rows = context_cot.astype(jnp.bfloat16).reshape(members, local_len, head_count, head_dim)
    head_grads = lax.all_to_all(grad_rows, "seq", split_axis=2, concat_axis=1, tiled=True)
    query_grads, key_parts, value_parts = attend_back(
        head_queries, all_keys, all_values, segment_ids, log_totals, head_grads, score_scale
    )
    query_cot_rows = lax.all_to_all(
        query_grads, "seq", split_axis=1, concat_axis=2, tiled=True
    ).reshape(members, local_len, head_count * head_dim)
    key_sum, value_sum = (
        lax.psum_scatter(
            key_parts.astype(jnp.bfloat16), "seq", scatter_dimension=1, tiled=True
        ).astype(jnp.float32),
        lax.psum_scatter(
            value_parts.astype(jnp.bfloat16), "seq", scatter_dimension=1, tiled=True
        ).astype(jnp.float32),
    )
    query_cot, query_in_grad, query_out_grad = project_back(
        query_cot_rows, query_back, qkv_in[:, 0], q_out, first_norm, query_latent
    )
    key_cot, key_in_grad, key_out_grad = project_back(
        key_sum.astype(jnp.bfloat16), key_back, qkv_in[:, 1], kv_out[:, 0], first_norm, key_latent
    )
    value_cot, value_in_grad, value_out_grad = project_back(
        value_sum.astype(jnp.bfloat16),
        value_back,
        qkv_in[:, 2],
        kv_out[:, 1],
        first_norm,
        value_latent,
    )
    input_grad = (
        mixed_grad + norm_back(input_rows, gain_attn_in, query_cot + key_cot + value_cot)
    ).astype(jnp.bfloat16)
    picked_grads = (
        jnp.stack([query_in_grad, key_in_grad, value_in_grad], 1),
        query_out_grad,
        jnp.stack([key_out_grad, value_out_grad], 1),
        o_in_grad,
        o_out_grad,
        jnp.stack([gate_in_grad, up_in_grad], 1),
        jnp.stack([gate_out_grad, up_out_grad], 1),
        down_in_grad,
        down_out_grad,
    )
    chooser_float = chooser.astype(jnp.float32)
    local_grads = tuple(
        (
            lax.dot_general(
                chooser_float,
                picked_grad,
                (((0,), (0,)), ((), ())),
                precision=highest,
                preferred_element_type=jnp.float32,
            )
            for picked_grad in picked_grads
        )
    )
    summed = lax.psum(local_grads, ("dp", "seq"))
    return (
        layer_output,
        input_grad,
        summed[0],
        summed[1],
        summed[2],
        summed[3],
        summed[4],
        summed[5],
        summed[6],
        summed[7],
        summed[8],
    )


def solution(mesh):
    placed = (
        P("dp", "seq", None),
        P("dp", "seq", None),
        P("dp", None),
        P("dp"),
        P(),
        P(),
        P(),
        P(),
        P(None, "dp"),
        P(None, "dp"),
        P(None, "dp"),
        P("dp", None),
        P(None, "dp"),
        P(None, "dp"),
        P("dp", None),
        P(),
        P(),
        P(),
        P(),
        P(),
        P(),
        P(),
        P(),
        P(),
    )
    return jax.shard_map(
        body,
        mesh=mesh,
        in_specs=placed,
        out_specs=(
            P("dp", "seq", None),
            P("dp", "seq", None),
            P(),
            P(),
            P(),
            P(),
            P(),
            P(),
            P(),
            P(),
            P(),
        ),
        check_vma=False,
    )
```

profile of v0, /device:TPU:1, one launch (start us, length us, event | category | flops | bytes accessed | tf_op | source)
XLA Modules:
  0.0 710.9 jit_solution(2763164076712794579)
XLA Ops:
  12.4 1.5 fusion.63
  14.0 27.7 %all_gather.36 = bf16[1152,256]{0,1:T(8,128)(2,1)S(1)} all-gather(bf16[1152,8]{0,1:T(8,128)(2,1)} %param.33), channel_id=1, replica_groups=mesh['dp'=32,'seq'=4] {'dp'}, dimensions={1}, use_global_device_ids=true | all-gather | bytes 608256 | tf_op jit(solution)/shard_map/all_gather | solution.py:162
  41.7 24.2 %all_gather.34 = bf16[1152,256]{0,1:T(8,128)(2,1)S(1)} all-gather(bf16[1152,8]{0,1:T(8,128)(2,1)S(1)} %copy-done.100), channel_id=1, replica_groups=mesh['dp'=32,'seq'=4] {'dp'}, dimensions={1}, use_global_device_ids=true | all-gather | bytes 608256 | tf_op jit(solution)/shard_map/all_gather | solution.py:163
  68.0 11.9 %all-gather.1 = bf16[1024,256]{1,0:T(8,128)(2,1)} all-gather(bf16[256,256]{1,0:T(8,128)(2,1)S(1)} %fusion.53), channel_id=3, replica_groups=mesh['dp'=32,'seq'=4] {'seq'}, dimensions={0}, use_global_device_ids=true | all-gather | bytes 655360 | tf_op jit(solution)/shard_map/all_gather | solution.py:203
  86.8 5.1 fusion.7
  91.9 2.8 fusion.149
  96.3 3.5 all-to-all-start
  99.8 14.8 %all-gather = bf16[1024,256]{1,0:T(8,128)(2,1)} all-gather(bf16[256,256]{1,0:T(8,128)(2,1)S(1)} %copy-done.60), channel_id=2, replica_groups=mesh['dp'=32,'seq'=4] {'seq'}, dimensions={0}, use_global_device_ids=true | all-gather | bytes 655360 | tf_op jit(solution)/shard_map/all_gather | solution.py:204
  116.1 3.6 fusion.24
  121.3 2.0 fusion.26
  126.9 3.8 reduce.16
  131.7 3.7 all-to-all-start.1
  137.2 5.1 all-to-all-done.1
  144.3 2.7 multiply_reduce_fusion.2
  149.0 27.6 %all-gather.12.cloned.1.call-done = bf16[1152,6912]{0,1:T(8,128)(2,1)} async-done(((bf16[1152,216]{0,1:T(8,128)(2,1)}), bf16[1152,6912]{0,1:T(8,128)(2,1)}) %all-gather.12.cloned.1.call-update) | async-done | bytes 15925264 | tf_op jit(solution)/shard_map/all_gather | solution.py:167
  176.6 16.0 %fusion.150 = f32[256,6912]{1,0:T(8,128)} fusion(bf16[256,1152]{1,0:T(8,128)(2,1)S(1)} %fusion.67, bf16[1152,6912]{0,1:T(8,128)(2,1)} %all-gather.12.cloned.1.call-done), kind=kOutput, calls=%fused_computation.280 | convolution fusion | flops 4076863488 | bytes 23592960 | tf_op jit(solution)/shard_map/sli,io->slo/dot_general | solution.py:29
  192.6 7.2 %convolution_add_fusion.2 = f32[256,6912]{1,0:T(8,128)} fusion(f32[256,6912]{1,0:T(8,128)} %fusion.150, bf16[256,16]{0,1:T(8,128)(2,1)S(1)} %convolution_convert_fusion.14, bf16[1,2,16,6912]{3,2,1,0:T(8,128)(2,1)S(1)} %copy-done.36), kind=kOutput, calls=%fused_computation.4 | convolution fusion | flops 58392576 | bytes 14385152 | tf_op jit(solution)/shard_map/slr,sro->slo/dot_general | solution.py:30
  199.8 49.2 %all-gather.14.cloned.1.call-done = bf16[1152,6912]{0,1:T(8,128)(2,1)} async-done(((bf16[1152,216]{0,1:T(8,128)(2,1)}), bf16[1152,6912]{0,1:T(8,128)(2,1)}) %all-gather.14.cloned.1.call-update) | async-done | bytes 15925264 | tf_op jit(solution)/shard_map/all_gather | solution.py:168
  249.0 16.0 %fusion.151 = f32[256,6912]{1,0:T(8,128)} fusion(bf16[256,1152]{1,0:T(8,128)(2,1)S(1)} %fusion.67, bf16[1152,6912]{0,1:T(8,128)(2,1)} %all-gather.14.cloned.1.call-done), kind=kOutput, calls=%fused_computation.281 | convolution fusion | flops 4076863488 | bytes 23592960 | tf_op jit(solution)/shard_map/sli,io->slo/dot_general | solution.py:29
  265.0 8.8 %multiply_convert_fusion.1 = (bf16[256,6912]{1,0:T(8,128)(2,1)S(1)}, f32[256,6912]{1,0:T(8,128)}) fusion(f32[256,6912]{1,0:T(8,128)} %convolution_add_fusion.2, f32[256,6912]{1,0:T(8,128)} %fusion.151, bf16[256,16]{0,1:T(8,128)(2,1)S(1)} %convolution_convert_fusion.13, bf16[1,2,16,6912]{3,2,1,0:T(8,128)(2,1)} %copy.122), kind=kOutput, calls=%fused_computation.15 | convolution fusion | flops 76087296 | bytes 25001984 | tf_op jit(solution)/shard_map/slr,sro->slo/dot_general | solution.py:30
  273.8 1.7 convolution_convert_fusion.8
  275.5 45.9 %all-gather.16.cloned.1.call-done = bf16[6912,1152]{1,0:T(8,128)(2,1)} async-done(((bf16[216,1152]{1,0:T(8,128)(2,1)}), bf16[6912,1152]{1,0:T(8,128)(2,1)}) %all-gather.16.cloned.1.call-update) | async-done | bytes 15925264 | tf_op jit(solution)/shard_map/all_gather | solution.py:169
  321.4 8.8 %fusion.152 = f32[256,1152]{1,0:T(8,128)S(1)} fusion(bf16[256,6912]{1,0:T(8,128)(2,1)S(1)} %get-tuple-element.47, bf16[6912,1152]{1,0:T(8,128)(2,1)} %all-gather.16.cloned.1.call-done), kind=kOutput, calls=%fused_computation.282 | convolution fusion | flops 4076863488 | bytes 20643840 | tf_op jit(solution)/shard_map/sli,io->slo/dot_general | solution.py:29
  335.2 13.4 %fusion.153 = f32[256,6912]{1,0:T(8,128)} fusion(bf16[256,1152]{1,0:T(8,128)(2,1)} %copy-done.28, bf16[6912,1152]{1,0:T(8,128)(2,1)} %all-gather.16.cloned.1.call-done), kind=kOutput, calls=%fused_computation.283 | convolution fusion | flops 4076863488 | bytes 23592960 | tf_op jit(solution)/shard_map/slo,io->sli/dot_general | solution.py:38
  348.6 11.8 %multiply_convert_fusion = (bf16[256,6912]{1,0:T(8,128)(2,1)S(1)}, bf16[256,6912]{1,0:T(8,128)(2,1)S(1)}) fusion(f32[256,6912]{1,0:T(8,128)} %convolution_add_fusion.2, f32[256,6912]{1,0:T(8,128)} %get-tuple-element.48, f32[256,6912]{1,0:T(8,128)} %fusion.153, bf16[256,16]{0,1:T(8,128)(2,1)S(1)} %convolution_convert_fusion.12, bf16[1,16,6912]{2,0,1:T(2,128)(2,1)} %fusion.24), kind=kOutput, calls=%fused_computation.14 | convolution fusion | flops 100859904 | bytes 28540928 | tf_op jit(solution)/shard_map/slr,sri->sli/dot_general | solution.py:39
  365.2 8.5 %fusion.154 = f32[256,1152]{1,0:T(8,128)S(1)} fusion(bf16[256,6912]{1,0:T(8,128)(2,1)S(1)} %get-tuple-element.31, bf16[1152,6912]{0,1:T(8,128)(2,1)} %all-gather.12.cloned.1.call-done), kind=kOutput, calls=%fused_computation.284 | convolution fusion | flops 4076863488 | bytes 20643840 | tf_op jit(solution)/shard_map/slo,io->sli/dot_general | solution.py:38
  374.4 4.9 fusion.155
  388.6 3.9 all-to-all-start.2
  395.2 3.7 broadcast_multiply_fusion
  398.9 2.1 broadcast_multiply_fusion.1
  402.2 1.8 fusion.85
  404.1 2.3 fusion.57
  406.5 1.8 fusion.34
  408.3 4.1 fusion.18
  412.5 2.9 fusion.55
  417.8 4.7 reduce.17
  422.5 2.1 reshape.973
  424.7 4.2 all-to-all-start.3
  432.0 5.2 all-to-all-done.3
  437.1 2.2 reshape.974
  442.8 10.0 %reduce-scatter.3.cloned.1.call-done = bf16[1,256,256]{2,1,0:T(8,128)(2,1)} async-done(((bf16[1,1024,256]{2,1,0:T(8,128)(2,1)}), bf16[1,256,256]{2,1,0:T(8,128)(2,1)}) %reduce-scatter.3.cloned.1.call-update) | async-done | bytes 131088 | tf_op jit(solution)/shard_map/reduce_scatter | solution.py:266
  465.4 219.8 %all-reduce.3.cloned.1.call-done = (f32[8,3,16,1152]{3,2,1,0:T(8,128)}, f32[8,16,1024]{2,1,0:T(8,128)}, f32[8,2,16,256]{3,2,1,0:T(8,128)}, f32[8,16,1024]{2,1,0:...) async-done(((f32[8,3,16,1152]{3,2,1,0:T(8,128)}, ...) | async-done | bytes 16056336 | tf_op jit(solution)/shard_map/psum | solution.py:314
  685.2 2.9 copy.136
  688.9 1.8 copy.138
  690.7 1.9 copy.139
  692.6 1.9 copy.140
  695.5 3.6 copy.142
  700.1 1.8 copy.143
  (386 shorter events, 77.1 us)
Async XLA Ops:
  7.2 79.6 %copy-start = (bf16[8,2,16,6912]{3,2,1,0:T(8,128)(2,1)S(1)}, bf16[8,2,16,6912]{3,2,1,0:T(8,128)(2,1)}, u32[]{:S(2)}) copy-start(bf16[8,2,16,6912]{3,2,1,0:T(8,128)(2,1)} %param.45) | copy-start | bytes 10616836
  7.2 84.7 %all-gather.8.cloned.1.call-start = ((), (), s32[]{:S(2)}) async-start(), calls=%async_computation.6 | async-start | bytes 2433024 | tf_op jit(solution)/shard_map/all_gather | solution.py:161
  7.9 136.4 %all-gather.10.cloned.1.call-start = ((), (), s32[]{:S(2)}) async-start(), calls=%async_computation.7 | async-start | bytes 2433024 | tf_op jit(solution)/shard_map/all_gather | solution.py:164
  8.7 167.9 %all-gather.12.cloned.1.call-start = ((), (), s32[]{:S(2)}) async-start(), calls=%async_computation.8 | async-start | bytes 16422912 | tf_op jit(solution)/shard_map/all_gather | solution.py:167
  9.4 239.6 %all-gather.14.cloned.1.call-start = ((), (), s32[]{:S(2)}) async-start(), calls=%async_computation.9 | async-start | bytes 16422912 | tf_op jit(solution)/shard_map/all_gather | solution.py:168
  10.0 56.8 %copy-start.82 = (f32[1152]{0:T(1024)S(1)}, f32[1152]{0:T(1024)}, u32[]{:S(2)}) copy-start(f32[1152]{0:T(1024)} %param.28) | copy-start | bytes 13828
  10.0 311.4 %all-gather.16.cloned.1.call-start = ((), (), s32[]{:S(2)}) async-start(), calls=%async_computation.10 | async-start | bytes 16422912 | tf_op jit(solution)/shard_map/all_gather | solution.py:169
  10.6 31.1 %copy-start.100 = (bf16[1152,8]{0,1:T(8,128)(2,1)S(1)}, bf16[1152,8]{0,1:T(8,128)(2,1)}, u32[]{:S(2)}) copy-start(bf16[1152,8]{0,1:T(8,128)(2,1)} %param.34) | copy-start | bytes 55300
  10.6 55.4 %copy-start.11 = (bf16[1,256,1152]{2,1,0:T(8,128)(2,1)S(1)}, bf16[1,256,1152]{2,1,0:T(8,128)(2,1)}, u32[]{:S(2)}) copy-start(bf16[1,256,1152]{2,1,0:T(8,128)(2,1)} %param.24) | copy-start | bytes 1769476
  12.4 72.2 %copy-start.77 = (bf16[1,2,16,256]{3,2,1,0:T(8,128)(2,1)}, bf16[1,2,16,256]{3,2,1,0:T(8,128)(2,1)S(1)}, u32[]{:S(2)}) copy-start(bf16[1,2,16,256]{3,2,1,0:T(8,128)(2,1)S(1)} %copy.125) | copy-start | bytes 49156
  14.0 71.5 %copy-start.52 = (bf16[1,3,16,1152]{3,2,1,0:T(8,128)(2,1)}, bf16[1,3,16,1152]{3,2,1,0:T(8,128)(2,1)S(1)}, u32[]{:S(2)}) copy-start(bf16[1,3,16,1152]{3,2,1,0:T(8,128)(2,1)S(1)} %copy.123) | copy-start | bytes 331780
  41.7 26.0 %copy-start.24 = (bf16[1152,256]{0,1:T(8,128)(2,1)}, bf16[1152,256]{0,1:T(8,128)(2,1)S(1)}, u32[]{:S(2)}) copy-start(bf16[1152,256]{0,1:T(8,128)(2,1)S(1)} %all_gather.36) | copy-start | bytes 1769476
  66.0 18.2 %copy-start.26 = (bf16[1152,256]{0,1:T(8,128)(2,1)}, bf16[1152,256]{0,1:T(8,128)(2,1)S(1)}, u32[]{:S(2)}) copy-start(bf16[1152,256]{0,1:T(8,128)(2,1)S(1)} %all_gather.34) | copy-start | bytes 1769476
  66.8 13.1 %copy-start.113 = (f32[256]{0:T(256)}, f32[256]{0:T(256)S(1)}, u32[]{:S(2)}) copy-start(f32[256]{0:T(256)S(1)} %fusion.111) | copy-start | bytes 3076
  66.8 13.1 %copy-start.96 = (s32[1,1024]{1,0:T(1,128)S(1)}, s32[1,1024]{1,0:T(1,128)}, u32[]{:S(2)}) copy-start(s32[1,1024]{1,0:T(1,128)} %param.26) | copy-start | bytes 12292
  66.8 13.7 %copy-start.75 = (bf16[8,16,1024]{2,1,0:T(8,128)(2,1)S(1)}, bf16[8,16,1024]{2,1,0:T(8,128)(2,1)}, u32[]{:S(2)}) copy-start(bf16[8,16,1024]{2,1,0:T(8,128)(2,1)} %param.40) | copy-start | bytes 786436
  66.8 14.6 %copy-start.76 = (bf16[8,16,1024]{2,1,0:T(8,128)(2,1)S(1)}, bf16[8,16,1024]{2,1,0:T(8,128)(2,1)}, u32[]{:S(2)}) copy-start(bf16[8,16,1024]{2,1,0:T(8,128)(2,1)} %param.42) | copy-start | bytes 786436
  67.0 18.5 %copy-start.2 = (bf16[256,1152]{1,0:T(8,128)(2,1)}, bf16[256,1152]{1,0:T(8,128)(2,1)S(1)}, u32[]{:S(2)}) copy-start(bf16[256,1152]{1,0:T(8,128)(2,1)S(1)} %fusion.68) | copy-start | bytes 1769476
  67.0 15.2 %copy-start.65 = (bf16[8,16,1152]{2,1,0:T(8,128)(2,1)S(1)}, bf16[8,16,1152]{2,1,0:T(8,128)(2,1)}, u32[]{:S(2)}) copy-start(bf16[8,16,1152]{2,1,0:T(8,128)(2,1)} %param.43) | copy-start | bytes 884740
  67.0 16.1 %copy-start.66 = (bf16[8,16,1152]{2,1,0:T(8,128)(2,1)S(1)}, bf16[8,16,1152]{2,1,0:T(8,128)(2,1)}, u32[]{:S(2)}) copy-start(bf16[8,16,1152]{2,1,0:T(8,128)(2,1)} %param.47) | copy-start | bytes 884740
  67.3 14.1 %copy-start.92 = (bf16[256,16]{0,1:T(8,128)(2,1)}, bf16[256,16]{0,1:T(8,128)(2,1)S(1)}, u32[]{:S(2)}) copy-start(bf16[256,16]{0,1:T(8,128)(2,1)S(1)} %convolution_convert_fusion.16) | copy-start | bytes 24580
  80.4 43.7 %copy-start.103 = (s32[1,512]{1,0:T(1,128)}, s32[1,512]{1,0:T(1,128)S(1)}, u32[]{:S(2)}) copy-start(s32[1,512]{1,0:T(1,128)S(1)} %get-tuple-element.36) | copy-start | bytes 6148
  85.7 9.0 %copy-start.84 = (bf16[256,16]{0,1:T(8,128)(2,1)}, bf16[256,16]{0,1:T(8,128)(2,1)S(1)}, u32[]{:S(2)}) copy-start(bf16[256,16]{0,1:T(8,128)(2,1)S(1)} %convolution_convert_fusion.15) | copy-start | bytes 24580
  95.0 19.6 %copy-start.57 = (bf16[1,2,16,1152]{3,0,2,1:T(2,128)(2,1)S(1)}, bf16[1,2,16,1152]{3,0,2,1:T(2,128)(2,1)}, u32[]{:S(2)}) copy-start(bf16[1,2,16,1152]{3,0,2,1:T(2,128)(2,1)} %fusion.71) | copy-start | bytes 221188
  95.1 20.3 %copy-start.39 = (bf16[1,2,16,6912]{3,0,2,1:T(2,128)(2,1)S(1)}, bf16[1,2,16,6912]{3,0,2,1:T(2,128)(2,1)}, u32[]{:S(2)}) copy-start(bf16[1,2,16,6912]{3,0,2,1:T(2,128)(2,1)} %fusion.7) | copy-start | bytes 1327108
  96.3 23.4 %all-to-all-start = ((bf16[1,256,4,256]{3,1,0,2:T(8,128)(2,1)}), bf16[1,256,4,256]{3,1,0,2:T(8,128)(2,1)S(1)}, u32[]{:S(2)}, u32[]{:S(2)}) async-start(bf16[1,256,4,256]{3,1,0,2:T(8,128)(2,1)} %copy.43), calls=%async_computation | async-start | bytes 1048576 | tf_op jit(solution)/shard_map/all_to_all | solution.py:201
  99.8 20.0 %copy-start.42 = (bf16[1024,256]{1,0:T(8,128)(2,1)S(1)}, bf16[1024,256]{1,0:T(8,128)(2,1)}, u32[]{:S(2)}) copy-start(bf16[1024,256]{1,0:T(8,128)(2,1)} %all-gather.1) | copy-start | bytes 1572868
  131.7 10.6 %all-to-all-start.1 = ((bf16[4,2,32768]{2,1,0:T(2,128)(2,1)}), bf16[4,2,32768]{2,1,0:T(2,128)(2,1)S(1)}, u32[]{:S(2)}, u32[]{:S(2)}) async-start(bf16[4,2,32768]{2,1,0:T(2,128)(2,1)} %reshape.971), calls=%async_computation.1 | async-start | bytes 1048576 | tf_op jit(solution)/shard_map/all_to_all | solution.py:207
  148.0 44.6 %copy-start.4 = (f32[1,256,1152]{2,1,0:T(8,128)}, f32[1,256,1152]{2,1,0:T(8,128)S(1)}, u32[]{:S(2)}) copy-start(f32[1,256,1152]{2,1,0:T(8,128)S(1)} %get-tuple-element.29) | copy-start | bytes 3538948
  148.0 44.5 %copy-start.109 = (f32[256]{0:T(256)}, f32[256]{0:T(256)S(1)}, u32[]{:S(2)}) copy-start(f32[256]{0:T(256)S(1)} %get-tuple-element.28) | copy-start | bytes 3076
  148.0 44.5 %copy-start.115 = (f32[256]{0:T(256)}, f32[256]{0:T(256)S(1)}, u32[]{:S(2)}) copy-start(f32[256]{0:T(256)S(1)} %fusion.113) | copy-start | bytes 3076
  148.3 100.7 %copy-start.14 = (bf16[256,1152]{1,0:T(8,128)(2,1)}, bf16[256,1152]{1,0:T(8,128)(2,1)S(1)}, u32[]{:S(2)}) copy-start(bf16[256,1152]{1,0:T(8,128)(2,1)S(1)} %fusion.67) | copy-start | bytes 1769476
  148.7 116.3 %copy-start.90 = (bf16[256,16]{0,1:T(8,128)(2,1)}, bf16[256,16]{0,1:T(8,128)(2,1)S(1)}, u32[]{:S(2)}) copy-start(bf16[256,16]{0,1:T(8,128)(2,1)S(1)} %convolution_convert_fusion.13) | copy-start | bytes 24580
  149.0 43.6 %copy-start.36 = (bf16[1,2,16,6912]{3,2,1,0:T(8,128)(2,1)S(1)}, bf16[1,2,16,6912]{3,2,1,0:T(8,128)(2,1)}, u32[]{:S(2)}) copy-start(bf16[1,2,16,6912]{3,2,1,0:T(8,128)(2,1)} %copy.122) | copy-start | bytes 1327108
  275.5 54.7 %copy-start.79 = (f32[1152]{0:T(1024)S(1)}, f32[1152]{0:T(1024)}, u32[]{:S(2)}) copy-start(f32[1152]{0:T(1024)} %param.31) | copy-start | bytes 13828
  348.6 11.8 %copy-start.37 = (bf16[1,2,16,6912]{3,2,1,0:T(8,128)(2,1)S(1)}, bf16[1,2,16,6912]{3,2,1,0:T(8,128)(2,1)}, u32[]{:S(2)}) copy-start(bf16[1,2,16,6912]{3,2,1,0:T(8,128)(2,1)} %copy.122) | copy-start | bytes 1327108
  363.8 10.3 %slice-start = ((s8[15925248]{0:T(1024)(128)(4,1)}), s8[4194304]{0:T(1024)(128)(4,1)S(1)}, s32[]{:S(2)}) async-start(s8[15925248]{0:T(1024)(128)(4,1)} %bitcast.519), calls=%async_computation.14 | async-start | bytes 8388608
  365.2 9.2 %slice-start.3 = ((s8[15925248]{0:T(1024)(128)(4,1)}), s8[3342336]{0:T(1024)(128)(4,1)S(1)}, s32[]{:S(2)}) async-start(s8[15925248]{0:T(1024)(128)(4,1)} %bitcast.519), calls=%async_computation.17 | async-start | bytes 6684672
  388.6 13.6 %all-to-all-start.2 = ((bf16[1,256,4,256]{3,1,0,2:T(8,128)(2,1)}), bf16[1,256,4,256]{3,1,0,2:T(8,128)(2,1)S(1)}, u32[]{:S(2)}, u32[]{:S(2)}) async-start(bf16[1,256,4,256]{3,1,0,2:T(8,128)(2,1)} %copy.46), calls=%async_computation.2 | async-start | bytes 1048576 | tf_op jit(solution)/shard_map/all_to_all | solution.py:258
  392.6 48.9 %reduce-scatter.5.cloned.1.call-start = ((), (), s32[]{:S(2)}) async-start(), calls=%async_computation.12 | async-start | bytes 655360 | tf_op jit(solution)/shard_map/reduce_scatter | solution.py:269
  417.8 11.1 %copy-start.33 = (bf16[512,1024]{0,1:T(8,128)(2,1)S(1)}, bf16[512,1024]{0,1:T(8,128)(2,1)}, u32[]{:S(2)}) copy-start(bf16[512,1024]{0,1:T(8,128)(2,1)} %copy-done.32) | copy-start | bytes 3145732
  424.7 12.5 %all-to-all-start.3 = ((bf16[4,2,32768]{2,1,0:T(2,128)(2,1)}), bf16[4,2,32768]{2,1,0:T(2,128)(2,1)}, u32[]{:S(2)}, u32[]{:S(2)}) async-start(bf16[4,2,32768]{2,1,0:T(2,128)(2,1)} %reshape.973), calls=%async_computation.3 | async-start | bytes 1048576 | tf_op jit(solution)/shard_map/all_to_all | solution.py:262
  428.9 23.9 %reduce-scatter.3.cloned.1.call-start = ((), (), s32[]{:S(2)}) async-start(), calls=%async_computation.11 | async-start | bytes 655360 | tf_op jit(solution)/shard_map/reduce_scatter | solution.py:266
  431.7 253.5 %all-reduce.3.cloned.1.call-start = ((), (), s32[]{:S(2)}) async-start(), calls=%async_computation.13 | async-start | bytes 32112640 | tf_op jit(solution)/shard_map/psum | solution.py:314
  439.9 14.2 %copy-start.95 = (bf16[256,16]{0,1:T(8,128)(2,1)S(1)}, bf16[256,16]{0,1:T(8,128)(2,1)}, u32[]{:S(2)}) copy-start(bf16[256,16]{0,1:T(8,128)(2,1)} %copy-done.94) | copy-start | bytes 24580
  439.9 15.3 %copy-start.93 = (bf16[256,16]{0,1:T(8,128)(2,1)S(1)}, bf16[256,16]{0,1:T(8,128)(2,1)}, u32[]{:S(2)}) copy-start(bf16[256,16]{0,1:T(8,128)(2,1)} %copy-done.92) | copy-start | bytes 24580
  685.2 9.4 %copy-start.49 = (f32[8,2,16,1152]{3,2,1,0:T(8,128)S(1)}, f32[8,2,16,1152]{3,2,1,0:T(8,128)}, u32[]{:S(2)}) copy-start(f32[8,2,16,1152]{3,2,1,0:T(8,128)} %get-tuple-element.65) | copy-start | bytes 3538948
  685.2 10.4 %copy-start.23 = (f32[8,2,16,6912]{3,2,1,0:T(8,128)S(1)}, f32[8,2,16,6912]{3,2,1,0:T(8,128)}, u32[]{:S(2)}) copy-start(f32[8,2,16,6912]{3,2,1,0:T(8,128)} %get-tuple-element.66) | copy-start | bytes 21233668
  (91 other events, 289.1 us)
Sparse Core Ops, SparseCore 0:
  10.3 48.0 all-gather.7
  60.6 43.6 all-gather.9
  106.5 69.9 all-gather.11
  178.7 70.2 all-gather.13
  251.1 70.2 all-gather.15
  408.4 19.4 reduce-scatter.4
  432.7 20.0 reduce-scatter.2
  460.4 224.7 all-reduce.2
where the time goes:
time: 716 us; the launch traced here: 711 us
  waiting for transfers between devices  366 us (51%)
  matrix products  161 us (22%)
  blocking collectives  78.7 us (11%)
  local copies, waits for them, and re-layouts  40.6 us (6%)
  other arithmetic  32.6 us (5%)
  between operations  16.5 us (2%)
  starting transfers between devices  16 us (2%)
    psum x1, waiting for transfers between devices, body(): summed = lax.psum(local_grads, ('dp', 'seq'))  220 us
    all_gather x1, waiting for transfers between devices, body(): lax.all_gather(w_up, 'dp', axis=1, tiled=True)  49.2 us
    dot_general x7, matrix products, project(): jnp.einsum('sli,io->slo', inputs, weight, preferred_element_type=jnp.floa...  47.1 us
    all_gather x1, waiting for transfers between devices, body(): lax.all_gather(w_down, 'dp', axis=0, tiled=True)  45.9 us
    unnamed x270, local copies, waits for them, and re-layouts  33.9 us
    dot_general x7, matrix products, project_back(): jnp.einsum('slo,io->sli', grad_rows, weight, preferred_element_type=jnp.f...  29.5 us
    all_gather x1, blocking collectives, body(): lax.all_gather(w_key, 'dp', axis=1, tiled=True)  27.7 us
    all_gather x1, waiting for transfers between devices, body(): lax.all_gather(w_gate, 'dp', axis=1, tiled=True)  27.6 us
  transfers between devices with their start and end apart: 12, of which 7 were waited for; matrix products, arithmetic and copies ran while one was open for 18% of the time, Pallas kernels for 0%

commit v1 on v0

v1 whole, which is shorter than its diff:
```python
import functools

import jax
import jax.numpy as jnp
from jax import lax
from jax.experimental import pallas as pl
from jax.experimental.pallas import tpu as pltpu
from jax.sharding import PartitionSpec as P

epsilon = 1e-06
softcap = 50.0
highest = lax.Precision.HIGHEST
MESH = pl.DeviceIdType.MESH
bf16 = jnp.bfloat16
f32 = jnp.float32

D = 1152
SEQ = 4
ROWS = 256
UNITS = 54
BLOCK = 64
TILE = 256
MIB = 1 << 20


def dot(a, b):
    return lax.dot_general(a, b, (((1,), (0,)), ((), ())), preferred_element_type=f32)


def dot_nt(a, b):
    return lax.dot_general(a, b, (((1,), (1,)), ((), ())), preferred_element_type=f32)


def dot_tn(a, b):
    return lax.dot_general(a, b, (((0,), (0,)), ((), ())), preferred_element_type=f32)


def normed(values, gain_vector):
    return values * lax.rsqrt(jnp.mean(values * values, -1, keepdims=True) + epsilon) * gain_vector


def norm_back(values, gain_vector, cotangent):
    inverse = lax.rsqrt(jnp.mean(values * values, -1, keepdims=True) + epsilon)
    scaled = cotangent * gain_vector
    mean_part = jnp.mean(scaled * values, -1, keepdims=True)
    return inverse * (scaled - values * (inverse * inverse * mean_part))


def seq_peers():
    dp, me = lax.axis_index("dp"), lax.axis_index("seq")
    return [(dp, lax.rem(me + shift, SEQ)) for shift in (1, 2, 3)]


def greet(peers):
    barrier = pltpu.get_barrier_semaphore()
    for peer in peers:
        pl.semaphore_signal(barrier, inc=1, device_id=peer, device_id_type=MESH)
    pl.semaphore_wait(barrier, len(peers))


def mlp_kernel(
    tokens, w_gate, w_up, w_down, first_gu, second_gate, second_up, first_down, second_down,
    mixed, out_grad, gain_in, gain_out,
    layer_out, mixed_grad, grad_gate_out, grad_up_out, grad_down_in, grad_gu_in, grad_down_out,
    act_gate, act_up, hidden, latents, down_latents, down_grads, total, thin, thin_gu,
    send_one, recv_one, send_two, recv_two,
    send_sem, recv_sem,
):
    me = lax.axis_index("seq")
    peers = seq_peers()
    steps = w_gate.shape[0]
    greet(peers)

    def forward(chunk):
        rows = tokens[chunk]
        latent = dot_nt(rows, first_gu[...]).astype(bf16)
        latents[chunk] = latent
        total[...] = jnp.zeros_like(total)
        thin[...] = jnp.zeros_like(thin)

        def step(j, _):
            gate = dot_nt(rows, w_gate[j]) + dot(latent, second_gate[j])
            upward = dot_nt(rows, w_up[j]) + dot(latent, second_up[j])
            inner = 0.7978845608028654 * (gate + 0.044715 * (gate * gate * gate))
            bent = jnp.tanh(inner)
            half = 0.5 * (1.0 + bent)
            gelu = gate * half
            slope = half + 0.5 * gate * (1.0 - bent * bent) * (
                0.7978845608028654 * (1.0 + 0.134145 * (gate * gate))
            )
            act_gate[j, chunk] = gelu
            act_up[j, chunk] = upward * slope
            mid = (gelu * upward).astype(bf16)
            hidden[j, chunk] = mid
            total[...] += dot(mid, w_down[j])
            thin[...] += dot_nt(mid, first_down[j])
            return 0

        lax.fori_loop(0, steps, step, 0)
        down_latent = thin[...].astype(bf16)
        down_latents[chunk] = down_latent
        return total[...] + dot(down_latent, second_down[...])

    def copy(src, dst, peer, slot):
        return pltpu.make_async_remote_copy(
            src_ref=src, dst_ref=dst, send_sem=send_sem.at[slot], recv_sem=recv_sem.at[slot],
            device_id=peer, device_id_type=MESH,
        )

    sent = []
    for shift in (2, 1, 3):
        chunk = lax.rem(me + shift, SEQ)
        send_one[shift - 1] = forward(chunk).astype(bf16)
        moving = copy(send_one.at[shift - 1], recv_one.at[shift - 1], peers[shift - 1], shift - 1)
        moving.start()
        sent.append(moving)
    down_proj = forward(me)
    for moving in sent:
        moving.wait()
    for slot in range(3):
        down_proj = down_proj + recv_one[slot].astype(f32)
    cotangent = out_grad[...].astype(f32)
    layer_out[...] = (mixed[...] + normed(down_proj, gain_out[...])).astype(bf16)
    down_grads[me] = norm_back(down_proj, gain_out[...], cotangent).astype(bf16)
    gathered = []
    for shift in (1, 3, 2):
        moving = copy(down_grads.at[me], down_grads.at[me], peers[shift - 1], 2 + shift)
        moving.start()
        gathered.append(moving)

    grad_gate_out[...] = jnp.zeros_like(grad_gate_out)
    grad_up_out[...] = jnp.zeros_like(grad_up_out)
    grad_down_in[...] = jnp.zeros_like(grad_down_in)
    grad_gu_in[...] = jnp.zeros_like(grad_gu_in)
    grad_down_out[...] = jnp.zeros_like(grad_down_out)

    def backward(chunk):
        rows = down_grads[chunk]
        latent = latents[chunk]
        latent_grad = dot_nt(rows, second_down[...]).astype(bf16)
        total[...] = jnp.zeros_like(total)
        thin_gu[...] = jnp.zeros_like(thin_gu)

        def step(j, _):
            hidden_grad = dot_nt(rows, w_down[j]) + dot(latent_grad, first_down[j])
            gate_grad = (hidden_grad * act_up[j, chunk]).astype(bf16)
            up_grad = (hidden_grad * act_gate[j, chunk]).astype(bf16)
            total[...] += dot(gate_grad, w_gate[j]) + dot(up_grad, w_up[j])
            thin_gu[...] += dot_nt(gate_grad, second_gate[j]) + dot_nt(up_grad, second_up[j])
            grad_gate_out[j] += dot_tn(latent, gate_grad)
            grad_up_out[j] += dot_tn(latent, up_grad)
            grad_down_in[j] += dot_tn(latent_grad, hidden[j, chunk])
            return 0

        lax.fori_loop(0, steps, step, 0)
        gu_grad = thin_gu[...].astype(bf16)
        grad_gu_in[...] += dot_tn(gu_grad, tokens[chunk])
        grad_down_out[...] += dot_tn(down_latents[chunk], rows)
        return total[...] + dot(gu_grad, first_gu[...])

    own = backward(me)
    returned = []
    for order, shift in ((0, 1), (1, 3), (2, 2)):
        gathered[order].wait()
        source = SEQ - shift
        chunk = lax.rem(me + source, SEQ)
        send_two[source - 1] = backward(chunk).astype(bf16)
        moving = copy(send_two.at[source - 1], recv_two.at[source - 1], peers[source - 1], 5 + source)
        moving.start()
        returned.append(moving)
    for moving in returned:
        moving.wait()
    for slot in range(3):
        own = own + recv_two[slot].astype(f32)
    mixed_grad[...] = cotangent + norm_back(mixed[...], gain_in[...], own)


def feed_forward(*arrays):
    steps = arrays[1].shape[0]
    vmem = pl.BlockSpec(memory_space=pltpu.VMEM)
    outs = [
        jax.ShapeDtypeStruct((ROWS, D), bf16),
        jax.ShapeDtypeStruct((ROWS, D), f32),
        jax.ShapeDtypeStruct((steps, 32, TILE), f32),
        jax.ShapeDtypeStruct((steps, 32, TILE), f32),
        jax.ShapeDtypeStruct((steps, 16, TILE), f32),
        jax.ShapeDtypeStruct((32, D), f32),
        jax.ShapeDtypeStruct((16, D), f32),
    ]
    return pl.pallas_call(
        mlp_kernel,
        out_shape=outs,
        in_specs=[vmem] * len(arrays),
        out_specs=[vmem] * len(outs),
        scratch_shapes=[
            pltpu.VMEM((steps, SEQ, ROWS, TILE), f32),
            pltpu.VMEM((steps, SEQ, ROWS, TILE), f32),
            pltpu.VMEM((steps, SEQ, ROWS, TILE), bf16),
            pltpu.VMEM((SEQ, ROWS, 32), bf16),
            pltpu.VMEM((SEQ, ROWS, 16), bf16),
            pltpu.VMEM((SEQ, ROWS, D), bf16),
            pltpu.VMEM((ROWS, D), f32),
            pltpu.VMEM((ROWS, 16), f32),
            pltpu.VMEM((ROWS, 32), f32),
            pltpu.VMEM((3, ROWS, D), bf16),
            pltpu.VMEM((3, ROWS, D), bf16),
            pltpu.VMEM((3, ROWS, D), bf16),
            pltpu.VMEM((3, ROWS, D), bf16),
            pltpu.SemaphoreType.DMA((9,)),
            pltpu.SemaphoreType.DMA((9,)),
        ],
        compiler_params=pltpu.CompilerParams(
            collective_id=1, has_side_effects=True, vmem_limit_bytes=62 * MIB
        ),
        name="feed_forward",
    )(*arrays)


def project(inputs, weight_rows, down_sel, up_sel):
    latent = dot_nt(inputs, down_sel).astype(bf16)
    return dot_nt(inputs, weight_rows) + dot(latent, up_sel), latent


def project_back(grad_rows, weight_rows, down_sel, up_sel, inputs, latent):
    latent_grad = dot_nt(grad_rows, up_sel).astype(bf16)
    input_cot = dot(grad_rows, weight_rows) + dot(latent_grad, down_sel)
    return input_cot, dot_tn(latent_grad, inputs), dot_tn(latent, grad_rows)


def my_quarter(rows, axis):
    me = lax.axis_index("seq")
    part = lax.dynamic_slice_in_dim(rows, me * UNITS, UNITS, axis)
    widths = [(0, 0)] * rows.ndim
    widths[axis] = (0, BLOCK - UNITS)
    return jnp.pad(part, widths)


def body(
    layer_input, out_grad, segment_ids, adapter_ids,
    gain_attn_in, gain_attn_out, gain_mlp_in, gain_mlp_out,
    w_query, w_key, w_value, w_out, w_gate, w_up, w_down,
    qkv_adapt_in, q_adapt_out, kv_adapt_out, o_adapt_in, o_adapt_out,
    mlp_adapt_in, mlp_adapt_out, down_adapt_in, down_adapt_out,
):
    me = lax.axis_index("seq")
    shards = 32
    x = layer_input[0].astype(f32)
    cotangent = out_grad[0]
    chosen = adapter_ids[0]
    pick = lambda table: lax.dynamic_index_in_dim(table, chosen, 0, keepdims=False)
    qkv_in, q_out, kv_out = pick(qkv_adapt_in), pick(q_adapt_out), pick(kv_adapt_out)
    o_in, o_out = pick(o_adapt_in), pick(o_adapt_out)
    mlp_in, mlp_out = pick(mlp_adapt_in), pick(mlp_adapt_out)
    down_in, down_out = pick(down_adapt_in), pick(down_adapt_out)

    attn_pack = jnp.concatenate([w_query.T, w_key.T, w_value.T, w_out], 0)
    attn_all = lax.all_gather(attn_pack, "dp", axis=0, tiled=False)
    wq = attn_all[:, :32].reshape(1024, D)
    wk = attn_all[:, 32:40].reshape(256, D)
    wv = attn_all[:, 40:48].reshape(256, D)
    wo = attn_all[:, 48:].reshape(1024, D)
    mlp_pack = jnp.stack([my_quarter(w_gate.T, 0), my_quarter(w_up.T, 0), my_quarter(w_down, 0)])
    mlp_all = lax.all_gather(mlp_pack, "dp", axis=1, tiled=True)
    steps = shards * BLOCK // TILE
    mlp_all = mlp_all.reshape(3, steps, TILE, D)

    def hidden_slice(table):
        part = my_quarter(table.reshape(16, shards, 216), 2)
        return part.reshape(16, steps, TILE).transpose(1, 0, 2)

    zeros = jnp.zeros((steps, 16, TILE), bf16)
    second_gate = jnp.concatenate([hidden_slice(mlp_out[0]), zeros], 1)
    second_up = jnp.concatenate([zeros, hidden_slice(mlp_out[1])], 1)
    first_down = hidden_slice(down_in)

    first_norm = normed(x, gain_attn_in).astype(bf16)
    q, q_latent = project(first_norm, wq, qkv_in[0], q_out)
    k, k_latent = project(first_norm, wk, qkv_in[1], kv_out[0])
    v, v_latent = project(first_norm, wv, qkv_in[2], kv_out[1])
    q = q.astype(bf16).reshape(ROWS, 4, 256)
    kv = jnp.concatenate([k, v], 1).astype(bf16)
    kv_all = lax.all_gather(kv, "seq", axis=0, tiled=True)
    keys, values = kv_all[:, :256], kv_all[:, 256:]
    segments = segment_ids[0]
    mine = lax.dynamic_slice_in_dim(segments, me * ROWS, ROWS)
    position = me * ROWS + jnp.arange(ROWS)
    allowed = (mine[:, None] == segments[None]) & (jnp.arange(1024)[None] <= position[:, None])
    scale = 1.0 / 16.0
    raw = jnp.einsum("qhe,ke->hqk", q, keys, preferred_element_type=f32)
    bent = jnp.tanh(raw * (scale / softcap))
    exponent = jnp.where(allowed[None], jnp.exp(softcap * bent), 0.0)
    probs = exponent / jnp.sum(exponent, -1, keepdims=True)
    probs_low = probs.astype(bf16)
    context = jnp.einsum("hqk,ke->qhe", probs_low, values, preferred_element_type=f32)
    context = context.astype(bf16).reshape(ROWS, 1024)
    o_latent = dot_nt(context, o_in).astype(bf16)
    attn_proj = dot(context, wo) + dot(o_latent, o_out)
    mixed = x + normed(attn_proj, gain_attn_out)
    second_norm = normed(mixed, gain_mlp_in).astype(bf16)
    tokens = lax.all_gather(second_norm, "seq", axis=0, tiled=False)

    layer_out, mixed_grad, g_gate, g_up, g_down_in, g_gu_in, g_down_out = feed_forward(
        tokens, mlp_all[0], mlp_all[1], mlp_all[2], mlp_in.reshape(32, D),
        second_gate, second_up, first_down, down_out,
        mixed, cotangent, gain_mlp_in[None], gain_mlp_out[None],
    )

    def hidden_full(part):
        part = part.transpose(1, 0, 2).reshape(16, shards, BLOCK)[:, :, :UNITS]
        full = jnp.zeros((16, shards, 4, UNITS), f32)
        full = lax.dynamic_update_slice_in_dim(full, part[:, :, None], me, 2)
        return full.reshape(16, shards * 4 * UNITS)

    attn_grad = norm_back(attn_proj, gain_attn_out, mixed_grad).astype(bf16)
    o_latent_grad = dot_nt(attn_grad, o_out).astype(bf16)
    context_grad = (dot_nt(attn_grad, wo) + dot(o_latent_grad, o_in)).astype(bf16)
    g_o_in = dot_tn(o_latent_grad, context)
    g_o_out = dot_tn(o_latent, attn_grad)
    head_grads = context_grad.reshape(ROWS, 4, 256)
    prob_grad = jnp.einsum("qhe,ke->hqk", head_grads, values, preferred_element_type=f32)
    centre = jnp.sum(probs * prob_grad, -1, keepdims=True)
    raw_grad = (probs * (prob_grad - centre) * (1.0 - bent * bent) * scale).astype(bf16)
    q_grad = jnp.einsum("hqk,ke->qhe", raw_grad, keys, preferred_element_type=f32)
    q_grad = q_grad.astype(bf16).reshape(ROWS, 1024)
    k_part = jnp.einsum("hqk,qhe->ke", raw_grad, q, preferred_element_type=f32)
    v_part = jnp.einsum("hqk,qhe->ke", probs_low, head_grads, preferred_element_type=f32)
    kv_grad = lax.psum_scatter(
        jnp.concatenate([k_part, v_part], 1).astype(bf16), "seq", scatter_dimension=0, tiled=True
    )
    k_grad, v_grad = kv_grad[:, :256], kv_grad[:, 256:]
    q_cot, g_q_in, g_q_out = project_back(q_grad, wq, qkv_in[0], q_out, first_norm, q_latent)
    k_cot, g_k_in, g_k_out = project_back(k_grad, wk, qkv_in[1], kv_out[0], first_norm, k_latent)
    v_cot, g_v_in, g_v_out = project_back(v_grad, wv, qkv_in[2], kv_out[1], first_norm, v_latent)
    input_grad = (mixed_grad + norm_back(x, gain_attn_in, q_cot + k_cot + v_cot)).astype(bf16)

    picked = (
        jnp.stack([g_q_in, g_k_in, g_v_in]),
        g_q_out,
        jnp.stack([g_k_out, g_v_out]),
        g_o_in,
        g_o_out,
        g_gu_in.reshape(2, 16, D),
        jnp.stack([hidden_full(g_gate[:, :16]), hidden_full(g_up[:, 16:])]),
        hidden_full(g_down_in),
        g_down_out,
    )
    chooser = (chosen == jnp.arange(8)).astype(f32)
    spread = tuple(chooser.reshape((8,) + (1,) * g.ndim) * g[None] for g in picked)
    summed = lax.psum(spread, ("dp", "seq"))
    return (layer_out[None], input_grad[None]) + tuple(summed)


def solution(mesh):
    tokens = P("dp", "seq", None)
    columns, rows = P(None, "dp"), P("dp", None)
    placed = (
        (tokens, tokens, P("dp", None), P("dp"))
        + (P(),) * 4
        + (columns, columns, columns, rows, columns, columns, rows)
        + (P(),) * 9
    )
    return jax.shard_map(
        body,
        mesh=mesh,
        in_specs=placed,
        out_specs=(tokens, tokens) + (P(),) * 9,
        check_vma=False,
    )
```

time: 716 us -> 677 us (0.946)
  Pallas kernels: 0 us -> 109 us
  matrix products: 161 us -> 59 us
  blocking collectives: 78.7 us -> 0 us
  local copies, waits for them, and re-layouts: 40.6 us -> 82.3 us
  starting transfers between devices: 16 us -> 0.25 us
  waiting for transfers between devices: 366 us -> 377 us
  other arithmetic: 32.6 us -> 23.2 us
    pallas_call x0 -> x1, Pallas kernels: none -> 109 us  [feed_forward(): pl.pallas_call(mlp_kernel, out_shape=outs, in_specs=[vmem] * len(arrays),...]
    dot_general x77 -> x38, matrix products: 161 us -> 59 us  [the longest x12 14.1 us: dot_nt(): lax.dot_general(a, b, (((1,), (1,)), ((), ())), preferred_element_type=f32)]
    all_gather x4 -> x0, blocking collectives: 78.7 us -> none  [the longest x1 27.7 us: body(): lax.all_gather(w_key, 'dp', axis=1, tiled=True)]
    dynamic_update_slice x0 -> x3, local copies, waits for them, and re-layouts: none -> 23.3 us  [hidden_full(): full = lax.dynamic_update_slice_in_dim(full, part[:, :, None], me, 2)]
    reduce_scatter x2 -> x1, waiting for transfers between devices: 10 us -> 26.4 us  [body(): lax.psum_scatter(jnp.concatenate([k_part, v_part], 1).astype(bf16), 'seq'...]
    slice x1 -> x3, local copies, waits for them, and re-layouts: 0.54 us -> 16.6 us  [the longest x1 11.2 us: body(): mlp_all[2]]
    all_to_all x4 -> x0, starting transfers between devices: 15.3 us -> none  [the longest x1 4.23 us: body(): lax.all_to_all(query_grads, 'seq', split_axis=1, concat_axis=2, tiled=True)]
    unnamed x270 -> x114, local copies, waits for them, and re-layouts: 33.9 us -> 20.3 us
  transfers between devices with their start and end apart: 12 -> 6, of which waited for: 7 -> 6; matrix products, arithmetic and copies ran while one was open for 18% -> 9% of each run, Pallas kernels for 0% -> 0%
where the time goes in v1:
time: 677 us; the launch traced here: 667 us
  waiting for transfers between devices  377 us (56%)
  Pallas kernels  109 us (16%)
  local copies, waits for them, and re-layouts  82.3 us (12%)
  matrix products  59 us (9%)
  other arithmetic  23.2 us (3%)
  between operations  16 us (2%)
    psum x1, waiting for transfers between devices, body(): summed = lax.psum(spread, ('dp', 'seq'))  219 us
    pallas_call x1, Pallas kernels, feed_forward(): pl.pallas_call(mlp_kernel, out_shape=outs, in_specs=[vmem] * len(arrays),...  109 us
    all_gather x1, waiting for transfers between devices, body(): attn_all = lax.all_gather(attn_pack, 'dp', axis=0, tiled=False)  49.4 us
    all_gather x1, waiting for transfers between devices, body(): mlp_all = lax.all_gather(mlp_pack, 'dp', axis=1, tiled=True)  49.1 us
    reduce_scatter x1, waiting for transfers between devices, body(): lax.psum_scatter(jnp.concatenate([k_part, v_part], 1).astype(bf16), 'seq'...  26.4 us
    dynamic_update_slice x3, local copies, waits for them, and re-layouts, hidden_full(): full = lax.dynamic_update_slice_in_dim(full, part[:, :, None], me, 2)  23.3 us
    all_gather x1, waiting for transfers between devices, body(): tokens = lax.all_gather(second_norm, 'seq', axis=0, tiled=False)  23 us
    unnamed x114, local copies, waits for them, and re-layouts  20.3 us
  transfers between devices with their start and end apart: 6, of which 6 were waited for; matrix products, arithmetic and copies ran while one was open for 9% of the time, Pallas kernels for 0%

profile of v1, /device:TPU:1, one launch (start us, length us, event | category | flops | bytes accessed | tf_op | source)
XLA Modules:
  0.0 667.1 jit_solution(15820274824495746091)
XLA Ops:
  7.3 1.8 pad_maximum_fusion.5
  9.8 1.3 fusion.23
  11.1 1.4 convolution_convert_fusion.8
  12.5 1.4 convolution_convert_fusion.7
  13.9 49.4 %all-gather.11.cloned.1.call-done = bf16[2560,1152]{1,0:T(8,128)(2,1)} async-done(((bf16[80,1152]{1,0:T(8,128)(2,1)}), bf16[2560,1152]{1,0:T(8,128)(2,1)}) %all-gather.11.cloned.1.call-update) | async-done | bytes 5898256 | tf_op jit(solution)/shard_map/all_gather | solution.py:257
  63.3 1.5 fusion.41
  64.8 1.5 fusion.40
  74.1 4.3 fusion.108
  78.4 1.4 copy-done.10
  82.0 10.7 %all-gather.7.cloned.1.call-done = bf16[1024,512]{0,1:T(8,128)(2,1)} async-done(((bf16[256,512]{0,1:T(8,128)(2,1)}), bf16[1024,512]{0,1:T(8,128)(2,1)}) %all-gather.7.cloned.1.call-update) | async-done | bytes 1048592 | tf_op jit(solution)/shard_map/all_gather | solution.py:282
  92.7 2.7 fusion.5
  95.4 1.6 convolution_convert_fusion
  97.5 1.2 convolution_convert_fusion.4
  112.5 1.4 dynamic-slice_bitcast_fusion.5.second_down
  113.9 1.5 constant_dynamic-slice_fusion.6
  115.4 49.1 %all-gather.9.cloned.1.call-done = bf16[3,2048,1152]{2,1,0:T(8,128)(2,1)} async-done(((bf16[3,64,1152]{2,1,0:T(8,128)(2,1)}), bf16[3,2048,1152]{2,1,0:T(8,128)(2,1)}) %all-gather.9.cloned.1.call-update) | async-done | bytes 14155792 | tf_op jit(solution)/shard_map/all_gather | solution.py:263
  164.5 11.2 %fusion.107 = (bf16[1,2048,1152]{2,1,0:T(8,128)(2,1)}, bf16[1,2048,1152]{2,1,0:T(8,128)(2,1)}, bf16[1,2048,1152]{2,1,0:T(8,128)(2,1)}) fusion(bf16[3,2048,1152]{2,1,0:T(8,128)(2,1)} %all-gather.9.cloned.1.call-done), kind=kLoop, calls=%fused_computation.179 | loop fusion | bytes 28311552 | tf_op jit(solution)/shard_map/slice | solution.py:303
  175.7 23.0 %all-gather.13.cloned.1.call-done = bf16[1024,1152]{1,0:T(8,128)(2,1)} async-done(((bf16[256,1152]{1,0:T(8,128)(2,1)}), bf16[1024,1152]{1,0:T(8,128)(2,1)}) %all-gather.13.cloned.1.call-update) | async-done | bytes 2359312 | tf_op jit(solution)/shard_map/all_gather | solution.py:300
  198.6 109.2 %feed_forward.1 = (bf16[256,1152]{1,0:T(8,128)(2,1)}, f32[256,1152]{1,0:T(8,128)}, f32[8,32,256]{2,1,0:T(8,128)}, f32[8,32,256]{2,1,0:T(8,128)}, f32[8,16,256]{2...) custom-call(bf16[4,256,1152]{2,1,0:T(8,128)(2,1)} %bitcast.313, bf16[8,256,1152]{2,1,0:T(8,128)(2,1)} %bitcast.299, ...), custom_call_target="tpu_custom_call" | custom-call | tf_op jit(solution)/shard_map/feed_forward/pallas_call | solution.py:190
  307.9 1.6 multiply_reduce_fusion
  314.0 4.7 fusion.20
  318.8 2.8 fusion.42
  321.5 9.0 %fusion.21 = bf16[1024,256]{0,1:T(8,128)(2,1)} fusion(bf16[256,4,256]{0,2,1:T(8,128)(2,1)S(1)} %bitcast.322, f32[1024,256,4]{1,0,2:T(8,128)} %fusion.42, f32[1024,256,4]{1,0,2:T(8,128)} %copy-done.51, f32[4,256]{1,0:T(4,128)S(1)} %get-tuple-element.47, pred[256,1024]{0,1:T(8,128)(4,1)S(1)} %copy-done.30), kind=kOutput, calls=%fused_computation.41 | convolution fusion | flops 553912320 | bytes 9703424 | tf_op jit(solution)/shard_map/hqk,qhe->ke/dot_general | solution.py:325
  330.6 8.4 %fusion.22 = bf16[256,4,256]{2,0,1:T(8,128)(2,1)S(1)} fusion(f32[1024,256,4]{1,0,2:T(8,128)} %fusion.42, f32[1024,256,4]{1,0,2:T(8,128)} %copy-done.51, bf16[1024,512]{0,1:T(8,128)(2,1)} %all-gather.7.cloned.1.call-done, f32[4,256]{1,0:T(4,128)S(1)} %get-tuple-element.47, pred[256,1024]{0,1:T(8,128)(4,1)S(1)} %copy-done.30), kind=kOutput, calls=%fused_computation.42 | convolution fusion | flops 553912320 | bytes 18358272 | tf_op jit(solution)/shard_map/hqk,ke->qhe/dot_general | solution.py:323
  340.4 1.2 broadcast.190.clone.1
  341.6 7.7 %dynamic_update_slice.9 = f32[16,32,4,54]{3,2,1,0:T(4,128)} dynamic-update-slice(f32[16,32,4,54]{3,2,1,0:T(4,128)} %broadcast.190.clone.1, f32[16,32,1,54]{3,2,1,0:T(1,128)S(1)} %bitcast.317, s32[]{:T(128)} %constant.41.clone.1, s32[]{:T(128)} %constant.41.clone.1, s32[]{:T(128)S(6)} %select_n.42, s32[]{:T(128)} %constant.41.clone.1) | dynamic-update-slice | bytes 221188 | tf_op jit(solution)/shard_map/dynamic_update_slice | solution.py:311
  349.3 2.1 stack_reshape.6
  351.6 1.2 broadcast.190.clone
  352.8 7.9 %dynamic_update_slice.10 = f32[16,32,4,54]{3,2,1,0:T(4,128)} dynamic-update-slice(f32[16,32,4,54]{3,2,1,0:T(4,128)} %broadcast.190.clone, f32[16,32,1,54]{3,2,1,0:T(1,128)S(1)} %bitcast.318, s32[]{:T(128)} %constant.41.clone.1, s32[]{:T(128)} %constant.41.clone.1, s32[]{:T(128)S(6)} %select_n.42, s32[]{:T(128)} %constant.41.clone.1) | dynamic-update-slice | bytes 221188 | tf_op jit(solution)/shard_map/dynamic_update_slice | solution.py:311
  360.7 2.1 stack_reshape.7
  363.0 1.2 broadcast.190.clone.2
  364.2 7.7 %dynamic_update_slice.11 = f32[16,32,4,54]{3,2,1,0:T(4,128)} dynamic-update-slice(f32[16,32,4,54]{3,2,1,0:T(4,128)} %broadcast.190.clone.2, f32[16,32,1,54]{3,2,1,0:T(1,128)S(1)} %bitcast.316, s32[]{:T(128)} %constant.41.clone.1, s32[]{:T(128)} %constant.41.clone.1, s32[]{:T(128)S(6)} %select_n.42, s32[]{:T(128)} %constant.41.clone.1) | dynamic-update-slice | bytes 221188 | tf_op jit(solution)/shard_map/dynamic_update_slice | solution.py:311
  371.9 2.1 mul.386
  374.0 1.2 broadcast_multiply_fusion.3
  375.2 2.1 broadcast_multiply_fusion.1
  378.5 1.2 broadcast_multiply_fusion.4
  380.0 1.2 broadcast_multiply_fusion.6
  381.1 3.7 broadcast_multiply_fusion
  384.8 26.4 %reduce-scatter.2.cloned.1.call-done = bf16[256,512]{0,1:T(8,128)(2,1)} async-done(((bf16[1024,512]{0,1:T(8,128)(2,1)}), bf16[256,512]{0,1:T(8,128)(2,1)}) %reduce-scatter.2.cloned.1.call-update) | async-done | bytes 262160 | tf_op jit(solution)/shard_map/reduce_scatter | solution.py:327
  415.2 1.4 broadcast_multiply_fusion.2
  420.1 1.6 convolution_add_fusion.1
  421.6 1.4 convolution_add_fusion
  423.1 1.2 fusion.24
  424.3 1.1 fusion.39
  425.5 218.5 %all-reduce.11.cloned.1.call-done = (f32[8,3,16,1152]{3,2,1,0:T(8,128)}, f32[8,16,1024]{2,1,0:T(8,128)}, f32[8,2,16,256]{3,2,1,0:T(8,128)}, f32[8,16,1024]{2,1,0...) async-done(((f32[8,3,16,1152]{3,2,1,0:T(8,128)}, ...) | async-done | bytes 16056336 | tf_op jit(solution)/shard_map/psum | solution.py:349
  644.9 3.1 copy.111
  652.1 3.6 copy.117
  656.7 1.8 copy.118
  (200 shorter events, 46.5 us)
Async XLA Ops:
  7.2 97.2 %copy-start = (bf16[8,16,6912]{2,1,0:T(8,128)(2,1)S(1)}, bf16[8,16,6912]{2,1,0:T(8,128)(2,1)}, u32[]{:S(2)}) copy-start(bf16[8,16,6912]{2,1,0:T(8,128)(2,1)} %param.46) | copy-start | bytes 5308420
  7.2 56.1 %copy-start.8 = (bf16[1,256,1152]{2,1,0:T(8,128)(2,1)S(1)}, bf16[1,256,1152]{2,1,0:T(8,128)(2,1)}, u32[]{:S(2)}) copy-start(bf16[1,256,1152]{2,1,0:T(8,128)(2,1)} %param.24) | copy-start | bytes 1769476
  7.2 56.1 %copy-start.38 = (f32[1152]{0:T(1024)S(1)}, f32[1152]{0:T(1024)}, u32[]{:S(2)}) copy-start(f32[1152]{0:T(1024)} %param.28) | copy-start | bytes 13828
  7.2 56.1 %all-gather.11.cloned.1.call-start = ((), (), s32[]{:S(2)}) async-start(), calls=%async_computation.4 | async-start | bytes 6082560 | tf_op jit(solution)/shard_map/all_gather | solution.py:257
  9.1 83.6 %all-gather.7.cloned.1.call-start = ((), (), s32[]{:S(2)}) async-start(), calls=%async_computation.1 | async-start | bytes 1310720 | tf_op jit(solution)/shard_map/all_gather | solution.py:282
  11.0 55.3 %copy-start.44 = (f32[256]{0:T(256)}, f32[256]{0:T(256)S(1)}, u32[]{:S(2)}) copy-start(f32[256]{0:T(256)S(1)} %fusion.23) | copy-start | bytes 3076
  11.1 67.3 %copy-start.48 = (f32[256]{0:T(256)}, f32[256]{0:T(256)S(1)}, u32[]{:S(2)}) copy-start(f32[256]{0:T(256)S(1)} %add_rsqrt_fusion.2) | copy-start | bytes 3076
  12.5 54.8 %copy-start.40 = (bf16[256,16]{0,1:T(8,128)(2,1)}, bf16[256,16]{0,1:T(8,128)(2,1)S(1)}, u32[]{:S(2)}) copy-start(bf16[256,16]{0,1:T(8,128)(2,1)S(1)} %convolution_convert_fusion.8) | copy-start | bytes 24580
  66.3 5.7 copy-start.47
  69.0 95.6 %all-gather.9.cloned.1.call-start = ((), (), s32[]{:S(2)}) async-start(), calls=%async_computation.2 | async-start | bytes 14598144 | tf_op jit(solution)/shard_map/all_gather | solution.py:263
  72.0 126.7 %all-gather.13.cloned.1.call-start = ((), (), s32[]{:S(2)}) async-start(), calls=%async_computation.5 | async-start | bytes 2949120 | tf_op jit(solution)/shard_map/all_gather | solution.py:300
  82.0 13.4 %copy-start.21 = (bf16[256,1024]{0,1:T(8,128)(2,1)}, bf16[256,1024]{0,1:T(8,128)(2,1)S(1)}, u32[]{:S(2)}) copy-start(bf16[256,1024]{0,1:T(8,128)(2,1)S(1)} %copy.88) | copy-start | bytes 1572868
  92.7 2.7 copy-start.27
  92.7 2.7 copy-start.29
  95.4 2.1 copy-start.51
  95.4 4.5 copy-start.2
  97.5 3.4 copy-start.13
  99.9 2.0 copy-start.34
  100.9 2.4 copy-start.39
  101.9 3.1 copy-start.46
  104.3 306.9 %reduce-scatter.2.cloned.1.call-start = ((), (), s32[]{:S(2)}) async-start(), calls=%async_computation.3 | async-start | bytes 1310720 | tf_op jit(solution)/shard_map/reduce_scatter | solution.py:327
  198.6 109.2 %copy-start.5 = (f32[256,1152]{1,0:T(8,128)S(1)}, f32[256,1152]{1,0:T(8,128)}, u32[]{:S(2)}) copy-start(f32[256,1152]{1,0:T(8,128)} %copy-done.4) | copy-start | bytes 3538948
  307.9 2.4 copy-start.3
  310.3 2.2 copy-start.14
  311.2 2.9 copy-start.30
  314.0 4.7 copy-start.28
  318.8 2.8 copy-start.22
  330.6 9.6 %copy-start.37 = (f32[8,32,256]{2,1,0:T(8,128)S(1)}, f32[8,32,256]{2,1,0:T(8,128)}, u32[]{:S(2)}) copy-start(f32[8,32,256]{2,1,0:T(8,128)} %get-tuple-element.21) | copy-start | bytes 786436
  339.9 11.4 %copy-start.36 = (f32[8,32,256]{2,1,0:T(8,128)S(1)}, f32[8,32,256]{2,1,0:T(8,128)}, u32[]{:S(2)}) copy-start(f32[8,32,256]{2,1,0:T(8,128)} %get-tuple-element.22) | copy-start | bytes 786436
  351.3 11.5 %copy-start.33 = (f32[8,16,256]{2,1,0:T(8,128)S(1)}, f32[8,16,256]{2,1,0:T(8,128)}, u32[]{:S(2)}) copy-start(f32[8,16,256]{2,1,0:T(8,128)} %get-tuple-element.23) | copy-start | bytes 393220
  360.7 13.3 %copy-start.32 = (f32[32,1152]{1,0:T(8,128)S(1)}, f32[32,1152]{1,0:T(8,128)}, u32[]{:S(2)}) copy-start(f32[32,1152]{1,0:T(8,128)} %get-tuple-element.20) | copy-start | bytes 442372
  360.7 13.3 %copy-start.42 = (f32[8]{0:T(128)S(1)}, f32[8]{0:T(128)}, u32[]{:S(2)}) copy-start(f32[8]{0:T(128)} %compare_convert_fusion) | copy-start | bytes 100
  374.0 3.3 copy-start.25
  374.0 3.3 copy-start.26
  378.4 265.7 %all-reduce.11.cloned.1.call-start = ((), (), s32[]{:S(2)}) async-start(), calls=%async_computation.6 | async-start | bytes 32112640 | tf_op jit(solution)/shard_map/psum | solution.py:349
  384.8 29.2 %copy-start.41 = (bf16[256,16]{0,1:T(8,128)(2,1)S(1)}, bf16[256,16]{0,1:T(8,128)(2,1)}, u32[]{:S(2)}) copy-start(bf16[256,16]{0,1:T(8,128)(2,1)} %copy-done.40) | copy-start | bytes 24580
  384.8 29.6 %copy-start.43 = (f32[8]{0:T(128)S(1)}, f32[8]{0:T(128)}, u32[]{:S(2)}) copy-start(f32[8]{0:T(128)} %compare_convert_fusion) | copy-start | bytes 100
  411.2 2.8 copy-start.16
  420.0 3.0 copy-start.11
  424.3 219.7 %copy-start.18 = (bf16[256,1152]{1,0:T(8,128)(2,1)S(1)}, bf16[256,1152]{1,0:T(8,128)(2,1)}, u32[]{:S(2)}) copy-start(bf16[256,1152]{1,0:T(8,128)(2,1)} %get-tuple-element.18) | copy-start | bytes 1769476
  644.0 3.9 copy-start.24
  644.0 4.7 copy-start.31
  644.0 5.4 copy-start.23
  644.0 6.2 copy-start.20
  644.0 7.0 %copy-start.17 = (f32[8,2,16,1152]{3,2,1,0:T(8,128)S(1)}, f32[8,2,16,1152]{3,2,1,0:T(8,128)}, u32[]{:S(2)}) copy-start(f32[8,2,16,1152]{3,2,1,0:T(8,128)} %get-tuple-element.75) | copy-start | bytes 3538948
  644.9 7.2 %copy-start.12 = (f32[8,2,16,6912]{3,2,1,0:T(8,128)S(1)}, f32[8,2,16,6912]{3,2,1,0:T(8,128)}, u32[]{:S(2)}) copy-start(f32[8,2,16,6912]{3,2,1,0:T(8,128)} %get-tuple-element.76) | copy-start | bytes 21233668
  652.1 4.6 copy-start.15
  656.6 3.2 copy-start.1
  (10 other events, 13.1 us)
Sparse Core Ops, SparseCore 0:
  11.0 52.2 all-gather.10
  69.1 23.5 all-gather.6
  95.5 68.9 all-gather.8
  166.6 31.9 all-gather.12
  378.5 32.6 reduce-scatter.1
  419.8 224.1 all-reduce.10

commit v2 on v1

--- a/solution.py
+++ b/solution.py
@@ -9,7 +9,6 @@
 
 epsilon = 1e-06
 softcap = 50.0
-highest = lax.Precision.HIGHEST
 MESH = pl.DeviceIdType.MESH
 bf16 = jnp.bfloat16
 f32 = jnp.float32
@@ -58,8 +57,277 @@
     pl.semaphore_wait(barrier, len(peers))
 
 
+def place():
+    dp = lax.axis_index("dp")
+    return lax.axis_index("seq"), dp // 8, lax.rem(dp // 2, 4), lax.rem(dp, 2)
+
+
+def at(x, y, z, core):
+    return ((lax.rem(y, 4) * 4 + lax.rem(z, 4)) * 2 + core, lax.rem(x, 4))
+
+
+def plane_peers():
+    x, y, z, core = place()
+    return [at(x, y + k, z, core) for k in (1, 2, 3)] + [at(x, y, z + k, core) for k in (1, 2, 3)]
+
+
+def sibling():
+    x, y, z, core = place()
+    return at(x, y, z, 1 - core)
+
+
+def remote(src, dst, send_sem, recv_sem, peer):
+    return pltpu.make_async_remote_copy(
+        src_ref=src, dst_ref=dst, send_sem=send_sem, recv_sem=recv_sem,
+        device_id=peer, device_id_type=MESH,
+    )
+
+
+class PlaneGather:
+    def __init__(self, own, buffer, send_sem, recv_sem):
+        self.x, self.y, self.z, self.core = place()
+        self.own, self.buffer, self.send, self.recv = own, buffer, send_sem, recv_sem
+
+    def _copy(self, src, dst, slot, peer):
+        return remote(src, dst, self.send.at[slot], self.recv.at[slot], peer)
+
+    def _first(self, k):
+        x, y, z, core = self.x, self.y, self.z, self.core
+        peer = at(x, y + k * (1 - core), z + k * core, core)
+        return self._copy(self.own, self.buffer.at[y, z, core], k - 1, peer)
+
+    def _line(self, core, back):
+        if core == 0:
+            return self.buffer.at[:, lax.rem(self.z + 4 - back, 4), 0]
+        return self.buffer.at[lax.rem(self.y + 4 - back, 4), :, 1]
+
+    def _second(self, core, k):
+        line = self._line(core, 0)
+        peer = at(self.x, self.y + k * core, self.z + k * (1 - core), core)
+        return self._copy(line, line, 2 + k, peer)
+
+    def _swap(self, core, back):
+        line = self._line(core, back)
+        return self._copy(line, line, 6 + back, at(self.x, self.y, self.z, 1 - core))
+
+    def _both(self, act):
+        for core in (0, 1):
+            pl.when(self.core == core)(functools.partial(act, core))
+
+    def start(self):
+        for k in (1, 2, 3):
+            self._first(k).start()
+
+    def middle(self):
+        for k in (1, 2, 3):
+            self._first(k).wait()
+
+        def act(core):
+            for k in (1, 3, 2):
+                self._second(core, k).start()
+            self._swap(core, 0).start()
+
+        self._both(act)
+
+    def late(self):
+        def act(core):
+            for k in (1, 3, 2):
+                self._second(core, k).wait()
+                self._swap(core, k).start()
+
+        self._both(act)
+
+    def finish(self):
+        def act(core):
+            for back in range(4):
+                self._swap(core, back).wait()
+
+        self._both(act)
+
+
+def allowed_pairs(segment_rows, segment_column, me, chunk):
+    keys = lax.broadcasted_iota(jnp.int32, (ROWS, ROWS), 1) + chunk * ROWS
+    queries = lax.broadcasted_iota(jnp.int32, (ROWS, ROWS), 0) + me * ROWS
+    return (segment_column[...] == segment_rows[chunk]) & (keys <= queries)
+
+
+SCORE = 1.0 / 16.0
+
+
+def attention_kernel(
+    layer_input, pack_qkv, pack_o, pack_gu, pack_down, segment_rows, segment_column,
+    gain_first, gain_second, gain_third,
+    first_qkv, second_q, second_kv, first_o, second_o,
+    all_gu, all_down, all_tokens, out_qkv, out_kv_rows, out_o, out_kv,
+    queries, totals, context, attn_proj, mixed, qkv_latent, o_latent,
+    got_qkv, got_o, kv_rows, first_norm, kv_all, second_norm,
+    sem_s, sem_r, kv_s, kv_r, tok_s, tok_r, loc,
+):
+    me, y, z, core = place()
+    line = seq_peers()
+    greet(line + plane_peers() + [sibling()])
+    gathers = [
+        PlaneGather(own, got, sem_s.at[i], sem_r.at[i])
+        for i, (own, got) in enumerate(
+            ((pack_qkv, got_qkv), (pack_o, got_o), (pack_gu, all_gu), (pack_down, all_down))
+        )
+    ]
+    g_qkv, g_o, g_gu, g_down = gathers
+    own_copies = [
+        pltpu.make_async_copy(g.own, g.buffer.at[y, z, core], loc.at[i])
+        for i, g in enumerate(gathers)
+    ]
+    g_qkv.start()
+    for moving in own_copies:
+        moving.start()
+    values = layer_input[...].astype(f32)
+    first_norm[...] = normed(values, gain_first[...]).astype(bf16)
+    latent = dot_nt(first_norm[...], first_qkv[...]).astype(bf16)
+    qkv_latent[...] = latent
+    for moving in own_copies:
+        moving.wait()
+    g_qkv.middle()
+    g_o.start()
+    g_qkv.late()
+    g_o.middle()
+    g_gu.start()
+    g_qkv.finish()
+
+    def unmix(i, _):
+        pairs = got_qkv[i, :, :, 32:48].astype(f32).reshape(8, 2, 8, D)
+        kv_rows[pl.ds(i * 64, 64)] = pairs[:, 0].reshape(64, D).astype(bf16)
+        kv_rows[pl.ds(256 + i * 64, 64)] = pairs[:, 1].reshape(64, D).astype(bf16)
+        return 0
+
+    lax.fori_loop(0, 4, unmix, 0)
+    kv = dot_nt(first_norm[...], kv_rows[...]) + dot(latent, second_kv[...])
+    kv_all[me] = kv.astype(bf16)
+
+    def kv_copy(shift):
+        return remote(kv_all.at[me], kv_all.at[me], kv_s.at[shift - 1], kv_r.at[shift - 1], line[shift - 1])
+
+    for shift in (1, 2, 3):
+        pl.when(me + shift < SEQ)(lambda shift=shift: kv_copy(shift).start())
+
+    def query(h, _):
+        rows = got_qkv[h, :, :, 0:32].reshape(256, D)
+        queries[h] = (dot_nt(first_norm[...], rows) + dot(latent, second_q[h])).astype(bf16)
+        context[h] = jnp.zeros((ROWS, 256), f32)
+        totals[h] = jnp.zeros((ROWS, 1), f32)
+        return 0
+
+    lax.fori_loop(0, 4, query, 0)
+    g_gu.middle()
+    g_down.start()
+
+    def attend(chunk):
+        keys, held = kv_all[chunk, :, 0:256], kv_all[chunk, :, 256:512]
+        allowed = allowed_pairs(segment_rows, segment_column, me, chunk)
+
+        def head(h, _):
+            bent = jnp.tanh(dot_nt(queries[h], keys) * (SCORE / softcap))
+            weight = jnp.where(allowed, jnp.exp(softcap * bent), 0.0).astype(bf16)
+            totals[h] += jnp.sum(weight.astype(f32), -1, keepdims=True)
+            context[h] += dot(weight, held)
+            return 0
+
+        lax.fori_loop(0, 4, head, 0)
+
+    attend(me)
+    g_o.late()
+    g_o.finish()
+    keep = [
+        pltpu.make_async_copy(got_qkv, out_qkv, loc.at[0]),
+        pltpu.make_async_copy(got_o, out_o, loc.at[1]),
+        pltpu.make_async_copy(kv_rows, out_kv_rows, loc.at[2]),
+    ]
+    for moving in keep:
+        moving.start()
+    for shift in (1, 2, 3):
+        def arrived(shift=shift):
+            kv_copy(shift).wait_recv()
+            attend(me - shift)
+
+        pl.when(me >= shift)(arrived)
+
+    total = jnp.zeros((ROWS, D), f32)
+    thin = jnp.zeros((ROWS, 16), f32)
+    for h in range(4):
+        context[h] = context[h] / totals[h]
+        low = context[h].astype(bf16)
+        total = total + dot(low, got_o[h].reshape(256, D))
+        thin = thin + dot_nt(low, first_o[h])
+    o_latent[...] = thin.astype(bf16)
+    proj = total + dot(o_latent[...], second_o[...])
+    attn_proj[...] = proj
+    mid = values + normed(proj, gain_second[...])
+    mixed[...] = mid
+    second_norm[...] = normed(mid, gain_third[...]).astype(bf16)
+    spread = [remote(second_norm, all_tokens.at[me], tok_s.at[i], tok_r.at[i], line[i]) for i in range(3)]
+    for moving in spread:
+        moving.start()
+    mine = pltpu.make_async_copy(second_norm, all_tokens.at[me], loc.at[3])
+    mine.start()
+    g_gu.late()
+    g_down.middle()
+    g_gu.finish()
+    g_down.late()
+    g_down.finish()
+    kept_kv = pltpu.make_async_copy(kv_all, out_kv, loc.at[4])
+    kept_kv.start()
+    for moving in keep + [mine, kept_kv]:
+        moving.wait()
+    for moving in spread:
+        moving.wait()
+    for shift in (1, 2, 3):
+        pl.when(me + shift < SEQ)(lambda shift=shift: kv_copy(shift).wait_send())
+
+
+def attention_forward(*arrays):
+    vmem = pl.BlockSpec(memory_space=pltpu.VMEM)
+    hbm = pl.BlockSpec(memory_space=pl.ANY)
+    shape = jax.ShapeDtypeStruct
+    outs = [
+        (shape((4, 4, 2, 128, D), bf16), hbm),
+        (shape((4, 4, 2, 64, D), bf16), hbm),
+        (shape((SEQ, ROWS, D), bf16), hbm),
+        (shape((4, 4, 2, 48, D), bf16), hbm),
+        (shape((512, D), bf16), hbm),
+        (shape((4, 4, 2, 32, D), bf16), hbm),
+        (shape((SEQ, ROWS, 512), bf16), hbm),
+        (shape((4, ROWS, 256), bf16), vmem),
+        (shape((4, ROWS, 1), f32), vmem),
+        (shape((4, ROWS, 256), f32), vmem),
+        (shape((ROWS, D), f32), vmem),
+        (shape((ROWS, D), f32), vmem),
+        (shape((ROWS, 48), bf16), vmem),
+        (shape((ROWS, 16), bf16), vmem),
+    ]
+    ins = [vmem, vmem, vmem, hbm, hbm] + [vmem] * (len(arrays) - 5)
+    dma = pltpu.SemaphoreType.DMA
+    return pl.pallas_call(
+        attention_kernel,
+        out_shape=[s for s, _ in outs],
+        in_specs=ins,
+        out_specs=[m for _, m in outs],
+        scratch_shapes=[
+            pltpu.VMEM((4, 4, 2, 48, D), bf16),
+            pltpu.VMEM((4, 4, 2, 32, D), bf16),
+            pltpu.VMEM((512, D), bf16),
+            pltpu.VMEM((ROWS, D), bf16),
+            pltpu.VMEM((SEQ, ROWS, 512), bf16),
+            pltpu.VMEM((ROWS, D), bf16),
+            dma((4, 10)), dma((4, 10)), dma((3,)), dma((3,)), dma((3,)), dma((3,)), dma((5,)),
+        ],
+        compiler_params=pltpu.CompilerParams(
+            collective_id=2, has_side_effects=True, vmem_limit_bytes=60 * MIB
+        ),
+        name="attention_forward",
+    )(*arrays)
+
+
 def mlp_kernel(
-    tokens, w_gate, w_up, w_down, first_gu, second_gate, second_up, first_down, second_down,
+    tokens, w_gu, w_down, first_gu, second_gate, second_up, first_down, second_down,
     mixed, out_grad, gain_in, gain_out,
     layer_out, mixed_grad, grad_gate_out, grad_up_out, grad_down_in, grad_gu_in, grad_down_out,
     act_gate, act_up, hidden, latents, down_latents, down_grads, total, thin, thin_gu,
@@ -68,8 +336,17 @@
 ):
     me = lax.axis_index("seq")
     peers = seq_peers()
-    steps = w_gate.shape[0]
+    steps = second_gate.shape[0]
     greet(peers)
+
+    def gate_rows(j):
+        return w_gu[j // 2, pl.ds(2 * lax.rem(j, 2), 2), :, 0:64].reshape(TILE, D)
+
+    def up_rows(j):
+        return w_gu[j // 2, pl.ds(2 * lax.rem(j, 2), 2), :, 64:128].reshape(TILE, D)
+
+    def down_rows(j):
+        return w_down[j // 2, pl.ds(2 * lax.rem(j, 2), 2)].reshape(TILE, D)
 
     def forward(chunk):
         rows = tokens[chunk]
@@ -79,8 +356,8 @@
         thin[...] = jnp.zeros_like(thin)
 
         def step(j, _):
-            gate = dot_nt(rows, w_gate[j]) + dot(latent, second_gate[j])
-            upward = dot_nt(rows, w_up[j]) + dot(latent, second_up[j])
+            gate = dot_nt(rows, gate_rows(j)) + dot(latent, second_gate[j])
+            upward = dot_nt(rows, up_rows(j)) + dot(latent, second_up[j])
             inner = 0.7978845608028654 * (gate + 0.044715 * (gate * gate * gate))
             bent = jnp.tanh(inner)
             half = 0.5 * (1.0 + bent)
@@ -92,7 +369,7 @@
             act_up[j, chunk] = upward * slope
             mid = (gelu * upward).astype(bf16)
             hidden[j, chunk] = mid
-            total[...] += dot(mid, w_down[j])
+            total[...] += dot(mid, down_rows(j))
             thin[...] += dot_nt(mid, first_down[j])
             return 0
 
@@ -142,10 +419,10 @@
         thin_gu[...] = jnp.zeros_like(thin_gu)
 
         def step(j, _):
-            hidden_grad = dot_nt(rows, w_down[j]) + dot(latent_grad, first_down[j])
+            hidden_grad = dot_nt(rows, down_rows(j)) + dot(latent_grad, first_down[j])
             gate_grad = (hidden_grad * act_up[j, chunk]).astype(bf16)
             up_grad = (hidden_grad * act_gate[j, chunk]).astype(bf16)
-            total[...] += dot(gate_grad, w_gate[j]) + dot(up_grad, w_up[j])
+            total[...] += dot(gate_grad, gate_rows(j)) + dot(up_grad, up_rows(j))
             thin_gu[...] += dot_nt(gate_grad, second_gate[j]) + dot_nt(up_grad, second_up[j])
             grad_gate_out[j] += dot_tn(latent, gate_grad)
             grad_up_out[j] += dot_tn(latent, up_grad)
@@ -176,7 +453,7 @@
 
 
 def feed_forward(*arrays):
-    steps = arrays[1].shape[0]
+    steps = 8
     vmem = pl.BlockSpec(memory_space=pltpu.VMEM)
     outs = [
         jax.ShapeDtypeStruct((ROWS, D), bf16),
@@ -216,15 +493,350 @@
     )(*arrays)
 
 
-def project(inputs, weight_rows, down_sel, up_sel):
-    latent = dot_nt(inputs, down_sel).astype(bf16)
-    return dot_nt(inputs, weight_rows) + dot(latent, up_sel), latent
-
-
-def project_back(grad_rows, weight_rows, down_sel, up_sel, inputs, latent):
-    latent_grad = dot_nt(grad_rows, up_sel).astype(bf16)
-    input_cot = dot(grad_rows, weight_rows) + dot(latent_grad, down_sel)
-    return input_cot, dot_tn(latent_grad, inputs), dot_tn(latent, grad_rows)
+EARLY = 52
+LATE = 10
+
+
+class LineSum:
+    def __init__(self, parts, landed, send_sem, recv_sem):
+        self.me, self.peers = lax.axis_index("seq"), seq_peers()
+        self.parts, self.landed, self.send, self.recv = parts, landed, send_sem, recv_sem
+
+    def _copy(self, shift):
+        return remote(
+            self.parts.at[lax.rem(self.me + shift, SEQ)], self.landed.at[shift - 1],
+            self.send.at[shift - 1], self.recv.at[shift - 1], self.peers[shift - 1],
+        )
+
+    def start(self):
+        for shift in (2, 1, 3):
+            self._copy(shift).start()
+
+    def finish(self):
+        for shift in (1, 3, 2):
+            self._copy(shift).wait()
+
+
+class PlaneExchange:
+    def __init__(self, first, second, third, fourth, send_sem, recv_sem):
+        self.x, self.y, self.z, self.core = place()
+        self.first, self.second, self.third, self.fourth = first, second, third, fourth
+        self.send, self.recv = send_sem, recv_sem
+
+    def _copy(self, src, dst, slot, peer):
+        return remote(src, dst, self.send.at[slot], self.recv.at[slot], peer)
+
+    def _along_y(self, k):
+        y = lax.rem(self.y + k, 4)
+        return self._copy(self.first.at[y], self.second.at[k], k - 1, at(self.x, y, self.z, self.core))
+
+    def _along_z(self, k):
+        z = lax.rem(self.z + k, 4)
+        return self._copy(self.second.at[:, z], self.third.at[k], 2 + k, at(self.x, self.y, z, self.core))
+
+    def _across(self):
+        return self._copy(self.third.at[:, :, 1 - self.core], self.fourth, 6, sibling())
+
+    def start(self):
+        for k in (2, 1, 3):
+            self._along_y(k).start()
+        self.second[0] = self.first[self.y]
+
+    def middle(self):
+        for k in (1, 3, 2):
+            self._along_y(k).wait()
+        for k in (2, 1, 3):
+            self._along_z(k).start()
+        self.third[0] = self.second[:, self.z]
+
+    def late(self):
+        for k in (1, 3, 2):
+            self._along_z(k).wait()
+        self._across().start()
+
+    def finish(self):
+        self._across().wait()
+
+    def total(self, chosen, count, out):
+        slots = self.first.shape[3]
+        out[...] = jnp.zeros_like(out)
+
+        def add(i, _):
+            kz, ky = i // 4, lax.rem(i, 4)
+            pair = (lax.rem(self.y + 4 - ky, 4) * 4 + lax.rem(self.z + 4 - kz, 4)) * 2
+            for own in (True, False):
+                source = pair + (self.core if own else 1 - self.core)
+                marks = chosen(source)
+                for slot in range(slots):
+                    held = self.third[kz, ky, self.core, slot] if own else self.fourth[kz, ky, slot]
+                    held = held.astype(f32)
+                    for a in range(count):
+                        out[slot, a] += marks[a : a + 1] * held
+            return 0
+
+        lax.fori_loop(0, 16, add, 0)
+
+
+class LineGather:
+    def __init__(self, buffer, send_sem, recv_sem):
+        self.me, self.peers = lax.axis_index("seq"), seq_peers()
+        self.buffer, self.send, self.recv = buffer, send_sem, recv_sem
+
+    def _copy(self, shift):
+        mine = self.buffer.at[self.me]
+        return remote(mine, mine, self.send.at[shift - 1], self.recv.at[shift - 1], self.peers[shift - 1])
+
+    def start(self):
+        for shift in (2, 1, 3):
+            self._copy(shift).start()
+
+    def finish(self):
+        for shift in (1, 3, 2):
+            self._copy(shift).wait()
+
+
+def attention_back_kernel(
+    layer_input, mixed_grad, attn_proj, context, totals, queries, kv_all,
+    segment_rows, segment_column, gain_first, gain_second,
+    first_qkv, second_q, second_kv, first_o, second_o, qkv_latent, o_latent,
+    got_qkv, kv_rows, got_o,
+    grad_gate_out, grad_up_out, grad_down_in, grad_gu_in, grad_down_out,
+    marks, marks_late,
+    input_grad, all_early, all_late,
+    attn_grad, head_grads, query_grads, centre, key_part, value_part, kv_send, kv_landed, kv_own,
+    packed, early, early_landed, early_sum, e2, e3, e4, early_total, early_line,
+    late, late_landed, late_sum, l2, l3, l4, late_total, late_line,
+    line_s, line_r, kv_s, kv_r, plane_s, plane_r, spread_s, spread_r, out_s, out_r, loc,
+):
+    me, y, z, core = place()
+    line = seq_peers()
+    greet(line + plane_peers() + [sibling()])
+
+    attn_grad[...] = norm_back(attn_proj[...], gain_second[...], mixed_grad[...]).astype(bf16)
+    o_grad = dot_nt(attn_grad[...], second_o[...]).astype(bf16)
+
+    def put(start, rows, buffer):
+        for i in range(rows.shape[1] // 128):
+            buffer[start + i] = rows[:, i * 128 : (i + 1) * 128].astype(bf16)
+
+    for h in range(4):
+        low = (dot_nt(attn_grad[...], got_o[h].reshape(256, D)) + dot(o_grad, first_o[h])).astype(bf16)
+        head_grads[h] = low
+        centre[h] = jnp.sum(low.astype(f32) * context[h], -1, keepdims=True)
+        query_grads[h] = jnp.zeros((ROWS, 256), f32)
+        put(189 + 2 * h, dot_tn(o_grad, context[h].astype(bf16)), early)
+    put(197, dot_tn(o_latent[...], attn_grad[...]), early)
+
+    for j in range(8):
+        packed[0:16, j * TILE : (j + 1) * TILE] = grad_gate_out[j, 0:16].astype(bf16)
+        packed[16:32, j * TILE : (j + 1) * TILE] = grad_up_out[j, 16:32].astype(bf16)
+        packed[32:48, j * TILE : (j + 1) * TILE] = grad_down_in[j].astype(bf16)
+
+    def unpad(j, _):
+        start = jnp.minimum((j * 128 // 216) // 2 * 128, 2048 - 256)
+        lane = start + lax.broadcasted_iota(jnp.int32, (256, 128), 0)
+        within = lane & 63
+        unit = (lane >> 6) * 216 + me * UNITS + within
+        goal = j * 128 + lax.broadcasted_iota(jnp.int32, (256, 128), 1)
+        chosen = jnp.where((unit == goal) & (within < UNITS), 1.0, 0.0).astype(bf16)
+        moved = dot(packed[:, pl.ds(pl.multiple_of(start, 128), 256)], chosen)
+        early[j] = moved[0:16].astype(bf16)
+        early[54 + j] = moved[16:32].astype(bf16)
+        early[108 + j] = moved[32:48].astype(bf16)
+        return 0
+
+    lax.fori_loop(0, 54, unpad, 0)
+    put(162, grad_gu_in[0:16], early)
+    put(171, grad_gu_in[16:32], early)
+    put(180, grad_down_out[...], early)
+    early[206] = jnp.zeros((16, 128), bf16)
+    early[207] = jnp.zeros((16, 128), bf16)
+    early_parts = early.reshape(SEQ, EARLY, 16, 128)
+    e_line = LineSum(early_parts, early_landed, line_s.at[0], line_r.at[0])
+    e_line.start()
+
+    def attend_back(chunk):
+        keys, held = kv_all[chunk, :, 0:256], kv_all[chunk, :, 256:512]
+        allowed = allowed_pairs(segment_rows, segment_column, me, chunk)
+        key_part[...] = jnp.zeros_like(key_part)
+        value_part[...] = jnp.zeros_like(value_part)
+
+        def head(h, _):
+            bent = jnp.tanh(dot_nt(queries[h], keys) * (SCORE / softcap))
+            weight = jnp.where(allowed, jnp.exp(softcap * bent), 0.0).astype(bf16).astype(f32)
+            probs = weight / totals[h]
+            prob_grad = dot_nt(head_grads[h], held)
+            raw_grad = (probs * (prob_grad - centre[h]) * ((1.0 - bent * bent) * SCORE)).astype(bf16)
+            query_grads[h] += dot(raw_grad, keys)
+            key_part[...] += dot_tn(raw_grad, queries[h])
+            value_part[...] += dot_tn(probs.astype(bf16), head_grads[h])
+            return 0
+
+        lax.fori_loop(0, 4, head, 0)
+
+    def kv_copy(shift):
+        peer = line[3 - shift]
+        return remote(kv_send.at[shift - 1], kv_landed.at[shift - 1], kv_s.at[shift - 1], kv_r.at[shift - 1], peer)
+
+    for shift in (3, 2, 1):
+        def earlier(shift=shift):
+            attend_back(me - shift)
+            kv_send[shift - 1, :, 0:256] = key_part[...].astype(bf16)
+            kv_send[shift - 1, :, 256:512] = value_part[...].astype(bf16)
+            kv_copy(shift).start()
+
+        pl.when(me >= shift)(earlier)
+
+    e_line.finish()
+
+    def add_early(i, _):
+        own = early_parts[me, i].astype(f32)
+        for s in range(3):
+            own = own + early_landed[s, i].astype(f32)
+        early_sum[i] = own.astype(bf16)
+        return 0
+
+    lax.fori_loop(0, EARLY, add_early, 0)
+    for i in range(EARLY, 64):
+        early_sum[i] = jnp.zeros((16, 128), bf16)
+    e_plane = PlaneExchange(early_sum.reshape(4, 4, 2, 2, 16, 128), e2, e3, e4, plane_s.at[0], plane_r.at[0])
+    e_plane.start()
+
+    attend_back(me)
+    kv_own[:, 0:256] = key_part[...]
+    kv_own[:, 256:512] = value_part[...]
+    e_plane.middle()
+    for shift in (1, 2, 3):
+        def landed(shift=shift):
+            kv_copy(shift).wait_recv()
+            kv_own[...] += kv_landed[shift - 1].astype(f32)
+
+        pl.when(me + shift < SEQ)(landed)
+    e_plane.late()
+
+    key_value = kv_own[...].astype(bf16)
+    values = layer_input[...].astype(f32)
+    first_norm = normed(values, gain_first[...]).astype(bf16)
+    thin = dot_nt(key_value, second_kv[...])
+    total = dot(key_value, kv_rows[...])
+    for h in range(4):
+        low = query_grads[h].astype(bf16)
+        total = total + dot(low, got_qkv[h, :, :, 0:32].reshape(256, D))
+        thin = thin + dot_nt(low, second_q[h])
+        put(27 + 2 * h, dot_tn(qkv_latent[...], low)[0:16], late)
+    qkv_grad = thin.astype(bf16)
+    total = total + dot(qkv_grad, first_qkv[...])
+    e_plane.finish()
+    e_plane.total(lambda s: marks[s], 8, early_total)
+    early_line[me] = early_total[...].astype(bf16)
+    e_spread = LineGather(early_line, spread_s.at[0], spread_r.at[0])
+    e_spread.start()
+
+    in_grad = dot_tn(qkv_grad, first_norm)
+    for i in range(3):
+        put(9 * i, in_grad[16 * i : 16 * i + 16], late)
+    kv_out_grad = dot_tn(qkv_latent[...], key_value)
+    put(35, kv_out_grad[16:32, 0:256], late)
+    put(37, kv_out_grad[32:48, 256:512], late)
+    late[39] = jnp.zeros((16, 128), bf16)
+    late_parts = late.reshape(SEQ, LATE, 16, 128)
+    l_line = LineSum(late_parts, late_landed, line_s.at[1], line_r.at[1])
+    l_line.start()
+    input_grad[...] = (mixed_grad[...] + norm_back(values, gain_first[...], total)).astype(bf16)
+
+    e_spread.finish()
+    own_early = pltpu.make_async_copy(early_line, all_early.at[y, z, core], loc.at[0])
+    own_early.start()
+    e_out = PlaneGather(early_line, all_early, out_s.at[0], out_r.at[0])
+    e_out.start()
+
+    l_line.finish()
+    for i in range(LATE):
+        own = late_parts[me, i].astype(f32)
+        for s in range(3):
+            own = own + late_landed[s, i].astype(f32)
+        low = own.astype(bf16)
+        for k in range(3 if i < LATE - 1 else 5):
+            late_sum[3 * i + k, 0] = low
+    l_plane = PlaneExchange(late_sum.reshape(4, 4, 2, 1, 16, 128), l2, l3, l4, plane_s.at[1], plane_r.at[1])
+    l_plane.start()
+    l_plane.middle()
+    l_plane.late()
+    l_plane.finish()
+    group = lax.rem((y * 4 + z) * 2 + core, 3)
+    l_plane.total(lambda s: marks_late[group, s], 3, late_total)
+    late_line[me] = late_total[...].astype(bf16)
+    l_spread = LineGather(late_line, spread_s.at[1], spread_r.at[1])
+    l_spread.start()
+    own_early.wait()
+    e_out.middle()
+    l_spread.finish()
+    own_late = pltpu.make_async_copy(late_line, all_late.at[y, z, core], loc.at[1])
+    own_late.start()
+    l_out = PlaneGather(late_line, all_late, out_s.at[1], out_r.at[1])
+    l_out.start()
+    own_late.wait()
+    l_out.middle()
+    e_out.late()
+    l_out.late()
+    e_out.finish()
+    l_out.finish()
+    for shift in (1, 2, 3):
+        pl.when(me >= shift)(lambda shift=shift: kv_copy(shift).wait_send())
+
+
+def attention_back(*arrays):
+    vmem = pl.BlockSpec(memory_space=pltpu.VMEM)
+    hbm = pl.BlockSpec(memory_space=pl.ANY)
+    shape = jax.ShapeDtypeStruct
+    dma = pltpu.SemaphoreType.DMA
+
+    def reduction(blocks, slots, count):
+        return [
+            pltpu.VMEM((SEQ * blocks, 16, 128), bf16),
+            pltpu.VMEM((3, blocks, 16, 128), bf16),
+            pltpu.VMEM((32 * slots, 16, 128) if slots > 1 else (32, 1, 16, 128), bf16),
+            pltpu.VMEM((4, 4, 2, slots, 16, 128), bf16),
+            pltpu.VMEM((4, 4, 2, slots, 16, 128), bf16),
+            pltpu.VMEM((4, 4, slots, 16, 128), bf16),
+            pltpu.VMEM((slots, count, 16, 128), f32),
+            pltpu.VMEM((SEQ, slots, count, 16, 128), bf16),
+        ]
+
+    return pl.pallas_call(
+        attention_back_kernel,
+        out_shape=[
+            shape((ROWS, D), bf16),
+            shape((4, 4, 2, SEQ, 2, 8, 16, 128), bf16),
+            shape((4, 4, 2, SEQ, 1, 3, 16, 128), bf16),
+        ],
+        in_specs=[vmem] * len(arrays),
+        out_specs=[vmem, hbm, hbm],
+        scratch_shapes=[
+            pltpu.VMEM((ROWS, D), bf16),
+            pltpu.VMEM((4, ROWS, 256), bf16),
+            pltpu.VMEM((4, ROWS, 256), f32),
+            pltpu.VMEM((4, ROWS, 1), f32),
+            pltpu.VMEM((ROWS, 256), f32),
+            pltpu.VMEM((ROWS, 256), f32),
+            pltpu.VMEM((3, ROWS, 512), bf16),
+            pltpu.VMEM((3, ROWS, 512), bf16),
+            pltpu.VMEM((ROWS, 512), f32),
+            pltpu.VMEM((48, 2048), bf16),
+        ]
+        + reduction(EARLY, 2, 8)
+        + reduction(LATE, 1, 3)
+        + [dma((2, 3))] * 2
+        + [dma((3,))] * 2
+        + [dma((2, 7))] * 2
+        + [dma((2, 3))] * 2
+        + [dma((2, 10))] * 2
+        + [dma((2,))],
+        compiler_params=pltpu.CompilerParams(
+            collective_id=3, has_side_effects=True, vmem_limit_bytes=60 * MIB
+        ),
+        name="attention_back",
+    )(*arrays)
 
 
 def my_quarter(rows, axis):
@@ -244,25 +856,23 @@
 ):
     me = lax.axis_index("seq")
     shards = 32
-    x = layer_input[0].astype(f32)
     cotangent = out_grad[0]
     chosen = adapter_ids[0]
+    ids = lax.all_gather(adapter_ids, "dp", axis=0, tiled=True)
+    marks = (ids[:, None] == jnp.arange(9)[None, :]).astype(f32)
+    marks_late = jnp.pad(marks.reshape(32, 3, 3).transpose(1, 0, 2), ((0, 0), (0, 0), (0, 5)))
+    marks_late = jnp.broadcast_to(marks_late[..., None], (3, 32, 8, 128))
+    marks = jnp.broadcast_to(marks[:, :8, None], (32, 8, 128))
     pick = lambda table: lax.dynamic_index_in_dim(table, chosen, 0, keepdims=False)
     qkv_in, q_out, kv_out = pick(qkv_adapt_in), pick(q_adapt_out), pick(kv_adapt_out)
     o_in, o_out = pick(o_adapt_in), pick(o_adapt_out)
     mlp_in, mlp_out = pick(mlp_adapt_in), pick(mlp_adapt_out)
     down_in, down_out = pick(down_adapt_in), pick(down_adapt_out)
 
-    attn_pack = jnp.concatenate([w_query.T, w_key.T, w_value.T, w_out], 0)
-    attn_all = lax.all_gather(attn_pack, "dp", axis=0, tiled=False)
-    wq = attn_all[:, :32].reshape(1024, D)
-    wk = attn_all[:, 32:40].reshape(256, D)
-    wv = attn_all[:, 40:48].reshape(256, D)
-    wo = attn_all[:, 48:].reshape(1024, D)
-    mlp_pack = jnp.stack([my_quarter(w_gate.T, 0), my_quarter(w_up.T, 0), my_quarter(w_down, 0)])
-    mlp_all = lax.all_gather(mlp_pack, "dp", axis=1, tiled=True)
+    pack_qkv = jnp.concatenate([w_query.T, w_key.T, w_value.T], 0)
+    pack_gu = jnp.concatenate([my_quarter(w_gate.T, 0), my_quarter(w_up.T, 0)], 0)
+    pack_down = my_quarter(w_down, 0)
     steps = shards * BLOCK // TILE
-    mlp_all = mlp_all.reshape(3, steps, TILE, D)
 
     def hidden_slice(table):
         part = my_quarter(table.reshape(16, shards, 216), 2)
@@ -273,81 +883,68 @@
     second_up = jnp.concatenate([zeros, hidden_slice(mlp_out[1])], 1)
     first_down = hidden_slice(down_in)
 
-    first_norm = normed(x, gain_attn_in).astype(bf16)
-    q, q_latent = project(first_norm, wq, qkv_in[0], q_out)
-    k, k_latent = project(first_norm, wk, qkv_in[1], kv_out[0])
-    v, v_latent = project(first_norm, wv, qkv_in[2], kv_out[1])
-    q = q.astype(bf16).reshape(ROWS, 4, 256)
-    kv = jnp.concatenate([k, v], 1).astype(bf16)
-    kv_all = lax.all_gather(kv, "seq", axis=0, tiled=True)
-    keys, values = kv_all[:, :256], kv_all[:, 256:]
     segments = segment_ids[0]
     mine = lax.dynamic_slice_in_dim(segments, me * ROWS, ROWS)
-    position = me * ROWS + jnp.arange(ROWS)
-    allowed = (mine[:, None] == segments[None]) & (jnp.arange(1024)[None] <= position[:, None])
-    scale = 1.0 / 16.0
-    raw = jnp.einsum("qhe,ke->hqk", q, keys, preferred_element_type=f32)
-    bent = jnp.tanh(raw * (scale / softcap))
-    exponent = jnp.where(allowed[None], jnp.exp(softcap * bent), 0.0)
-    probs = exponent / jnp.sum(exponent, -1, keepdims=True)
-    probs_low = probs.astype(bf16)
-    context = jnp.einsum("hqk,ke->qhe", probs_low, values, preferred_element_type=f32)
-    context = context.astype(bf16).reshape(ROWS, 1024)
-    o_latent = dot_nt(context, o_in).astype(bf16)
-    attn_proj = dot(context, wo) + dot(o_latent, o_out)
-    mixed = x + normed(attn_proj, gain_attn_out)
-    second_norm = normed(mixed, gain_mlp_in).astype(bf16)
-    tokens = lax.all_gather(second_norm, "seq", axis=0, tiled=False)
-
+    second_q = jnp.pad(q_out, ((0, 32), (0, 0))).reshape(48, 4, 256).transpose(1, 0, 2)
+    blank = jnp.zeros((16, 256), bf16)
+    second_kv = jnp.concatenate(
+        [
+            jnp.zeros((16, 512), bf16),
+            jnp.concatenate([kv_out[0], blank], 1),
+            jnp.concatenate([blank, kv_out[1]], 1),
+        ],
+        0,
+    )
+    (
+        w_gu_all, w_down_all, tokens, qkv_all, kv_rows, o_all, kv_all,
+        q, totals, context, attn_proj, mixed, qkv_latent, o_latent,
+    ) = attention_forward(
+        layer_input[0], pack_qkv, w_out, pack_gu, pack_down,
+        segments.reshape(SEQ, 1, ROWS), mine[:, None],
+        gain_attn_in[None], gain_attn_out[None], gain_mlp_in[None],
+        qkv_in.reshape(48, D), second_q, second_kv,
+        o_in.reshape(16, 4, 256).transpose(1, 0, 2), o_out,
+    )
     layer_out, mixed_grad, g_gate, g_up, g_down_in, g_gu_in, g_down_out = feed_forward(
-        tokens, mlp_all[0], mlp_all[1], mlp_all[2], mlp_in.reshape(32, D),
+        tokens, w_gu_all, w_down_all, mlp_in.reshape(32, D),
         second_gate, second_up, first_down, down_out,
         mixed, cotangent, gain_mlp_in[None], gain_mlp_out[None],
     )
 
-    def hidden_full(part):
-        part = part.transpose(1, 0, 2).reshape(16, shards, BLOCK)[:, :, :UNITS]
-        full = jnp.zeros((16, shards, 4, UNITS), f32)
-        full = lax.dynamic_update_slice_in_dim(full, part[:, :, None], me, 2)
-        return full.reshape(16, shards * 4 * UNITS)
-
-    attn_grad = norm_back(attn_proj, gain_attn_out, mixed_grad).astype(bf16)
-    o_latent_grad = dot_nt(attn_grad, o_out).astype(bf16)
-    context_grad = (dot_nt(attn_grad, wo) + dot(o_latent_grad, o_in)).astype(bf16)
-    g_o_in = dot_tn(o_latent_grad, context)
-    g_o_out = dot_tn(o_latent, attn_grad)
-    head_grads = context_grad.reshape(ROWS, 4, 256)
-    prob_grad = jnp.einsum("qhe,ke->hqk", head_grads, values, preferred_element_type=f32)
-    centre = jnp.sum(probs * prob_grad, -1, keepdims=True)
-    raw_grad = (probs * (prob_grad - centre) * (1.0 - bent * bent) * scale).astype(bf16)
-    q_grad = jnp.einsum("hqk,ke->qhe", raw_grad, keys, preferred_element_type=f32)
-    q_grad = q_grad.astype(bf16).reshape(ROWS, 1024)
-    k_part = jnp.einsum("hqk,qhe->ke", raw_grad, q, preferred_element_type=f32)
-    v_part = jnp.einsum("hqk,qhe->ke", probs_low, head_grads, preferred_element_type=f32)
-    kv_grad = lax.psum_scatter(
-        jnp.concatenate([k_part, v_part], 1).astype(bf16), "seq", scatter_dimension=0, tiled=True
+    input_grad, all_early, all_late = attention_back(
+        layer_input[0], mixed_grad, attn_proj, context, totals, q, kv_all,
+        segments.reshape(SEQ, 1, ROWS), mine[:, None], gain_attn_in[None], gain_attn_out[None],
+        qkv_in.reshape(48, D), second_q, second_kv,
+        o_in.reshape(16, 4, 256).transpose(1, 0, 2), o_out, qkv_latent, o_latent,
+        qkv_all, kv_rows, o_all,
+        g_gate, g_up, g_down_in, g_gu_in, g_down_out,
+        marks, marks_late,
     )
-    k_grad, v_grad = kv_grad[:, :256], kv_grad[:, 256:]
-    q_cot, g_q_in, g_q_out = project_back(q_grad, wq, qkv_in[0], q_out, first_norm, q_latent)
-    k_cot, g_k_in, g_k_out = project_back(k_grad, wk, qkv_in[1], kv_out[0], first_norm, k_latent)
-    v_cot, g_v_in, g_v_out = project_back(v_grad, wv, qkv_in[2], kv_out[1], first_norm, v_latent)
-    input_grad = (mixed_grad + norm_back(x, gain_attn_in, q_cot + k_cot + v_cot)).astype(bf16)
-
-    picked = (
-        jnp.stack([g_q_in, g_k_in, g_v_in]),
-        g_q_out,
-        jnp.stack([g_k_out, g_v_out]),
-        g_o_in,
-        g_o_out,
-        g_gu_in.reshape(2, 16, D),
-        jnp.stack([hidden_full(g_gate[:, :16]), hidden_full(g_up[:, 16:])]),
-        hidden_full(g_down_in),
-        g_down_out,
+    early = all_early.reshape(32, SEQ, 2, 8, 16, 128).transpose(1, 0, 2, 3, 4, 5)
+    early = early.reshape(SEQ, 64, 8, 16, 128)[:, :EARLY].reshape(SEQ * EARLY, 8, 16, 128)
+    late = all_late.reshape(32, SEQ, 3, 16, 128)[:30].reshape(LATE, 3, SEQ, 3, 16, 128)
+    late = late.transpose(2, 0, 1, 3, 4, 5).reshape(SEQ * LATE, 9, 16, 128)[:, :8]
+
+    def table(blocks, start, count):
+        part = blocks[start : start + count].transpose(1, 2, 0, 3)
+        return part.reshape(8, 16, count * 128).astype(f32)
+
+    def tables(blocks, start, count, many):
+        return jnp.stack([table(blocks, start + i * count, count) for i in range(many)], 1)
+
+    return (
+        layer_out[None],
+        input_grad[None],
+        tables(late, 0, 9, 3),
+        table(late, 27, 8),
+        tables(late, 35, 2, 2),
+        table(early, 189, 8),
+        table(early, 197, 9),
+        tables(early, 162, 9, 2),
+        tables(early, 0, 54, 2),
+        table(early, 108, 54),
+        table(early, 180, 9),
     )
-    chooser = (chosen == jnp.arange(8)).astype(f32)
-    spread = tuple(chooser.reshape((8,) + (1,) * g.ndim) * g[None] for g in picked)
-    summed = lax.psum(spread, ("dp", "seq"))
-    return (layer_out[None], input_grad[None]) + tuple(summed)
 
 
 def solution(mesh):

time: 677 us -> 429 us (0.63)
  waiting for transfers between devices: 377 us -> 0 us
  Pallas kernels: 109 us -> 321 us
  matrix products: 59 us -> 0 us
  blocking collectives: 0 us -> 19.5 us
  local copies, waits for them, and re-layouts: 82.3 us -> 67.6 us
  between operations: 16 us -> 2.38 us
  other arithmetic: 23.2 us -> 10.4 us
    psum x1 -> x0, waiting for transfers between devices: 219 us -> none  [body(): summed = lax.psum(spread, ('dp', 'seq'))]
    pallas_call x0 -> x2, Pallas kernels: none -> 209 us  [the longest x1 105 us: attention_forward(): pl.pallas_call(attention_kernel, out_shape=[s for s, _ in outs], in_specs...]
    all_gather x4 -> x0, waiting for transfers between devices: 132 us -> none  [the longest x1 49.4 us: body(): attn_all = lax.all_gather(attn_pack, 'dp', axis=0, tiled=False)]
    dot_general x38 -> x0, matrix products: 59 us -> none  [the longest x12 14.1 us: dot_nt(): lax.dot_general(a, b, (((1,), (1,)), ((), ())), preferred_element_type=f32)]
    reduce_scatter x1 -> x0, waiting for transfers between devices: 26.4 us -> none  [body(): lax.psum_scatter(jnp.concatenate([k_part, v_part], 1).astype(bf16), 'seq'...]
    dynamic_update_slice x3 -> x0, local copies, waits for them, and re-layouts: 23.3 us -> none  [hidden_full(): full = lax.dynamic_update_slice_in_dim(full, part[:, :, None], me, 2)]
    unnamed x0 -> x1, blocking collectives: none -> 19.5 us
    convert_element_type x0 -> x23, local copies, waits for them, and re-layouts: none -> 16.9 us  [table(): return part.reshape(8, 16, count * 128).astype(f32)]
  transfers between devices with their start and end apart: 6 -> 0, of which waited for: 6 -> 0; matrix products, arithmetic and copies ran while one was open for 9% -> 0% of each run, Pallas kernels for 0% -> 0%
where the time goes in v2:
time: 429 us; the launch traced here: 421 us
  Pallas kernels  321 us (75%)
  local copies, waits for them, and re-layouts  67.6 us (16%)
  blocking collectives  19.5 us (5%)
  other arithmetic  10.4 us (2%)
    pallas_call x1, Pallas kernels, feed_forward(): pl.pallas_call(mlp_kernel, out_shape=outs, in_specs=[vmem] * len(arrays),...  112 us
    pallas_call x1, Pallas kernels, attention_forward(): pl.pallas_call(attention_kernel, out_shape=[s for s, _ in outs], in_specs...  105 us
    pallas_call x1, Pallas kernels, attention_back(): pl.pallas_call(attention_back_kernel, out_shape=[shape((ROWS, D), bf16),...  104 us
    unnamed x1, blocking collectives  19.5 us
    convert_element_type x23, local copies, waits for them, and re-layouts, table(): return part.reshape(8, 16, count * 128).astype(f32)  16.9 us
    unnamed x39, local copies, waits for them, and re-layouts  11.3 us
    reshape x1, local copies, waits for them, and re-layouts, body(): all_early.reshape(32, SEQ, 2, 8, 16, 128).transpose(1, 0, 2, 3, 4, 5)  10.3 us

profile of v2, /device:TPU:1, one launch (start us, length us, event | category | flops | bytes accessed | tf_op | source)
XLA Modules:
  0.0 421.0 jit_solution(17983629012979180576)
XLA Ops:
  1.5 0.7 dynamic-slice_bitcast_fusion.6
  2.2 0.7 fusion.7.second_kv
  2.9 1.0 dynamic-slice_bitcast_fusion
  4.0 0.7 fusion.2.pack_gu
  4.7 0.8 dynamic-slice_bitcast_fusion.4
  6.1 1.5 constant_dynamic-slice_fusion.8
  7.7 0.8 constant_dynamic-slice_fusion.7
  9.1 1.4 dynamic-slice_bitcast_fusion.3.second_o
  10.5 0.9 constant_dynamic-slice_fusion.10
  11.4 0.7 pad.37.pack_down
  12.1 0.7 fusion.9
  12.8 0.8 copy.60.segment_column
  15.4 0.7 pad_maximum_fusion.pack_qkv
  16.0 104.6 %attention_forward.1 = (bf16[4,4,2,128,1152]{4,3,2,1,0:T(8,128)(2,1)}, bf16[4,4,2,64,1152]{4,3,2,1,0:T(8,128)(2,1)}, bf16[4,256,1152]{2,1,0:T(8,128)(2,1)}, bf16...) custom-call(bf16[256,1152]{1,0:T(8,128)(2,1)} %bitcast.122, ...), custom_call_target="tpu_custom_call" | custom-call | tf_op jit(solution)/shard_map/attention_forward/pallas_call | solution.py:308
  120.7 1.1 constant_dynamic-slice_fusion.5
  121.8 0.8 reshape_squeeze.12
  122.6 0.8 reshape.235
  123.8 0.7 concatenate.27.second_up
  125.3 0.8 reshape_squeeze.11
  126.4 0.7 concatenate.26.second_gate
  127.1 1.5 constant_dynamic-slice_fusion.6
  128.6 1.4 dynamic-slice_bitcast_fusion.2.second_down
  130.6 112.3 %feed_forward.1 = (bf16[256,1152]{1,0:T(8,128)(2,1)}, f32[256,1152]{1,0:T(8,128)}, f32[8,32,256]{2,1,0:T(8,128)}, f32[8,32,256]{2,1,0:T(8,128)}, f32[8,16,256]{2...) custom-call(bf16[4,256,1152]{2,1,0:T(8,128)(2,1)} %get-tuple-element.35.tokens, ...), custom_call_target="tpu_custom_call" | custom-call | tf_op jit(solution)/shard_map/feed_forward/pallas_call | solution.py:467
  243.5 0.8 dynamic-update-slice
  244.2 19.5 %all-reduce.12 = s32[32]{0:T(128)S(1)} all-reduce(s32[32]{0:T(128)S(1)} %dynamic-update-slice), channel_id=1, replica_groups=mesh['dp'=32,'seq'=4] {'dp'}, use_global_device_ids=true, to_apply=%add.12 | all-reduce | flops 32 | bytes 256
  263.8 0.9 broadcast_in_dim.52.marks_late
  264.8 0.8 broadcast_in_dim.51.marks
  265.5 104.2 %attention_back.1 = (bf16[256,1152]{1,0:T(8,128)(2,1)}, bf16[4,4,2,4,2,8,16,128]{7,6,5,4,3,2,1,0:T(8,128)(2,1)}, bf16[4,4,2,4,1,3,16,128]{7,6,5,4,3,2,1,0:T(8,128)(2,1)}) custom-call(bf16[256,1152]{1,0:T(8,128)(2,1)} %bitcast.123, f32[256,1152]{1,0:T(8,128)} %get-tuple-element.40.mixed_grad, f32[256,1152]{1,0:T(8,128)} %get-tuple-element.41.attn_proj, ...), custom_call_target="tpu_custom_call" | custom-call | tf_op jit(solution)/shard_map/attention_back/pallas_call | solution.py:806
  369.8 10.3 %copy.72 = bf16[32,4,2,8,16,128]{5,4,3,2,0,1:T(8,128)(2,1)} copy(bf16[32,4,2,8,16,128]{5,4,3,2,1,0:T(8,128)(2,1)} %bitcast.117) | data formatting | bytes 16777216 | tf_op jit(solution)/shard_map/reshape | solution.py:923
  380.1 4.7 %slice.106 = bf16[4,52,8,16,128]{4,3,2,1,0:T(8,128)(2,1)S(1)} slice(bf16[4,64,8,16,128]{4,3,2,1,0:T(8,128)(2,1)} %bitcast.113), slice={[0:4], [0:52], [0:8], [0:16], [0:128]} | slice | bytes 13631488 | tf_op jit(solution)/shard_map/slice | solution.py:924
  384.8 3.4 convert_bitcast_fusion
  388.6 2.4 copy.77
  391.0 2.8 convert_element_type.210
  393.9 2.4 copy.78
  396.2 3.1 convert_element_type.212
  399.9 3.4 copy.84
  403.3 1.5 convert_bitcast_fusion.1
  405.7 1.1 copy.83
  406.8 1.2 copy-done.3
  408.0 2.0 copy.101
  410.0 0.9 copy.102
  410.9 0.9 copy.103
  411.7 1.8 copy_bitcast_fusion.3
  414.4 0.7 copy.82
  416.7 1.3 copy.81
  418.0 0.8 copy_bitcast_fusion.4
  418.9 0.8 copy.113
  419.7 0.8 copy.114
  (79 shorter events, 10.1 us)
Async XLA Ops:
  0.6 121.9 %copy-start = (bf16[8,16,6912]{2,1,0:T(8,128)(2,1)S(1)}, bf16[8,16,6912]{2,1,0:T(8,128)(2,1)}, u32[]{:S(2)}) copy-start(bf16[8,16,6912]{2,1,0:T(8,128)(2,1)} %param.46) | copy-start | bytes 5308420
  0.7 12.9 %copy-start.10 = (f32[1152]{0:T(1024)S(1)}, f32[1152]{0:T(1024)}, u32[]{:S(2)}) copy-start(f32[1152]{0:T(1024)} %param.28) | copy-start | bytes 13828
  0.7 13.5 %copy-start.11 = (f32[1152]{0:T(1024)S(1)}, f32[1152]{0:T(1024)}, u32[]{:S(2)}) copy-start(f32[1152]{0:T(1024)} %param.29) | copy-start | bytes 13828
  0.7 14.1 %copy-start.12 = (f32[1152]{0:T(1024)S(1)}, f32[1152]{0:T(1024)}, u32[]{:S(2)}) copy-start(f32[1152]{0:T(1024)} %param.30) | copy-start | bytes 13828
  0.7 14.7 %copy-start.7 = (bf16[1152,32]{0,1:T(8,128)(2,1)S(1)}, bf16[1152,32]{0,1:T(8,128)(2,1)}, u32[]{:S(2)}) copy-start(bf16[1152,32]{0,1:T(8,128)(2,1)} %param.32) | copy-start | bytes 221188
  0.7 14.7 %copy-start.9 = (bf16[1152,8]{0,1:T(8,128)(2,1)S(1)}, bf16[1152,8]{0,1:T(8,128)(2,1)}, u32[]{:S(2)}) copy-start(bf16[1152,8]{0,1:T(8,128)(2,1)} %param.33) | copy-start | bytes 55300
  0.7 14.7 %copy-start.8 = (bf16[1152,8]{0,1:T(8,128)(2,1)S(1)}, bf16[1152,8]{0,1:T(8,128)(2,1)}, u32[]{:S(2)}) copy-start(bf16[1152,8]{0,1:T(8,128)(2,1)} %param.34) | copy-start | bytes 55300
  123.4 6.6 %copy-start.13 = (f32[1152]{0:T(1024)S(1)}, f32[1152]{0:T(1024)}, u32[]{:S(2)}) copy-start(f32[1152]{0:T(1024)} %param.31) | copy-start | bytes 13828
  130.6 112.3 %copy-start.14 = (u32[128]{0:T(128)S(1)}, u32[128]{0:T(128)}, u32[]{:S(2)}) copy-start(u32[128]{0:T(128)} %constant.93) | copy-start | bytes 1540
  384.8 3.8 copy-start.2
  405.6 2.4 copy-start.3
  410.0 3.5 copy-start.4
  416.7 2.2 copy-start.5
  416.7 3.8 copy-start.1
  418.0 1.7 copy-start.6

commit v3 on v2

v3 whole, which is shorter than its diff:
```python
import functools

import jax
import jax.numpy as jnp
from jax import lax
from jax.experimental import pallas as pl
from jax.experimental.pallas import tpu as pltpu
from jax.sharding import PartitionSpec as P

epsilon = 1e-06
softcap = 50.0
MESH = pl.DeviceIdType.MESH
bf16 = jnp.bfloat16
f32 = jnp.float32

D = 1152
SEQ = 4
ROWS = 256
UNITS = 54
BLOCK = 64
TILE = 256
MIB = 1 << 20


def dot(a, b):
    return lax.dot_general(a, b, (((1,), (0,)), ((), ())), preferred_element_type=f32)


def dot_nt(a, b):
    return lax.dot_general(a, b, (((1,), (1,)), ((), ())), preferred_element_type=f32)


def dot_tn(a, b):
    return lax.dot_general(a, b, (((0,), (0,)), ((), ())), preferred_element_type=f32)


def normed(values, gain_vector):
    return values * lax.rsqrt(jnp.mean(values * values, -1, keepdims=True) + epsilon) * gain_vector


def norm_back(values, gain_vector, cotangent):
    inverse = lax.rsqrt(jnp.mean(values * values, -1, keepdims=True) + epsilon)
    scaled = cotangent * gain_vector
    mean_part = jnp.mean(scaled * values, -1, keepdims=True)
    return inverse * (scaled - values * (inverse * inverse * mean_part))


def seq_peers():
    dp, me = lax.axis_index("dp"), lax.axis_index("seq")
    return [(dp, lax.rem(me + shift, SEQ)) for shift in (1, 2, 3)]


def greet(peers):
    barrier = pltpu.get_barrier_semaphore()
    for peer in peers:
        pl.semaphore_signal(barrier, inc=1, device_id=peer, device_id_type=MESH)
    pl.semaphore_wait(barrier, len(peers))


def staged_call(kernel, name, operands, kinds, results, scratch, collective_id=None):
    count, made = len(operands), len(results)
    held = [i for i in range(count) if kinds[i] == "v"]
    given = [i for i in range(made) if results[i][2] == "v"]

    def body(*refs):
        outer = list(refs[: count + made])
        inner = list(outer)
        rest = refs[count + made :]
        for n, i in enumerate(held):
            inner[i] = rest[n]
        for n, i in enumerate(given):
            inner[count + i] = rest[len(held) + n]
        sems, rest = rest[len(held) + len(given)], rest[len(held) + len(given) + 1 :]
        ins = {i: pltpu.make_async_copy(outer[i], inner[i], sems.at[n]) for n, i in enumerate(held)}
        outs = {
            i: pltpu.make_async_copy(inner[count + i], outer[count + i], sems.at[len(held) + n])
            for n, i in enumerate(given)
        }
        waiting, leaving = set(ins), []
        for moving in ins.values():
            moving.start()

        def arrive(*which):
            for i in which or sorted(waiting):
                if i in waiting:
                    waiting.discard(i)
                    ins[i].wait()

        def leave(*which):
            for i in which:
                outs[i].start()
                leaving.append(i)

        kernel(arrive, leave, *inner, *rest)
        leave(*[i for i in given if i not in leaving])
        for i in given:
            outs[i].wait()

    spaces = {"v": pl.ANY, "h": pl.ANY, "s": pltpu.SMEM}
    params = dict(vmem_limit_bytes=62 * MIB)
    if collective_id is not None:
        params.update(collective_id=collective_id, has_side_effects=True)
    return pl.pallas_call(
        body,
        out_shape=[jax.ShapeDtypeStruct(shape, dtype) for shape, dtype, _ in results],
        in_specs=[pl.BlockSpec(memory_space=spaces[k]) for k in kinds],
        out_specs=[pl.BlockSpec(memory_space=pl.ANY)] * made,
        scratch_shapes=[pltpu.VMEM(operands[i].shape, operands[i].dtype) for i in held]
        + [pltpu.VMEM(results[i][0], results[i][1]) for i in given]
        + [pltpu.SemaphoreType.DMA((len(held) + len(given),))]
        + scratch,
        compiler_params=pltpu.CompilerParams(**params),
        name=name,
    )(*operands)


def place():
    dp = lax.axis_index("dp")
    return lax.axis_index("seq"), dp // 8, lax.rem(dp // 2, 4), lax.rem(dp, 2)


def at(x, y, z, core):
    return ((lax.rem(y, 4) * 4 + lax.rem(z, 4)) * 2 + core, lax.rem(x, 4))


def plane_peers():
    x, y, z, core = place()
    return [at(x, y + k, z, core) for k in (1, 2, 3)] + [at(x, y, z + k, core) for k in (1, 2, 3)]


def sibling():
    x, y, z, core = place()
    return at(x, y, z, 1 - core)


def remote(src, dst, send_sem, recv_sem, peer):
    return pltpu.make_async_remote_copy(
        src_ref=src, dst_ref=dst, send_sem=send_sem, recv_sem=recv_sem,
        device_id=peer, device_id_type=MESH,
    )


class PlaneGather:
    def __init__(self, own, buffer, send_sem, recv_sem):
        self.x, self.y, self.z, self.core = place()
        self.own, self.buffer, self.send, self.recv = own, buffer, send_sem, recv_sem

    def _copy(self, src, dst, slot, peer):
        return remote(src, dst, self.send.at[slot], self.recv.at[slot], peer)

    def _first(self, k):
        x, y, z, core = self.x, self.y, self.z, self.core
        peer = at(x, y + k * (1 - core), z + k * core, core)
        return self._copy(self.own, self.buffer.at[y, z, core], k - 1, peer)

    def _line(self, core, back):
        if core == 0:
            return self.buffer.at[:, lax.rem(self.z + 4 - back, 4), 0]
        return self.buffer.at[lax.rem(self.y + 4 - back, 4), :, 1]

    def _second(self, core, k):
        line = self._line(core, 0)
        peer = at(self.x, self.y + k * core, self.z + k * (1 - core), core)
        return self._copy(line, line, 2 + k, peer)

    def _pass(self, core, half):
        back, k = ((1, 1), (3, 3))[half]
        line = self._line(core, back).at[2 * half : 2 * half + 2]
        peer = at(self.x, self.y + k * core, self.z + k * (1 - core), core)
        return self._copy(line, line, (4, 10)[half], peer)

    def _swap(self, core, back):
        line = self._line(core, back)
        return self._copy(line, line, 6 + back, at(self.x, self.y, self.z, 1 - core))

    def _both(self, act):
        for core in (0, 1):
            pl.when(self.core == core)(functools.partial(act, core))

    def start(self):
        for k in (2, 1, 3):
            self._first(k).start()

    def middle(self):
        for k in (1, 3, 2):
            self._first(k).wait()

        def act(core):
            for k in (1, 3):
                self._second(core, k).start()
            self._swap(core, 0).start()

        self._both(act)

    def late(self):
        def act(core):
            for half, k in ((0, 1), (1, 3)):
                self._second(core, k).wait()
                self._pass(core, half).start()
                self._swap(core, k).start()

        self._both(act)

    def last(self):
        def act(core):
            for half in (0, 1):
                self._pass(core, half).wait()
            self._swap(core, 2).start()

        self._both(act)

    def finish(self):
        def act(core):
            for back in (0, 1, 3, 2):
                self._swap(core, back).wait()

        self._both(act)


def allowed_pairs(segment_rows, segment_column, me, chunk):
    keys = lax.broadcasted_iota(jnp.int32, (ROWS, ROWS), 1) + chunk * ROWS
    queries = lax.broadcasted_iota(jnp.int32, (ROWS, ROWS), 0) + me * ROWS
    return (segment_column[...] == segment_rows[chunk]) & (keys <= queries)


SCORE = 1.0 / 16.0


def attention_kernel(
    arrive, leave,
    layer_input, pack_qkv, pack_o, pack_gu, pack_down, segment_rows, segment_column, gains,
    first_qkv, second_q, second_kv, first_o, second_o,
    all_gu, all_down, all_tokens, out_qkv, out_kv_rows, out_o, out_kv,
    queries, totals, context, attn_proj, mixed, qkv_latent, o_latent,
    got_qkv, got_o, kv_rows, first_norm, kv_all, second_norm,
    sem_s, sem_r, kv_s, kv_r, tok_s, tok_r, loc,
):
    me, y, z, core = place()
    line = seq_peers()
    greet(line + plane_peers() + [sibling()])
    gathers = [
        PlaneGather(own, got, sem_s.at[i], sem_r.at[i])
        for i, (own, got) in enumerate(
            (
                (pack_qkv, got_qkv), (pack_o, got_o), (pack_gu, all_gu), (pack_down, all_down),
            )
        )
    ]
    g_qkv, g_o, g_gu, g_down = gathers
    own_copies = [
        pltpu.make_async_copy(g.own, g.buffer.at[y, z, core], loc.at[i])
        for i, g in enumerate(gathers)
    ]
    arrive(1)
    g_qkv.start()
    own_copies[0].start()
    arrive()
    for moving in own_copies[1:]:
        moving.start()
    gain_first, gain_second, gain_third = gains[0:1], gains[1:2], gains[2:3]
    values = layer_input[...].astype(f32)
    first_norm[...] = normed(values, gain_first).astype(bf16)
    latent = dot_nt(first_norm[...], first_qkv[...]).astype(bf16)
    qkv_latent[...] = latent
    for moving in own_copies:
        moving.wait()
    g_qkv.middle()
    g_o.start()
    g_qkv.late()
    g_gu.start()
    g_qkv.last()
    g_o.middle()
    g_qkv.finish()

    def unmix(i, _):
        pairs = got_qkv[i, :, :, 32:48].astype(f32).reshape(8, 2, 8, D)
        kv_rows[pl.ds(i * 64, 64)] = pairs[:, 0].reshape(64, D).astype(bf16)
        kv_rows[pl.ds(256 + i * 64, 64)] = pairs[:, 1].reshape(64, D).astype(bf16)
        return 0

    lax.fori_loop(0, 4, unmix, 0)
    kv = dot_nt(first_norm[...], kv_rows[...]) + dot(latent, second_kv[...])
    kv_all[me] = kv.astype(bf16)

    def kv_copy(shift):
        return remote(kv_all.at[me], kv_all.at[me], kv_s.at[shift - 1], kv_r.at[shift - 1], line[shift - 1])

    for shift in (1, 2, 3):
        pl.when(me + shift < SEQ)(lambda shift=shift: kv_copy(shift).start())

    def query(h, _):
        rows = got_qkv[h, :, :, 0:32].reshape(256, D)
        queries[h] = (dot_nt(first_norm[...], rows) + dot(latent, second_q[h])).astype(bf16)
        context[h] = jnp.zeros((ROWS, 256), f32)
        totals[h] = jnp.zeros((ROWS, 1), f32)
        return 0

    lax.fori_loop(0, 4, query, 0)
    g_gu.middle()
    g_down.start()

    def attend(chunk):
        keys, held = kv_all[chunk, :, 0:256], kv_all[chunk, :, 256:512]
        allowed = allowed_pairs(segment_rows, segment_column, me, chunk)

        def head(h, _):
            bent = jnp.tanh(dot_nt(queries[h], keys) * (SCORE / softcap))
            weight = jnp.where(allowed, jnp.exp(softcap * bent), 0.0).astype(bf16)
            totals[h] += jnp.sum(weight.astype(f32), -1, keepdims=True)
            context[h] += dot(weight, held)
            return 0

        lax.fori_loop(0, 4, head, 0)

    attend(me)
    g_o.late()
    g_o.last()
    for shift in (1, 2, 3):
        def arrived(shift=shift):
            kv_copy(shift).wait_recv()
            attend(me - shift)

        pl.when(me >= shift)(arrived)

    g_o.finish()
    keep = [
        pltpu.make_async_copy(got_qkv, out_qkv, loc.at[0]),
        pltpu.make_async_copy(got_o, out_o, loc.at[1]),
        pltpu.make_async_copy(kv_rows, out_kv_rows, loc.at[2]),
    ]
    for moving in keep:
        moving.start()
    g_gu.late()
    g_down.middle()
    total = jnp.zeros((ROWS, D), f32)
    thin = jnp.zeros((ROWS, 16), f32)
    for h in range(4):
        context[h] = context[h] / totals[h]
        low = context[h].astype(bf16)
        total = total + dot(low, got_o[h].reshape(256, D))
        thin = thin + dot_nt(low, first_o[h])
    o_latent[...] = thin.astype(bf16)
    proj = total + dot(o_latent[...], second_o[...])
    attn_proj[...] = proj
    mid = values + normed(proj, gain_second)
    mixed[...] = mid
    second_norm[...] = normed(mid, gain_third).astype(bf16)
    ahead, _, behind = line

    def passed(chunk, rows, slot, peer):
        block = all_tokens.at[chunk, rows]
        return remote(block, block, tok_s.at[slot], tok_r.at[slot], peer)

    to_ahead = remote(second_norm, all_tokens.at[me], tok_s.at[0], tok_r.at[0], ahead)
    to_behind = remote(second_norm, all_tokens.at[me], tok_s.at[1], tok_r.at[1], behind)
    to_ahead.start()
    to_behind.start()
    mine = pltpu.make_async_copy(second_norm, all_tokens.at[me], loc.at[3])
    mine.start()
    leave(7, 8, 9, 10, 11, 12, 13)
    kept_kv = pltpu.make_async_copy(kv_all, out_kv, loc.at[5])
    kept_kv.start()
    g_gu.last()
    g_down.late()
    to_ahead.wait()
    on_ahead = passed(lax.rem(me + 3, SEQ), slice(0, 128), 2, ahead)
    on_ahead.start()
    to_behind.wait()
    on_behind = passed(lax.rem(me + 1, SEQ), slice(128, 256), 3, behind)
    on_behind.start()
    g_gu.finish()
    g_down.last()
    g_down.finish()
    for moving in keep + [mine, kept_kv]:
        moving.wait()
    on_ahead.wait()
    on_behind.wait()
    for shift in (1, 2, 3):
        pl.when(me + shift < SEQ)(lambda shift=shift: kv_copy(shift).wait_send())


def attention_forward(*arrays):
    dma = pltpu.SemaphoreType.DMA
    return staged_call(
        attention_kernel, "attention_forward", arrays, "v" * len(arrays),
        [
            ((4, 4, 2, 2 * BLOCK, D), bf16, "h"),
            ((4, 4, 2, BLOCK, D), bf16, "h"),
            ((SEQ, ROWS, D), bf16, "h"),
            ((4, 4, 2, 48, D), bf16, "h"),
            ((512, D), bf16, "h"),
            ((4, 4, 2, 32, D), bf16, "h"),
            ((SEQ, ROWS, 512), bf16, "h"),
            ((4, ROWS, 256), bf16, "v"),
            ((4, ROWS, 1), f32, "v"),
            ((4, ROWS, 256), f32, "v"),
            ((ROWS, D), f32, "v"),
            ((ROWS, D), f32, "v"),
            ((ROWS, 48), bf16, "v"),
            ((ROWS, 16), bf16, "v"),
        ],
        [
            pltpu.VMEM((4, 4, 2, 48, D), bf16),
            pltpu.VMEM((4, 4, 2, 32, D), bf16),
            pltpu.VMEM((512, D), bf16),
            pltpu.VMEM((ROWS, D), bf16),
            pltpu.VMEM((SEQ, ROWS, 512), bf16),
            pltpu.VMEM((ROWS, D), bf16),
            dma((4, 11)), dma((4, 11)), dma((3,)), dma((3,)), dma((4,)), dma((4,)), dma((6,)),
        ],
        collective_id=2,
    )


WIDE = D + 128
HIDDEN = 32 * BLOCK
HALF = ROWS // 2
ROOT = 0.7978845608028654
CUBE = ROOT * 0.044715
FF_BLOCKS = 48


def mlp_kernel(
    arrive, leave,
    tokens, all_gu, all_down, ext_gu, ext_down, first_gu, second_down, mixed, out_grad, gains,
    layer_out, mixed_grad, early,
    w_gu, w_down, inputs, down_grads, hidden, act_gate, act_up, total,
    down_latents, gu_grads, hold_next, hold_back, packed,
    far, landed_half, near, landed, far_two, landed_half_two, near_two, landed_two,
    rs_s, rs_r, ag_s, ag_r, loc,
):
    me = lax.axis_index("seq")
    ahead, across, behind = seq_peers()
    slots = [me] + [lax.rem(me + k, SEQ) for k in (1, 3, 2)]
    copies = [
        pltpu.make_async_copy(src, dst, loc.at[i])
        for i, (src, dst) in enumerate(
            [(tokens.at[chunk], inputs.at[slot, :, 0:D]) for slot, chunk in enumerate(slots)]
            + [
                (all_gu, w_gu.at[:, :, :, :, 0:D]),
                (ext_gu, w_gu.at[:, :, :, :, D:WIDE]),
                (all_down, w_down.at[:, :, :, :, 0:D]),
                (ext_down, w_down.at[:, :, :, :, D:WIDE]),
            ]
        )
    ]
    for moving in copies:
        moving.start()
    greet([ahead, behind])
    arrive()
    gain_in, gain_out = gains[2:3], gains[3:4]

    def gate_rows(j):
        return w_gu[j // 2, pl.ds(2 * lax.rem(j, 2), 2), :, 0:64].reshape(TILE, WIDE)

    def up_rows(j):
        return w_gu[j // 2, pl.ds(2 * lax.rem(j, 2), 2), :, 64:128].reshape(TILE, WIDE)

    def down_rows(j):
        return w_down[j // 2, pl.ds(2 * lax.rem(j, 2), 2)].reshape(TILE, WIDE)

    def lanes(j, size=TILE):
        return pl.ds(pl.multiple_of(j * size, size), size)

    def forward(slot, many, before_down=None):
        size = many * ROWS
        part = slice(slot, slot + many)
        inputs[part, :, D:WIDE] = (
            dot_nt(inputs[part, :, 0:D].reshape(size, D), first_gu[...]).astype(bf16).reshape(many, ROWS, 128)
        )

        def step(j, _):
            rows = inputs[part].reshape(size, WIDE)
            gate = dot_nt(rows, gate_rows(j))
            upward = dot_nt(rows, up_rows(j))
            square = gate * gate
            bent = jnp.tanh(gate * (ROOT + CUBE * square))
            half = 0.5 * bent + 0.5
            gelu = gate * half
            slope = half + gelu * ((1.0 - bent) * (ROOT + 3.0 * CUBE * square))
            shape = (many, ROWS, TILE)
            hidden[part, :, lanes(j)] = (gelu * upward).astype(bf16).reshape(shape)
            act_gate[part, :, lanes(j)] = gelu.astype(bf16).reshape(shape)
            act_up[part, :, lanes(j)] = (upward * slope).astype(bf16).reshape(shape)
            return 0

        lax.fori_loop(0, 8, step, 0, unroll=2)
        if before_down is not None:
            before_down()

        def close(n, _):
            rows = hidden[part].reshape(size, HIDDEN)
            total[0:size, lanes(n)] = dot(rows, w_down[:, :, :, :, lanes(n)].reshape(HIDDEN, TILE))
            return 0

        lax.fori_loop(0, 5, close, 0)
        down_latent = total[0:size, D:WIDE].astype(bf16)
        down_latents[slot * ROWS : slot * ROWS + size] = down_latent
        total[0:size, 0:D] += dot(down_latent, second_down[...])

    def backward(slot, many):
        size = many * ROWS
        part = slice(slot, slot + many)
        latent_grad = dot_nt(down_grads[part, :, 0:D].reshape(size, D), second_down[...])
        down_grads[part, :, D:WIDE] = latent_grad.astype(bf16).reshape(many, ROWS, 128)

        def step(j, _):
            shape = (many, ROWS, TILE)
            hidden_grad = dot_nt(down_grads[part].reshape(size, WIDE), down_rows(j)).reshape(shape)
            gate_grad = (hidden_grad * act_up[part, :, lanes(j)].astype(f32)).astype(bf16)
            up_grad = (hidden_grad * act_gate[part, :, lanes(j)].astype(f32)).astype(bf16)
            act_up[part, :, lanes(j)] = gate_grad
            act_gate[part, :, lanes(j)] = up_grad
            return 0

        lax.fori_loop(0, 8, step, 0, unroll=2)

        def close(n, _):
            total[0:size, lanes(n)] = dot(
                act_up[part].reshape(size, HIDDEN), w_gu[:, :, :, 0:64, lanes(n)].reshape(HIDDEN, TILE)
            ) + dot(
                act_gate[part].reshape(size, HIDDEN), w_gu[:, :, :, 64:128, lanes(n)].reshape(HIDDEN, TILE)
            )
            return 0

        lax.fori_loop(0, 5, close, 0)
        gu_grad = total[0:size, D:WIDE].astype(bf16)
        gu_grads[slot * ROWS : slot * ROWS + size] = gu_grad
        total[0:size, 0:D] += dot(gu_grad, first_gu[...])

    def factors():
        latent = inputs[:, :, D:WIDE].reshape(SEQ * ROWS, 128)[:, 0:32]
        latent_grad = down_grads[:, :, D:WIDE].reshape(SEQ * ROWS, 128)[:, 32:48]

        def piece(j, _):
            gate_part = dot_tn(latent, act_up[:, :, lanes(j)].reshape(SEQ * ROWS, TILE))
            up_part = dot_tn(latent, act_gate[:, :, lanes(j)].reshape(SEQ * ROWS, TILE))
            down_part = dot_tn(latent_grad, hidden[:, :, lanes(j)].reshape(SEQ * ROWS, TILE))
            packed[0:16, lanes(j)] = gate_part[0:16].astype(bf16)
            packed[16:32, lanes(j)] = up_part[16:32].astype(bf16)
            packed[32:48, lanes(j)] = down_part.astype(bf16)
            return 0

        lax.fori_loop(0, 8, piece, 0)

    low, high = slice(0, HALF), slice(HALF, ROWS)

    def scatter_far(buffer, into, base):
        buffer[...] = total[0:ROWS, 0:D].astype(bf16)
        moves = [
            remote(buffer.at[low], into.at[0], rs_s.at[base], rs_r.at[base], behind),
            remote(buffer.at[high], into.at[1], rs_s.at[base + 1], rs_r.at[base + 1], ahead),
        ]
        for moving in moves:
            moving.start()
        return moves

    def scatter_near(buffer, into, base):
        return [
            remote(buffer.at[0, low], into.at[0, low], rs_s.at[base], rs_r.at[base], ahead),
            remote(buffer.at[0, high], into.at[0, high], rs_s.at[base + 1], rs_r.at[base + 1], ahead),
            remote(buffer.at[1, high], into.at[1, high], rs_s.at[base + 2], rs_r.at[base + 2], behind),
            remote(buffer.at[1, low], into.at[1, low], rs_s.at[base + 3], rs_r.at[base + 3], behind),
        ]

    def keep_near(buffer, moves):
        buffer[0, low] = total[0:HALF, 0:D].astype(bf16)
        moves[0].start()
        buffer[1, high] = total[ROWS + HALF : 2 * ROWS, 0:D].astype(bf16)
        moves[2].start()
        hold_next[...] = total[HALF:ROWS, 0:D]
        hold_back[...] = total[ROWS : ROWS + HALF, 0:D]

    def merge(buffer, half, far_moves, moves):
        far_moves[1].wait()
        buffer[0, high] = (hold_next[...] + half[1].astype(f32)).astype(bf16)
        moves[1].start()
        far_moves[0].wait()
        buffer[1, low] = (hold_back[...] + half[0].astype(f32)).astype(bf16)
        moves[3].start()

    for moving in copies[:6]:
        moving.wait()

    def down_here():
        for moving in copies[6:]:
            moving.wait()

    forward(3, 1, down_here)
    far_moves = scatter_far(far, landed_half, 0)
    near_moves = scatter_near(near, landed, 2)
    forward(1, 2)
    keep_near(near, near_moves)
    merge(near, landed_half, far_moves, near_moves)
    forward(0, 1)
    for moving in near_moves:
        moving.wait()
    down_proj = total[0:ROWS, 0:D] + landed[0].astype(f32) + landed[1].astype(f32)
    layer_out[...] = (mixed[...] + normed(down_proj, gain_out)).astype(bf16)
    leave(0)
    down_grads[0, :, 0:D] = norm_back(down_proj, gain_out, out_grad[...].astype(f32)).astype(bf16)

    def passed(from_slot, to_slot, rows, index, peer):
        return remote(
            down_grads.at[from_slot, rows, 0:D], down_grads.at[to_slot, rows, 0:D],
            ag_s.at[index], ag_r.at[index], peer,
        )

    whole = slice(0, ROWS)
    to_ahead, to_behind = passed(0, 2, whole, 0, ahead), passed(0, 1, whole, 1, behind)
    to_ahead.start()
    to_behind.start()
    backward(0, 1)
    mixed_grad[...] = total[0:ROWS, 0:D]
    to_ahead.wait()
    on_ahead = passed(2, 3, low, 2, ahead)
    on_ahead.start()
    to_behind.wait()
    on_behind = passed(1, 3, high, 3, behind)
    on_behind.start()
    near_moves = scatter_near(near_two, landed_two, 8)
    backward(1, 2)
    keep_near(near_two, near_moves)
    on_ahead.wait()
    on_behind.wait()
    backward(3, 1)
    far_moves = scatter_far(far_two, landed_half_two, 6)
    factors()
    merge(near_two, landed_half_two, far_moves, near_moves)

    def unpad(j, _):
        start = jnp.minimum((j * 128 // 216) // 2 * 128, HIDDEN // 2 - 256)
        lane = start + lax.broadcasted_iota(jnp.int32, (256, 128), 0)
        within = lane & 63
        unit = (lane >> 6) * 216 + me * UNITS + within
        goal = j * 128 + lax.broadcasted_iota(jnp.int32, (256, 128), 1)
        chosen = jnp.where((unit == goal) & (within < UNITS), 1.0, 0.0).astype(bf16)
        for half in (0, 1):
            rows = packed[:, pl.ds(pl.multiple_of(start + half * HIDDEN // 2, 128), 256)]
            moved = dot(rows, chosen).astype(bf16)
            for i in range(3):
                early[54 * i + 27 * half + j] = moved[16 * i : 16 * i + 16]
        return 0

    lax.fori_loop(0, 27, unpad, 0)
    all_gu_grads = gu_grads[...]
    gu_part = dot_tn(all_gu_grads[:, 0:32], inputs[:, :, 0:D].reshape(SEQ * ROWS, D))
    down_part = dot_tn(down_latents[:, 32:48], down_grads[:, :, 0:D].reshape(SEQ * ROWS, D))

    def put(start, rows):
        for i in range(9):
            early[start + i] = rows[:, i * 128 : (i + 1) * 128].astype(bf16)

    put(162, gu_part[0:16])
    put(171, gu_part[16:32])
    put(180, down_part)
    for i in range(189, 192):
        early[i] = jnp.zeros((16, 128), bf16)
    for moving in near_moves:
        moving.wait()
    own = mixed_grad[...] + landed_two[0].astype(f32) + landed_two[1].astype(f32)
    mixed_grad[...] = out_grad[...].astype(f32) + norm_back(mixed[...], gain_in, own)


def feed_forward(*arrays):
    dma = pltpu.SemaphoreType.DMA
    exchange = [
        pltpu.VMEM((ROWS, D), bf16),
        pltpu.VMEM((2, HALF, D), bf16),
        pltpu.VMEM((2, ROWS, D), bf16),
        pltpu.VMEM((2, ROWS, D), bf16),
    ]
    return staged_call(
        mlp_kernel, "feed_forward", arrays, "hhhhh" + "v" * (len(arrays) - 5),
        [((ROWS, D), bf16, "v"), ((ROWS, D), f32, "v"), ((SEQ * FF_BLOCKS, 16, 128), bf16, "v")],
        [
            pltpu.VMEM((4, 4, 2, 2 * BLOCK, WIDE), bf16),
            pltpu.VMEM((4, 4, 2, BLOCK, WIDE), bf16),
            pltpu.VMEM((SEQ, ROWS, WIDE), bf16),
            pltpu.VMEM((SEQ, ROWS, WIDE), bf16),
            pltpu.VMEM((SEQ, ROWS, HIDDEN), bf16),
            pltpu.VMEM((SEQ, ROWS, HIDDEN), bf16),
            pltpu.VMEM((SEQ, ROWS, HIDDEN), bf16),
            pltpu.VMEM((2 * ROWS, WIDE), f32),
            pltpu.VMEM((SEQ * ROWS, 128), bf16),
            pltpu.VMEM((SEQ * ROWS, 128), bf16),
            pltpu.VMEM((HALF, D), f32),
            pltpu.VMEM((HALF, D), f32),
            pltpu.VMEM((48, HIDDEN), bf16),
        ]
        + exchange
        + exchange
        + [dma((12,)), dma((12,)), dma((4,)), dma((4,)), dma((8,))],
        collective_id=1,
    )


LATE = 14


class LineSum:
    def __init__(self, parts, landed, send_sem, recv_sem):
        self.me, self.peers = lax.axis_index("seq"), seq_peers()
        self.parts, self.landed, self.send, self.recv = parts, landed, send_sem, recv_sem

    def _copy(self, shift):
        return remote(
            self.parts.at[lax.rem(self.me + shift, SEQ)], self.landed.at[shift - 1],
            self.send.at[shift - 1], self.recv.at[shift - 1], self.peers[shift - 1],
        )

    def start(self):
        for shift in (2, 1, 3):
            self._copy(shift).start()

    def finish(self):
        for shift in (1, 3, 2):
            self._copy(shift).wait()


class PlaneExchange:
    def __init__(self, first, second, third, fourth, send_sem, recv_sem):
        self.x, self.y, self.z, self.core = place()
        self.first, self.second, self.third, self.fourth = first, second, third, fourth
        self.send, self.recv = send_sem, recv_sem

    def _copy(self, src, dst, slot, peer):
        return remote(src, dst, self.send.at[slot], self.recv.at[slot], peer)

    def _along_y(self, k):
        y = lax.rem(self.y + k, 4)
        return self._copy(self.first.at[y], self.second.at[k], k - 1, at(self.x, y, self.z, self.core))

    def _along_z(self, k):
        z = lax.rem(self.z + k, 4)
        return self._copy(self.second.at[:, z], self.third.at[k], 2 + k, at(self.x, self.y, z, self.core))

    def _across(self):
        return self._copy(self.third, self.fourth, 6, sibling())

    def start(self):
        for k in (2, 1, 3):
            self._along_y(k).start()
        self.second[0] = self.first[self.y]

    def middle(self):
        for k in (1, 3, 2):
            self._along_y(k).wait()
        for k in (2, 1, 3):
            self._along_z(k).start()
        self.third[0] = self.second[:, self.z]

    def late(self):
        for k in (1, 3, 2):
            self._along_z(k).wait()
        self._across().start()

    def finish(self):
        self._across().wait()

    def total(self, marks, out):
        slots = self.first.shape[2]
        out[...] = jnp.zeros_like(out)

        def add(i, _):
            kz, ky = i // 4, lax.rem(i, 4)
            for held, known in ((self.third, marks.third), (self.fourth, marks.fourth)):
                weights = known[kz, ky, 0, self.core]
                for slot in range(slots):
                    rows = held[kz, ky, slot].astype(f32)
                    for a in range(4):
                        out[slot, a] += weights[a : a + 1] * rows
            return 0

        lax.fori_loop(0, 16, add, 0)


class LineGather:
    def __init__(self, buffer, send_sem, recv_sem):
        self.me, self.peers = lax.axis_index("seq"), seq_peers()
        self.buffer, self.send, self.recv = buffer, send_sem, recv_sem

    def _copy(self, shift):
        mine = self.buffer.at[self.me]
        return remote(mine, mine, self.send.at[shift - 1], self.recv.at[shift - 1], self.peers[shift - 1])

    def start(self):
        for shift in (2, 1, 3):
            self._copy(shift).start()

    def finish(self):
        for shift in (1, 3, 2):
            self._copy(shift).wait()


def attention_back_kernel(
    arrive, leave,
    layer_input, mixed_grad, attn_proj, context, totals, queries, kv_all,
    segment_rows, segment_column, gains,
    first_qkv, second_q, second_kv, first_o, second_o, qkv_latent, o_latent,
    got_qkv, kv_rows, got_o,
    early, own_marks,
    input_grad, all_early, all_late,
    m1, m2, m3, m4, attn_grad, head_grads, query_grads, centre, key_part, value_part, kv_send, kv_landed, kv_own,
    early_landed, early_sum, e2, e3, e4, early_total, early_line,
    late, late_landed, late_sum, l2, l3, l4, late_total, late_line,
    line_s, line_r, kv_s, kv_r, plane_s, plane_r, spread_s, spread_r, out_s, out_r, loc,
):
    me, y, z, core = place()
    line = seq_peers()
    greet(line + plane_peers() + [sibling()])
    arrive(20)
    early_parts = early.reshape(SEQ, FF_BLOCKS, 16, 128)
    e_line = LineSum(early_parts, early_landed, line_s.at[0], line_r.at[0])
    e_line.start()
    arrive(21)
    for i in range(4):
        for k in range(4):
            m1[i, k, 0] = own_marks[...]
    m_plane = PlaneExchange(m1, m2, m3, m4, plane_s.at[2], plane_r.at[2])
    m_plane.start()
    arrive(*range(17))
    gain_first, gain_second = gains[0:1], gains[1:2]

    attn_grad[...] = norm_back(attn_proj[...], gain_second, mixed_grad[...]).astype(bf16)
    o_grad = dot_nt(attn_grad[...], second_o[...]).astype(bf16)

    def put(start, rows, buffer):
        for i in range(rows.shape[1] // 128):
            buffer[start + i] = rows[:, i * 128 : (i + 1) * 128].astype(bf16)

    m_plane.middle()
    arrive(19)
    for h in range(4):
        low = (dot_nt(attn_grad[...], got_o[h].reshape(256, D)) + dot(o_grad, first_o[h])).astype(bf16)
        head_grads[h] = low
        centre[h] = jnp.sum(low.astype(f32) * context[h], -1, keepdims=True)
        query_grads[h] = jnp.zeros((ROWS, 256), f32)
        put(39 + 2 * h, dot_tn(o_grad, context[h].astype(bf16)), late)
    put(47, dot_tn(o_latent[...], attn_grad[...]), late)

    def attend_back(chunk):
        keys, held = kv_all[chunk, :, 0:256], kv_all[chunk, :, 256:512]
        allowed = allowed_pairs(segment_rows, segment_column, me, chunk)
        key_part[...] = jnp.zeros_like(key_part)
        value_part[...] = jnp.zeros_like(value_part)

        def head(h, _):
            bent = jnp.tanh(dot_nt(queries[h], keys) * (SCORE / softcap))
            weight = jnp.where(allowed, jnp.exp(softcap * bent), 0.0).astype(bf16).astype(f32)
            probs = weight / totals[h]
            prob_grad = dot_nt(head_grads[h], held)
            raw_grad = (probs * (prob_grad - centre[h]) * ((1.0 - bent * bent) * SCORE)).astype(bf16)
            query_grads[h] += dot(raw_grad, keys)
            key_part[...] += dot_tn(raw_grad, queries[h])
            value_part[...] += dot_tn(probs.astype(bf16), head_grads[h])
            return 0

        lax.fori_loop(0, 4, head, 0)

    def kv_copy(shift):
        peer = line[3 - shift]
        return remote(kv_send.at[shift - 1], kv_landed.at[shift - 1], kv_s.at[shift - 1], kv_r.at[shift - 1], peer)

    for shift in (3, 2, 1):
        def earlier(shift=shift):
            attend_back(me - shift)
            kv_send[shift - 1, :, 0:256] = key_part[...].astype(bf16)
            kv_send[shift - 1, :, 256:512] = value_part[...].astype(bf16)
            kv_copy(shift).start()

        pl.when(me >= shift)(earlier)

    attend_back(me)
    kv_own[:, 0:256] = key_part[...]
    kv_own[:, 256:512] = value_part[...]
    m_plane.late()

    e_line.finish()

    def add_early(i, _):
        for k in range(3):
            own = early_parts[me, 3 * i + k].astype(f32)
            for s in range(3):
                own = own + early_landed[s, 3 * i + k].astype(f32)
            low = own.astype(bf16)
            early_sum[i // 4, lax.rem(i, 4), k] = low
        return 0

    lax.fori_loop(0, 16, add_early, 0)
    e_plane = PlaneExchange(early_sum, e2, e3, e4, plane_s.at[0], plane_r.at[0])
    e_plane.start()

    m_plane.finish()
    e_plane.middle()
    e_plane.late()
    e_plane.finish()
    e_plane.total(m_plane, early_total)
    early_line[me] = early_total[...].astype(bf16)
    e_spread = LineGather(early_line, spread_s.at[0], spread_r.at[0])
    e_spread.start()
    for shift in (1, 2, 3):
        def landed(shift=shift):
            kv_copy(shift).wait_recv()
            kv_own[...] += kv_landed[shift - 1].astype(f32)

        pl.when(me + shift < SEQ)(landed)

    arrive(17, 18)
    key_value = kv_own[...].astype(bf16)
    values = layer_input[...].astype(f32)
    first_norm = normed(values, gain_first).astype(bf16)
    thin = dot_nt(key_value, second_kv[...])
    total = dot(key_value, kv_rows[...])
    for h in range(4):
        low = query_grads[h].astype(bf16)
        total = total + dot(low, got_qkv[h, :, :, 0:32].reshape(256, D))
        thin = thin + dot_nt(low, second_q[h])
        put(27 + 2 * h, dot_tn(qkv_latent[...], low)[0:16], late)
    qkv_grad = thin.astype(bf16)
    total = total + dot(qkv_grad, first_qkv[...])
    e_spread.finish()
    own_early = pltpu.make_async_copy(early_line, all_early.at[y, z, core], loc.at[0])
    own_early.start()
    e_out = PlaneGather(early_line, all_early, out_s.at[0], out_r.at[0])
    e_out.start()

    in_grad = dot_tn(qkv_grad, first_norm)
    for i in range(3):
        put(9 * i, in_grad[16 * i : 16 * i + 16], late)
    kv_out_grad = dot_tn(qkv_latent[...], key_value)
    put(35, kv_out_grad[16:32, 0:256], late)
    put(37, kv_out_grad[32:48, 256:512], late)
    late_parts = late.reshape(SEQ, LATE, 16, 128)
    l_line = LineSum(late_parts, late_landed, line_s.at[1], line_r.at[1])
    l_line.start()
    input_grad[...] = (mixed_grad[...] + norm_back(values, gain_first, total)).astype(bf16)

    leave(0)

    l_line.finish()
    for i in range(16):
        low = jnp.zeros((16, 128), bf16)
        if i < LATE:
            own = late_parts[me, i].astype(f32)
            for s in range(3):
                own = own + late_landed[s, i].astype(f32)
            low = own.astype(bf16)
        late_sum[i // 4, i % 4, 0] = low
    l_plane = PlaneExchange(late_sum, l2, l3, l4, plane_s.at[1], plane_r.at[1])
    l_plane.start()
    own_early.wait()
    e_out.middle()
    l_plane.middle()
    l_plane.late()
    l_plane.finish()
    l_plane.total(m_plane, late_total)
    late_line[me] = late_total[...].astype(bf16)
    l_spread = LineGather(late_line, spread_s.at[1], spread_r.at[1])
    l_spread.start()
    l_spread.finish()
    own_late = pltpu.make_async_copy(late_line, all_late.at[y, z, core], loc.at[1])
    own_late.start()
    l_out = PlaneGather(late_line, all_late, out_s.at[1], out_r.at[1])
    l_out.start()
    e_out.late()
    own_late.wait()
    l_out.middle()
    l_out.late()
    e_out.last()
    l_out.last()
    e_out.finish()
    l_out.finish()
    for shift in (1, 2, 3):
        pl.when(me >= shift)(lambda shift=shift: kv_copy(shift).wait_send())


def attention_back(*arrays):
    dma = pltpu.SemaphoreType.DMA
    marks = pltpu.VMEM((4, 4, 1, 2, 8, 128), f32)

    def reduction(blocks, slots):
        whole = pltpu.VMEM((4, 4, slots, 16, 128), bf16)
        return [
            pltpu.VMEM((3, blocks, 16, 128), bf16), whole, whole, whole, whole,
            pltpu.VMEM((slots, 4, 16, 128), f32),
            pltpu.VMEM((SEQ, slots, 4, 16, 128), bf16),
        ]

    return staged_call(
        attention_back_kernel, "attention_back", arrays, "v" * len(arrays),
        [
            ((ROWS, D), bf16, "v"),
            ((4, 4, 2, SEQ, 3, 4, 16, 128), bf16, "h"),
            ((4, 4, 2, SEQ, 1, 4, 16, 128), bf16, "h"),
        ],
        [
            marks, marks, marks, marks,
            pltpu.VMEM((ROWS, D), bf16),
            pltpu.VMEM((4, ROWS, 256), bf16),
            pltpu.VMEM((4, ROWS, 256), f32),
            pltpu.VMEM((4, ROWS, 1), f32),
            pltpu.VMEM((ROWS, 256), f32),
            pltpu.VMEM((ROWS, 256), f32),
            pltpu.VMEM((3, ROWS, 512), bf16),
            pltpu.VMEM((3, ROWS, 512), bf16),
            pltpu.VMEM((ROWS, 512), f32),
        ]
        + reduction(FF_BLOCKS, 3)
        + [pltpu.VMEM((SEQ * LATE, 16, 128), bf16)]
        + reduction(LATE, 1)
        + [dma((2, 3))] * 2
        + [dma((3,))] * 2
        + [dma((3, 7))] * 2
        + [dma((2, 3))] * 2
        + [dma((2, 11))] * 2
        + [dma((2,))],
        collective_id=3,
    )


def tables_kernel(
    early, late, qkv_in, q_out, kv_out, o_in, o_out, mlp_in, mlp_out, down_in, down_out
):
    def copy(source, start, count, out):
        for i in range(count):
            x, place = divmod(start + i, FF_BLOCKS if source is early else LATE)
            owner, slot = divmod(place, 3 if source is early else 1)
            out[:, i * 128 : (i + 1) * 128] = source[owner // 4, owner % 4, 0, x, slot, 0].astype(f32)

    for i in range(2):
        copy(early, 54 * i, 54, mlp_out.at[0, i])
        copy(early, 162 + 9 * i, 9, mlp_in.at[0, i])
        copy(late, 35 + 2 * i, 2, kv_out.at[0, i])
    copy(early, 108, 54, down_in.at[0])
    copy(early, 180, 9, down_out.at[0])
    for i in range(3):
        copy(late, 9 * i, 9, qkv_in.at[0, i])
    copy(late, 27, 8, q_out.at[0])
    copy(late, 39, 8, o_in.at[0])
    copy(late, 47, 9, o_out.at[0])


def put_tables(early, late):
    shapes = (
        (3, 16, D), (16, 1024), (2, 16, 256), (16, 1024), (16, D),
        (2, 16, D), (2, 16, 6912), (16, 6912), (16, D),
    )

    def one(shape):
        rest = len(shape)
        return pl.BlockSpec((1,) + shape, lambda a, rest=rest: (a,) + (0,) * rest)

    def blocks(slots):
        return pl.BlockSpec(
            (4, 4, 1, SEQ, slots, 1, 16, 128), lambda a: (0, 0, a // 4, 0, 0, a % 4, 0, 0)
        )

    return pl.pallas_call(
        tables_kernel,
        grid=(8,),
        out_shape=[jax.ShapeDtypeStruct((8,) + shape, f32) for shape in shapes],
        in_specs=[blocks(3), blocks(1)],
        out_specs=[one(shape) for shape in shapes],
        compiler_params=pltpu.CompilerParams(vmem_limit_bytes=62 * MIB),
        name="tables",
    )(early, late)


def prepare_kernel(
    arrive, leave, ids, place_x, segments, w_query, w_key, w_value, w_gate, w_up, w_down,
    qkv_adapt_in, q_adapt_out, kv_adapt_out, o_adapt_in, o_adapt_out,
    mlp_adapt_in, mlp_adapt_out, down_adapt_in, down_adapt_out,
    pack_qkv, pack_gu, pack_down, own_marks, segment_rows, segment_column,
    first_qkv, second_q, second_kv, first_o, second_o, first_gu, second_down, ext_gu, ext_down,
    table, q_held, kv_held, o_held, in_held, out_held, sem,
):
    chosen, me = ids[0], place_x[0]
    mlp_out, down_in = mlp_adapt_out.at[chosen], down_adapt_in.at[chosen]
    moves = [
        (mlp_out.at[0], table.at[0:16]),
        (mlp_out.at[1], table.at[16:32]),
        (down_in, table.at[32:48]),
        (q_adapt_out.at[chosen], q_held),
        (kv_adapt_out.at[chosen], kv_held),
        (o_adapt_in.at[chosen], o_held),
        (o_adapt_out.at[chosen], second_o),
        (mlp_adapt_in.at[chosen], in_held),
        (down_adapt_out.at[chosen], out_held),
        (qkv_adapt_in.at[chosen], first_qkv),
    ]
    moves = [pltpu.make_async_copy(src, dst, sem.at[i]) for i, (src, dst) in enumerate(moves)]
    for moving in moves:
        moving.start()
    iota = lambda shape, axis: lax.broadcasted_iota(jnp.int32, shape, axis)
    ones = lambda where: jnp.where(where, 1.0, 0.0).astype(bf16)

    def placed(count, first):
        return ones(iota((48, count), 0) == iota((48, count), 1) + first)

    table[48:128] = jnp.zeros((80, 6912), bf16)
    arrive()
    rows = dot(placed(32, 0), w_query[...]) + dot(placed(8, 32), w_key[...])
    pack_qkv[...] = (rows + dot(placed(8, 40), w_value[...])).astype(bf16)
    row, unit = iota((BLOCK, 216), 0), iota((BLOCK, 216), 1)
    quarter = ones((unit == me * UNITS + row) & (row < UNITS))
    pack_gu[0:64] = dot(quarter, w_gate[...]).astype(bf16)
    pack_gu[64:128] = dot(quarter, w_up[...]).astype(bf16)
    pack_down[...] = dot(quarter, w_down[...]).astype(bf16)

    leave(0, 1, 2)
    adapter = iota((8, 128), 0)
    for half in (0, 1):
        own_marks[half] = jnp.where((adapter + 4 * half == chosen) & (adapter < 4), 1.0, 0.0)
    for i in range(SEQ):
        segment_rows[i] = segments[:, i * ROWS : (i + 1) * ROWS]
    square = iota((ROWS, ROWS), 0) == iota((ROWS, ROWS), 1)
    segment_column[...] = jnp.sum(jnp.where(square, segment_rows[me], 0), -1, keepdims=True)

    for moving in moves:
        moving.wait()
    second_q[...] = jnp.zeros_like(second_q)
    for h in range(4):
        second_q[h, 0:16] = q_held[:, h * 256 : (h + 1) * 256]
        first_o[h] = o_held[:, h * 256 : (h + 1) * 256]
    second_kv[...] = jnp.zeros_like(second_kv)
    second_kv[16:32, 0:256] = kv_held[0]
    second_kv[32:48, 256:512] = kv_held[1]
    first_gu[0:16] = in_held[0]
    first_gu[16:32] = in_held[1]
    first_gu[32:128] = jnp.zeros((96, D), bf16)
    second_down[0:32] = jnp.zeros((32, D), bf16)
    second_down[32:48] = out_held[...]
    second_down[48:128] = jnp.zeros((80, D), bf16)

    def spread(p, _):
        first = 432 * p + me * UNITS
        start = jnp.minimum(first // 128 * 128, 6912 - 512)
        row = iota((128, 512), 0)
        within = row & 63
        unit = first + (row >> 6) * 216 + within
        picked = ones((unit == start + iota((128, 512), 1)) & (within < UNITS))
        held = dot_nt(picked, table[:, pl.ds(pl.multiple_of(start, 128), 512)])
        lane = iota((128, 128), 1)
        gate = jnp.where(lane < 16, held, 0.0).astype(bf16)
        upward = jnp.where((lane >= 16) & (lane < 32), held, 0.0).astype(bf16)
        down = jnp.where(lane >= 32, held, 0.0).astype(bf16)
        for i in (0, 1):
            half = slice(64 * i, 64 * i + 64)
            ext_gu[2 * p + i, 0:64] = gate[half]
            ext_gu[2 * p + i, 64:128] = upward[half]
            ext_down[2 * p + i] = down[half]
        return 0

    lax.fori_loop(0, 16, spread, 0)


def prepare(*arrays):
    shapes = [
        ((48, D), bf16), ((128, D), bf16), ((64, D), bf16), ((2, 8, 128), f32),
        ((SEQ, 1, ROWS), jnp.int32), ((ROWS, 1), jnp.int32),
        ((3, 16, D), bf16), ((4, 48, 256), bf16), ((48, 512), bf16), ((4, 16, 256), bf16), ((16, D), bf16),
        ((128, D), bf16), ((128, D), bf16), ((32, 2 * BLOCK, 128), bf16), ((32, BLOCK, 128), bf16),
    ]
    return staged_call(
        prepare_kernel, "prepare", arrays, "ss" + "v" * 7 + "h" * 9,
        [shape + ("v",) for shape in shapes],
        [
            pltpu.VMEM((128, 6912), bf16),
            pltpu.VMEM((16, 1024), bf16),
            pltpu.VMEM((2, 16, 256), bf16),
            pltpu.VMEM((16, 1024), bf16),
            pltpu.VMEM((2, 16, D), bf16),
            pltpu.VMEM((16, D), bf16),
            pltpu.SemaphoreType.DMA((10,)),
        ],
    )


def body(
    layer_input, out_grad, segment_ids, adapter_ids,
    gain_attn_in, gain_attn_out, gain_mlp_in, gain_mlp_out,
    w_query, w_key, w_value, w_out, w_gate, w_up, w_down,
    qkv_adapt_in, q_adapt_out, kv_adapt_out, o_adapt_in, o_adapt_out,
    mlp_adapt_in, mlp_adapt_out, down_adapt_in, down_adapt_out,
):
    me = lax.axis_index("seq").astype(jnp.int32)
    (
        pack_qkv, pack_gu, pack_down, own_marks, segment_rows, segment_column,
        first_qkv, second_q, second_kv, first_o, second_o, first_gu, second_down, ext_gu, ext_down,
    ) = prepare(
        adapter_ids, me.reshape(1), segment_ids, w_query.T, w_key.T, w_value.T, w_gate.T, w_up.T, w_down,
        qkv_adapt_in, q_adapt_out, kv_adapt_out, o_adapt_in, o_adapt_out,
        mlp_adapt_in, mlp_adapt_out, down_adapt_in, down_adapt_out,
    )
    first_qkv = first_qkv.reshape(48, D)
    gains = jnp.stack([gain_attn_in, gain_attn_out, gain_mlp_in, gain_mlp_out])
    (
        w_gu_all, w_down_all, tokens, qkv_all, kv_rows, o_all, kv_all,
        q, totals, context, attn_proj, mixed, qkv_latent, o_latent,
    ) = attention_forward(
        layer_input[0], pack_qkv, w_out, pack_gu, pack_down, segment_rows, segment_column, gains,
        first_qkv, second_q, second_kv, first_o, second_o,
    )
    layer_out, mixed_grad, early = feed_forward(
        tokens, w_gu_all, w_down_all,
        ext_gu.reshape(4, 4, 2, 2 * BLOCK, 128), ext_down.reshape(4, 4, 2, BLOCK, 128),
        first_gu, second_down, mixed, out_grad[0], gains,
    )
    input_grad, all_early, all_late = attention_back(
        layer_input[0], mixed_grad, attn_proj, context, totals, q, kv_all,
        segment_rows, segment_column, gains,
        first_qkv, second_q, second_kv, first_o, second_o, qkv_latent, o_latent,
        qkv_all, kv_rows, o_all, early, own_marks,
    )
    return (layer_out[None], input_grad[None]) + tuple(put_tables(all_early, all_late))


def solution(mesh):
    tokens = P("dp", "seq", None)
    columns, rows = P(None, "dp"), P("dp", None)
    placed = (
        (tokens, tokens, P("dp", None), P("dp"))
        + (P(),) * 4
        + (columns, columns, columns, rows, columns, columns, rows)
        + (P(),) * 9
    )
    return jax.shard_map(
        body,
        mesh=mesh,
        in_specs=placed,
        out_specs=(tokens, tokens) + (P(),) * 9,
        check_vma=False,
    )
```

time: 429 us -> 283 us (0.66); the launches traced: 421 us -> 283 us
  local copies, waits for them, and re-layouts: 67.6 us -> 4.44 us
  Pallas kernels: 321 us -> 276 us
  blocking collectives: 19.5 us -> 0 us
  other arithmetic: 10.4 us -> 0.62 us
    pallas_call x3 -> x5, Pallas kernels: 321 us -> 276 us  [the longest x4 266 us: staged_call(): pl.pallas_call(body, out_shape=[jax.ShapeDtypeStruct(shape, dtype) for sh...]
    unnamed x1 -> x0, blocking collectives: 19.5 us -> none
    convert_element_type x23 -> x0, local copies, waits for them, and re-layouts: 16.9 us -> none  [table(): return part.reshape(8, 16, count * 128).astype(f32)]
    reshape x11 -> x0, local copies, waits for them, and re-layouts: 13.5 us -> none  [the longest x1 10.3 us: body(): all_early.reshape(32, SEQ, 2, 8, 16, 128).transpose(1, 0, 2, 3, 4, 5)]
    unnamed x39 -> x6, local copies, waits for them, and re-layouts: 11.3 us -> 1.64 us
    slice x4 -> x0, local copies, waits for them, and re-layouts: 6.26 us -> none  [the longest x1 4.67 us: body(): early.reshape(SEQ, 64, 8, 16, 128)[:, :EARLY]]
    dynamic_slice x8 -> x0, local copies, waits for them, and re-layouts: 6.14 us -> none  [the longest x4 3.85 us: body(): lax.dynamic_index_in_dim(table, chosen, 0, keepdims=False)]
    broadcast_in_dim x9 -> x0, local copies, waits for them, and re-layouts: 5.54 us -> none  [the longest x2 1.48 us: body(): mine[:, None]]
where the time goes in v3:
time: 283 us
  Pallas kernels  276 us (98%)
  local copies, waits for them, and re-layouts  4.44 us (2%)
    pallas_call x4, Pallas kernels, staged_call(): pl.pallas_call(body, out_shape=[jax.ShapeDtypeStruct(shape, dtype) for sh...  266 us
    pallas_call x1, Pallas kernels, put_tables(): pl.pallas_call(tables_kernel, grid=(8,), out_shape=[jax.ShapeDtypeStruct(...  10.4 us

profile of v3, /device:TPU:1, one launch (start us, length us, event | category | flops | bytes accessed | tf_op | source)
XLA Modules:
  0.0 282.8 jit_solution(11234001037942071626)
XLA Ops:
  1.3 0.7 stack.15
  2.0 0.7 stack.16
  2.7 0.7 stack.17
  3.4 0.7 stack.18
  4.1 0.6 pad_maximum_fusion.refs_7_.refs_9_
  4.7 7.2 %prepare.1 = (bf16[48,1152]{1,0:T(8,128)(2,1)}, bf16[128,1152]{1,0:T(8,128)(2,1)}, bf16[64,1152]{1,0:T(8,128)(2,1)}, f32[2,8,128]{2,1,0:T(8,128)}, s32[4,1,256]{...) custom-call(s32[1]{0:T(128)S(6)} %copy.37.refs_0_, ...), custom_call_target="tpu_custom_call" | custom-call | tf_op jit(solution)/shard_map/prepare/pallas_call | solution.py:103
  11.9 84.9 %attention_forward.1 = (bf16[4,4,2,128,1152]{4,3,2,1,0:T(8,128)(2,1)}, bf16[4,4,2,64,1152]{4,3,2,1,0:T(8,128)(2,1)}, bf16[4,256,1152]{2,1,0:T(8,128)(2,1)}, bf16...) custom-call(bf16[256,1152]{1,0:T(8,128)(2,1)} %bitcast.13, ...), custom_call_target="tpu_custom_call" | custom-call | tf_op jit(solution)/shard_map/attention_forward/pallas_call | solution.py:103
  96.9 88.3 %feed_forward.1 = (bf16[256,1152]{1,0:T(8,128)(2,1)}, f32[256,1152]{1,0:T(8,128)}, bf16[192,16,128]{2,1,0:T(8,128)(2,1)}) custom-call(bf16[4,256,1152]{2,1,0:T(8,128)(2,1)} %get-tuple-element.65.refs_0_, bf16[4,4,2,128,1152]{4,3,2,1,0:T(8,128)(2,1)} %get-tuple-element.66.refs_1_, bf16[4,4,2,64,1152]{4,3,2,1,0:T(8,128)(2,1)} %get-tuple-element.67.refs_2_, ...), custom_call_target="tpu_custom_call" | custom-call | tf_op jit(solution)/shard_map/feed_forward/pallas_call | solution.py:103
  185.2 85.6 %attention_back.1 = (bf16[256,1152]{1,0:T(8,128)(2,1)}, bf16[4,4,2,4,3,4,16,128]{7,6,5,4,3,2,1,0:T(8,128)(2,1)}, bf16[4,4,2,4,1,4,16,128]{7,6,5,4,3,2,1,0:T(8,128)(2,1)}) custom-call(bf16[256,1152]{1,0:T(8,128)(2,1)} %bitcast.14, f32[256,1152]{1,0:T(8,128)} %get-tuple-element.74.refs_1_, f32[256,1152]{1,0:T(8,128)} %get-tuple-element.75.refs_2_, ...), custom_call_target="tpu_custom_call" | custom-call | tf_op jit(solution)/shard_map/attention_back/pallas_call | solution.py:103
  270.8 0.0 copy-start
  270.8 0.0 copy-start.1
  270.8 10.4 %tables.1 = (f32[8,3,16,1152]{3,2,1,0:T(8,128)}, f32[8,16,1024]{2,1,0:T(8,128)}, f32[8,2,16,256]{3,2,1,0:T(8,128)}, f32[8,16,1024]{2,1,0:T(8,128)}, f32[8,16,115...) custom-call(bf16[4,4,2,4,3,4,16,128]{7,6,5,4,3,2,1,0:T(8,128)(2,1)} , ...), custom_call_target="tpu_custom_call" | custom-call | tf_op jit(solution)/shard_map/tables/pallas_call | solution.py:1059
  281.2 0.0 copy-done
  281.2 0.8 copy.38
  282.0 0.0 copy-done.1
  282.0 0.8 copy.39
Async XLA Ops:
  270.8 10.4 %copy-start = (bf16[256,1152]{1,0:T(8,128)(2,1)S(1)}, bf16[256,1152]{1,0:T(8,128)(2,1)}, u32[]{:S(2)}) copy-start(bf16[256,1152]{1,0:T(8,128)(2,1)} %get-tuple-element.73) | copy-start | bytes 1769476
  270.8 11.2 %copy-start.1 = (bf16[256,1152]{1,0:T(8,128)(2,1)S(1)}, bf16[256,1152]{1,0:T(8,128)(2,1)}, u32[]{:S(2)}) copy-start(bf16[256,1152]{1,0:T(8,128)(2,1)} %get-tuple-element.87) | copy-start | bytes 1769476

commit v4 on v3

v4 whole, which is shorter than its diff:
```python
import functools

import jax
import jax.numpy as jnp
from jax import lax
from jax.experimental import pallas as pl
from jax.experimental.pallas import tpu as pltpu
from jax.sharding import PartitionSpec as P

epsilon = 1e-06
softcap = 50.0
MESH = pl.DeviceIdType.MESH
bf16 = jnp.bfloat16
f32 = jnp.float32

D = 1152
SEQ = 4
ROWS = 256
UNITS = 54
BLOCK = 64
TILE = 256
MIB = 1 << 20


def dot(a, b):
    return lax.dot_general(a, b, (((1,), (0,)), ((), ())), preferred_element_type=f32)


def dot_nt(a, b):
    return lax.dot_general(a, b, (((1,), (1,)), ((), ())), preferred_element_type=f32)


def dot_tn(a, b):
    return lax.dot_general(a, b, (((0,), (0,)), ((), ())), preferred_element_type=f32)


def normed(values, gain_vector):
    return values * lax.rsqrt(jnp.mean(values * values, -1, keepdims=True) + epsilon) * gain_vector


def norm_back(values, gain_vector, cotangent):
    inverse = lax.rsqrt(jnp.mean(values * values, -1, keepdims=True) + epsilon)
    scaled = cotangent * gain_vector
    mean_part = jnp.mean(scaled * values, -1, keepdims=True)
    return inverse * (scaled - values * (inverse * inverse * mean_part))


def seq_peers():
    dp, me = lax.axis_index("dp"), lax.axis_index("seq")
    return [(dp, lax.rem(me + shift, SEQ)) for shift in (1, 2, 3)]


def greet(peers):
    barrier = pltpu.get_barrier_semaphore()
    for peer in peers:
        pl.semaphore_signal(barrier, inc=1, device_id=peer, device_id_type=MESH)
    pl.semaphore_wait(barrier, len(peers))


def staged_call(kernel, name, operands, kinds, results, scratch, collective_id=None):
    count, made = len(operands), len(results)
    held = [i for i in range(count) if kinds[i] == "v"]
    given = [i for i in range(made) if results[i][2] == "v"]

    def body(*refs):
        outer = list(refs[: count + made])
        inner = list(outer)
        rest = refs[count + made :]
        for n, i in enumerate(held):
            inner[i] = rest[n]
        for n, i in enumerate(given):
            inner[count + i] = rest[len(held) + n]
        sems, rest = rest[len(held) + len(given)], rest[len(held) + len(given) + 1 :]
        ins = {i: pltpu.make_async_copy(outer[i], inner[i], sems.at[n]) for n, i in enumerate(held)}
        outs = {
            i: pltpu.make_async_copy(inner[count + i], outer[count + i], sems.at[len(held) + n])
            for n, i in enumerate(given)
        }
        waiting, leaving = set(ins), []
        for moving in ins.values():
            moving.start()

        def arrive(*which):
            for i in which or sorted(waiting):
                if i in waiting:
                    waiting.discard(i)
                    ins[i].wait()

        def leave(*which):
            for i in which:
                outs[i].start()
                leaving.append(i)

        kernel(arrive, leave, *inner, *rest)
        leave(*[i for i in given if i not in leaving])
        for i in given:
            outs[i].wait()

    spaces = {"v": pl.ANY, "h": pl.ANY, "s": pltpu.SMEM}
    params = dict(vmem_limit_bytes=63 * MIB)
    if collective_id is not None:
        params.update(collective_id=collective_id, has_side_effects=True)
    return pl.pallas_call(
        body,
        out_shape=[jax.ShapeDtypeStruct(shape, dtype) for shape, dtype, _ in results],
        in_specs=[pl.BlockSpec(memory_space=spaces[k]) for k in kinds],
        out_specs=[pl.BlockSpec(memory_space=pl.ANY)] * made,
        scratch_shapes=[pltpu.VMEM(operands[i].shape, operands[i].dtype) for i in held]
        + [pltpu.VMEM(results[i][0], results[i][1]) for i in given]
        + [pltpu.SemaphoreType.DMA((len(held) + len(given),))]
        + scratch,
        compiler_params=pltpu.CompilerParams(**params),
        name=name,
    )(*operands)


def place():
    dp = lax.axis_index("dp")
    return lax.axis_index("seq"), dp // 8, lax.rem(dp // 2, 4), lax.rem(dp, 2)


def at(x, y, z, core):
    return ((lax.rem(y, 4) * 4 + lax.rem(z, 4)) * 2 + core, lax.rem(x, 4))


def plane_peers():
    x, y, z, core = place()
    return [at(x, y + k, z, core) for k in (1, 2, 3)] + [at(x, y, z + k, core) for k in (1, 2, 3)]


def sibling():
    x, y, z, core = place()
    return at(x, y, z, 1 - core)


def remote(src, dst, send_sem, recv_sem, peer):
    return pltpu.make_async_remote_copy(
        src_ref=src, dst_ref=dst, send_sem=send_sem, recv_sem=recv_sem,
        device_id=peer, device_id_type=MESH,
    )


class PlaneGather:
    def __init__(self, own, buffer, send_sem, recv_sem):
        self.x, self.y, self.z, self.core = place()
        self.own, self.buffer, self.send, self.recv = own, buffer, send_sem, recv_sem

    def _copy(self, src, dst, slot, peer):
        return remote(src, dst, self.send.at[slot], self.recv.at[slot], peer)

    def _first(self, k):
        x, y, z, core = self.x, self.y, self.z, self.core
        peer = at(x, y + k * (1 - core), z + k * core, core)
        return self._copy(self.own, self.buffer.at[y, z, core], k - 1, peer)

    def _line(self, core, back):
        if core == 0:
            return self.buffer.at[:, lax.rem(self.z + 4 - back, 4), 0]
        return self.buffer.at[lax.rem(self.y + 4 - back, 4), :, 1]

    def _second(self, core, k):
        line = self._line(core, 0)
        peer = at(self.x, self.y + k * core, self.z + k * (1 - core), core)
        return self._copy(line, line, 2 + k, peer)

    def _pass(self, core, half):
        back, k = ((1, 1), (3, 3))[half]
        line = self._line(core, back).at[2 * half : 2 * half + 2]
        peer = at(self.x, self.y + k * core, self.z + k * (1 - core), core)
        return self._copy(line, line, (4, 10)[half], peer)

    def _swap(self, core, back):
        line = self._line(core, back)
        return self._copy(line, line, 6 + back, at(self.x, self.y, self.z, 1 - core))

    def _both(self, act):
        for core in (0, 1):
            pl.when(self.core == core)(functools.partial(act, core))

    def start(self):
        for k in (2, 1, 3):
            self._first(k).start()

    def middle(self):
        for k in (1, 3, 2):
            self._first(k).wait()

        def act(core):
            for k in (1, 3):
                self._second(core, k).start()
            self._swap(core, 0).start()

        self._both(act)

    def late(self):
        def act(core):
            for half, k in ((0, 1), (1, 3)):
                self._second(core, k).wait()
                self._pass(core, half).start()
                self._swap(core, k).start()

        self._both(act)

    def last(self):
        def act(core):
            for half in (0, 1):
                self._pass(core, half).wait()
            self._swap(core, 2).start()

        self._both(act)

    def finish(self):
        def act(core):
            for back in (0, 1, 3, 2):
                self._swap(core, back).wait()

        self._both(act)


class LineSum:
    def __init__(self, parts, landed, send_sem, recv_sem):
        self.me, self.peers = lax.axis_index("seq"), seq_peers()
        self.parts, self.landed, self.send, self.recv = parts, landed, send_sem, recv_sem

    def _copy(self, shift):
        return remote(
            self.parts.at[lax.rem(self.me + shift, SEQ)], self.landed.at[shift - 1],
            self.send.at[shift - 1], self.recv.at[shift - 1], self.peers[shift - 1],
        )

    def start(self):
        for shift in (2, 1, 3):
            self._copy(shift).start()

    def finish(self):
        for shift in (1, 3, 2):
            self._copy(shift).wait()


class PlaneExchange:
    def __init__(self, first, second, third, fourth, send_sem, recv_sem):
        self.x, self.y, self.z, self.core = place()
        self.first, self.second, self.third, self.fourth = first, second, third, fourth
        self.send, self.recv = send_sem, recv_sem

    def _copy(self, src, dst, slot, peer):
        return remote(src, dst, self.send.at[slot], self.recv.at[slot], peer)

    def _along_y(self, k):
        y = lax.rem(self.y + k, 4)
        return self._copy(self.first.at[y], self.second.at[k], k - 1, at(self.x, y, self.z, self.core))

    def _along_z(self, k):
        z = lax.rem(self.z + k, 4)
        return self._copy(self.second.at[:, z], self.third.at[k], 2 + k, at(self.x, self.y, z, self.core))

    def _across(self):
        return self._copy(self.third, self.fourth, 6, sibling())

    def start(self):
        for k in (2, 1, 3):
            self._along_y(k).start()
        self.second[0] = self.first[self.y]

    def middle(self):
        for k in (1, 3, 2):
            self._along_y(k).wait()
        for k in (2, 1, 3):
            self._along_z(k).start()
        self.third[0] = self.second[:, self.z]

    def late(self):
        for k in (1, 3, 2):
            self._along_z(k).wait()
        self._across().start()

    def finish(self):
        self._across().wait()

    def total(self, marks, out):
        slots = self.first.shape[2]
        out[...] = jnp.zeros_like(out)

        def add(i, _):
            kz, ky = i // 4, lax.rem(i, 4)
            for held, known in ((self.third, marks.third), (self.fourth, marks.fourth)):
                weights = known[kz, ky, 0, self.core]
                for slot in range(slots):
                    rows = held[kz, ky, slot].astype(f32)
                    for a in range(4):
                        out[slot, a] += weights[a : a + 1] * rows
            return 0

        lax.fori_loop(0, 16, add, 0)


class LineGather:
    def __init__(self, buffer, send_sem, recv_sem):
        self.me, self.peers = lax.axis_index("seq"), seq_peers()
        self.buffer, self.send, self.recv = buffer, send_sem, recv_sem

    def _copy(self, shift):
        mine = self.buffer.at[self.me]
        return remote(mine, mine, self.send.at[shift - 1], self.recv.at[shift - 1], self.peers[shift - 1])

    def start(self):
        for shift in (2, 1, 3):
            self._copy(shift).start()

    def finish(self):
        for shift in (1, 3, 2):
            self._copy(shift).wait()


WIDE = D + 128
HIDDEN = 32 * BLOCK
HALF = ROWS // 2
ROOT = 0.7978845608028654
CUBE = ROOT * 0.044715
FF_BLOCKS = 48
LATE = 14
SCORE = 1.0 / 16.0


def allowed_pairs(segment_rows, segment_column, me, chunk):
    keys = lax.broadcasted_iota(jnp.int32, (ROWS, ROWS), 1) + chunk * ROWS
    queries = lax.broadcasted_iota(jnp.int32, (ROWS, ROWS), 0) + me * ROWS
    return (segment_column[...] == segment_rows[chunk]) & (keys <= queries)


def layer_kernel(
    arrive, leave,
    layer_input, pack_qkv, pack_o, pack_gu, pack_down, segment_rows, segment_column, gains,
    first_qkv, second_q, second_kv, first_o, second_o,
    ext_gu, ext_down, first_gu, second_down, out_grad, own_marks,
    layer_out, input_grad, all_early, all_late,
    queries, totals, context, attn_proj, qkv_latent, o_latent, mixed_grad, early_sum,
    got_qkv, got_o, first_norm, kv_all, mixed,
    w_gu, w_down, inputs, down_grads, hidden, act_gate, act_up, total,
    down_latents, gu_grads, packed, early, early_landed,
    far, landed_half, near, landed,
    m1, m2, m3, m4, e2, e3, e4, early_total, early_line,
    late, late_landed, late_sum, l2, l3, l4, late_total, late_line,
    sem_s, sem_r, kv_s, kv_r, tok_s, tok_r, rs_s, rs_r, ag_s, ag_r, line_s, line_r, loc,
    back_s, back_r, plane_s, plane_r, spread_s, spread_r, out_s, out_r,
):
    me, y, z, core = place()
    line = seq_peers()
    ahead, _, behind = line
    greet(line + plane_peers() + [sibling()])

    all_gu, all_down = w_gu.at[:, :, :, :, 0:D], w_down.at[:, :, :, :, 0:D]
    gathers = [
        PlaneGather(own, got, sem_s.at[i], sem_r.at[i])
        for i, (own, got) in enumerate(
            ((pack_qkv, got_qkv), (pack_o, got_o), (pack_gu, all_gu), (pack_down, all_down))
        )
    ]
    g_qkv, g_o, g_gu, g_down = gathers
    own_copies = [
        pltpu.make_async_copy(g.own, g.buffer.at[y, z, core], loc.at[i]) for i, g in enumerate(gathers)
    ]
    ext_copies = [
        pltpu.make_async_copy(ext_gu, w_gu.at[:, :, :, :, D:WIDE], loc.at[4]),
        pltpu.make_async_copy(ext_down, w_down.at[:, :, :, :, D:WIDE], loc.at[5]),
    ]
    arrive(1)
    g_qkv.start()
    own_copies[0].start()
    arrive()
    for moving in own_copies[1:] + ext_copies:
        moving.start()
    gain_first, gain_second, gain_third, gain_fourth = [gains[i : i + 1] for i in range(4)]
    first_norm[...] = normed(layer_input[...].astype(f32), gain_first).astype(bf16)
    latent = dot_nt(first_norm[...], first_qkv[...]).astype(bf16)
    qkv_latent[...] = latent
    for moving in own_copies:
        moving.wait()
    g_qkv.middle()
    g_o.start()
    g_qkv.late()
    g_gu.start()
    g_down.start()
    g_qkv.last()
    g_o.middle()
    g_qkv.finish()

    def unmix(i, _):
        pairs = got_qkv[i, :, :, 32:48].astype(f32).reshape(8, 2, 8, D)
        got_qkv[i, 0:2, :, 32:48] = pairs[:, 0].reshape(2, 2, 16, D).astype(bf16)
        got_qkv[i, 2:4, :, 32:48] = pairs[:, 1].reshape(2, 2, 16, D).astype(bf16)
        return 0

    lax.fori_loop(0, 4, unmix, 0)
    key_rows = lambda: got_qkv[:, 0:2, :, 32:48].reshape(256, D)
    value_rows = lambda: got_qkv[:, 2:4, :, 32:48].reshape(256, D)
    kv_low = dot(latent, second_kv[...])
    kv_all[me, :, 0:256] = (dot_nt(first_norm[...], key_rows()) + kv_low[:, 0:256]).astype(bf16)
    kv_all[me, :, 256:512] = (dot_nt(first_norm[...], value_rows()) + kv_low[:, 256:512]).astype(bf16)

    def kv_copy(shift):
        return remote(kv_all.at[me], kv_all.at[me], kv_s.at[shift - 1], kv_r.at[shift - 1], line[shift - 1])

    for shift in (1, 2, 3):
        pl.when(me + shift < SEQ)(lambda shift=shift: kv_copy(shift).start())

    def query(h, _):
        rows = got_qkv[h, :, :, 0:32].reshape(256, D)
        queries[h] = (dot_nt(first_norm[...], rows) + dot(latent, second_q[h])).astype(bf16)
        context[h] = jnp.zeros((ROWS, 256), f32)
        return 0

    lax.fori_loop(0, 4, query, 0)
    totals[...] = jnp.zeros_like(totals)
    head_lane = lax.broadcasted_iota(jnp.int32, (ROWS, 128), 1)

    def total_of(h):
        return jnp.sum(jnp.where(head_lane == h, totals[...], 0.0), -1, keepdims=True)

    g_gu.middle()
    g_down.middle()

    def attend(chunk):
        keys, held = kv_all[chunk, :, 0:256], kv_all[chunk, :, 256:512]
        allowed = allowed_pairs(segment_rows, segment_column, me, chunk)

        def head(h, _):
            bent = jnp.tanh(dot_nt(queries[h], keys) * (SCORE / softcap))
            weight = jnp.where(allowed, jnp.exp(softcap * bent), 0.0).astype(bf16)
            totals[...] += jnp.where(head_lane == h, jnp.sum(weight.astype(f32), -1, keepdims=True), 0.0)
            context[h] += dot(weight, held)
            return 0

        lax.fori_loop(0, 4, head, 0)

    attend(me)
    g_o.late()
    g_o.last()
    for shift in (1, 2, 3):
        def arrived(shift=shift):
            kv_copy(shift).wait_recv()
            attend(me - shift)

        pl.when(me >= shift)(arrived)

    g_o.finish()
    proj = jnp.zeros((ROWS, D), f32)
    thin = jnp.zeros((ROWS, 16), f32)
    for h in range(4):
        context[h] = context[h] / total_of(h)
        low = context[h].astype(bf16)
        proj = proj + dot(low, got_o[h].reshape(256, D))
        thin = thin + dot_nt(low, first_o[h])
    o_latent[...] = thin.astype(bf16)
    proj = proj + dot(o_latent[...], second_o[...])
    attn_proj[...] = proj
    mid = layer_input[...].astype(f32) + normed(proj, gain_second)
    mixed[...] = mid
    inputs[0, :, 0:D] = normed(mid, gain_third).astype(bf16)

    low, high = slice(0, HALF), slice(HALF, ROWS)

    def passing(buffer, send, recv):
        def move(from_slot, to_slot, rows, index, peer):
            src, dst = buffer.at[from_slot, rows, 0:D], buffer.at[to_slot, rows, 0:D]
            return remote(src, dst, send.at[index], recv.at[index], peer)

        return [
            move(0, 2, low, 0, ahead), move(0, 1, high, 1, behind),
            move(0, 2, high, 2, ahead), move(0, 1, low, 3, behind),
            move(2, 3, low, 4, ahead), move(1, 3, high, 5, behind),
        ]

    token_moves = passing(inputs, tok_s, tok_r)
    for i in range(4):
        token_moves[i].start()
    g_gu.late()
    for i in range(4):
        for k in range(4):
            m1[i, k, 0] = own_marks[...]
    m_plane = PlaneExchange(m1, m2, m3, m4, plane_s.at[2], plane_r.at[2])
    g_down.late()
    g_gu.last()
    for moving in ext_copies:
        moving.wait()
    g_gu.finish()

    def gate_rows(j):
        return w_gu[j // 2, pl.ds(2 * lax.rem(j, 2), 2), :, 0:64].reshape(TILE, WIDE)

    def up_rows(j):
        return w_gu[j // 2, pl.ds(2 * lax.rem(j, 2), 2), :, 64:128].reshape(TILE, WIDE)

    def down_rows(j):
        return w_down[j // 2, pl.ds(2 * lax.rem(j, 2), 2)].reshape(TILE, WIDE)

    def lanes(j, size=TILE):
        return pl.ds(pl.multiple_of(j * size, size), size)

    def forward_open(slot, many):
        size = many * ROWS
        part = slice(slot, slot + many)
        inputs[part, :, D:WIDE] = (
            dot_nt(inputs[part, :, 0:D].reshape(size, D), first_gu[...]).astype(bf16).reshape(many, ROWS, 128)
        )

        def step(j, _):
            rows = inputs[part].reshape(size, WIDE)
            gate = dot_nt(rows, gate_rows(j))
            upward = dot_nt(rows, up_rows(j))
            square = gate * gate
            bent = jnp.tanh(gate * (ROOT + CUBE * square))
            half = 0.5 * bent + 0.5
            gelu = gate * half
            slope = half + gelu * ((1.0 - bent) * (ROOT + 3.0 * CUBE * square))
            shape = (many, ROWS, TILE)
            hidden[part, :, lanes(j)] = (gelu * upward).astype(bf16).reshape(shape)
            act_gate[part, :, lanes(j)] = gelu.astype(bf16).reshape(shape)
            act_up[part, :, lanes(j)] = (upward * slope).astype(bf16).reshape(shape)
            return 0

        lax.fori_loop(0, 8, step, 0, unroll=2)

    def forward_close(slot, many):
        size = many * ROWS
        part = slice(slot, slot + many)

        def close(n, _):
            rows = hidden[part].reshape(size, HIDDEN)
            total[0:size, lanes(n)] = dot(rows, w_down[:, :, :, :, lanes(n)].reshape(HIDDEN, TILE))
            return 0

        lax.fori_loop(0, 5, close, 0)
        down_latent = total[0:size, D:WIDE].astype(bf16)
        down_latents[slot * ROWS : slot * ROWS + size] = down_latent
        total[0:size, 0:D] += dot(down_latent, second_down[...])

    def backward_open(slot, many):
        size = many * ROWS
        part = slice(slot, slot + many)
        latent_grad = dot_nt(down_grads[part, :, 0:D].reshape(size, D), second_down[...])
        down_grads[part, :, D:WIDE] = latent_grad.astype(bf16).reshape(many, ROWS, 128)

        def step(j, _):
            shape = (many, ROWS, TILE)
            hidden_grad = dot_nt(down_grads[part].reshape(size, WIDE), down_rows(j)).reshape(shape)
            gate_grad = (hidden_grad * act_up[part, :, lanes(j)].astype(f32)).astype(bf16)
            up_grad = (hidden_grad * act_gate[part, :, lanes(j)].astype(f32)).astype(bf16)
            act_up[part, :, lanes(j)] = gate_grad
            act_gate[part, :, lanes(j)] = up_grad
            return 0

        lax.fori_loop(0, 8, step, 0, unroll=2)

    def backward_close(slot, many):
        size = many * ROWS
        part = slice(slot, slot + many)

        def close(n, _):
            total[0:size, lanes(n)] = dot(
                act_up[part].reshape(size, HIDDEN), w_gu[:, :, :, 0:64, lanes(n)].reshape(HIDDEN, TILE)
            ) + dot(
                act_gate[part].reshape(size, HIDDEN), w_gu[:, :, :, 64:128, lanes(n)].reshape(HIDDEN, TILE)
            )
            return 0

        lax.fori_loop(0, 5, close, 0)
        gu_grad = total[0:size, D:WIDE].astype(bf16)
        gu_grads[slot * ROWS : slot * ROWS + size] = gu_grad
        total[0:size, 0:D] += dot(gu_grad, first_gu[...])

    def factors():
        latent = inputs[:, :, D:WIDE].reshape(SEQ * ROWS, 128)[:, 0:32]
        latent_grad = down_grads[:, :, D:WIDE].reshape(SEQ * ROWS, 128)[:, 32:48]

        def piece(j, _):
            gate_part = dot_tn(latent, act_up[:, :, lanes(j)].reshape(SEQ * ROWS, TILE))
            up_part = dot_tn(latent, act_gate[:, :, lanes(j)].reshape(SEQ * ROWS, TILE))
            down_part = dot_tn(latent_grad, hidden[:, :, lanes(j)].reshape(SEQ * ROWS, TILE))
            packed[0:16, lanes(j)] = gate_part[0:16].astype(bf16)
            packed[16:32, lanes(j)] = up_part[16:32].astype(bf16)
            packed[32:48, lanes(j)] = down_part.astype(bf16)
            return 0

        lax.fori_loop(0, 8, piece, 0, unroll=2)

    def scatter(base, finish, others, own=None):
        finish(3, 1)
        far[...] = total[0:ROWS, 0:D].astype(bf16)
        far_moves = [
            remote(far.at[low], landed_half.at[0], rs_s.at[base + 4], rs_r.at[base + 4], behind),
            remote(far.at[high], landed_half.at[1], rs_s.at[base + 5], rs_r.at[base + 5], ahead),
        ]
        for moving in far_moves:
            moving.start()
        finish(1, 2)
        near_moves = [
            remote(near.at[0, low], landed.at[0, low], rs_s.at[base], rs_r.at[base], ahead),
            remote(near.at[0, high], landed.at[0, high], rs_s.at[base + 1], rs_r.at[base + 1], ahead),
            remote(near.at[1, high], landed.at[1, high], rs_s.at[base + 2], rs_r.at[base + 2], behind),
            remote(near.at[1, low], landed.at[1, low], rs_s.at[base + 3], rs_r.at[base + 3], behind),
        ]
        near[0, low] = total[0:HALF, 0:D].astype(bf16)
        near_moves[0].start()
        near[1, high] = total[ROWS + HALF : 2 * ROWS, 0:D].astype(bf16)
        near_moves[2].start()
        near[0, high] = total[HALF:ROWS, 0:D].astype(bf16)
        near[1, low] = total[ROWS : ROWS + HALF, 0:D].astype(bf16)
        if own is not None:
            own()
        far_moves[1].wait()
        near[0, high] = (near[0, high].astype(f32) + landed_half[1].astype(f32)).astype(bf16)
        near_moves[1].start()
        far_moves[0].wait()
        near[1, low] = (near[1, low].astype(f32) + landed_half[0].astype(f32)).astype(bf16)
        near_moves[3].start()
        others()
        for moving in near_moves:
            moving.wait()

    def forward_own():
        forward_close(0, 1)
        mixed_grad[...] = total[0:ROWS, 0:D]

    m_plane.start()
    forward_open(0, 1)
    token_moves[0].wait()
    token_moves[4].start()
    token_moves[1].wait()
    token_moves[5].start()
    token_moves[2].wait()
    token_moves[3].wait()
    forward_open(1, 2)
    g_down.last()
    token_moves[4].wait()
    token_moves[5].wait()
    forward_open(3, 1)
    g_down.finish()
    scatter(0, forward_close, forward_own)
    m_plane.middle()
    down_proj = mixed_grad[...] + landed[0].astype(f32) + landed[1].astype(f32)
    layer_out[...] = (mixed[...] + normed(down_proj, gain_fourth)).astype(bf16)
    leave(0)
    down_grads[0, :, 0:D] = norm_back(down_proj, gain_fourth, out_grad[...].astype(f32)).astype(bf16)
    grad_moves = passing(down_grads, ag_s, ag_r)
    for i in range(4):
        grad_moves[i].start()

    early_parts = early.reshape(SEQ, FF_BLOCKS, 16, 128)
    e_line = LineSum(early_parts, early_landed, line_s.at[0], line_r.at[0])

    def unpad(j, _):
        start = jnp.minimum((j * 128 // 216) // 2 * 128, HIDDEN // 2 - 256)
        lane = start + lax.broadcasted_iota(jnp.int32, (256, 128), 0)
        within = lane & 63
        unit = (lane >> 6) * 216 + me * UNITS + within
        goal = j * 128 + lax.broadcasted_iota(jnp.int32, (256, 128), 1)
        chosen = jnp.where((unit == goal) & (within < UNITS), 1.0, 0.0).astype(bf16)
        for half in (0, 1):
            rows = packed[:, pl.ds(pl.multiple_of(start + half * HIDDEN // 2, 128), 256)]
            moved = dot(rows, chosen).astype(bf16)
            for i in range(3):
                early[54 * i + 27 * half + j] = moved[16 * i : 16 * i + 16]
        return 0

    def put(start, rows, buffer):
        for i in range(rows.shape[1] // 128):
            buffer[start + i] = rows[:, i * 128 : (i + 1) * 128].astype(bf16)

    def spread_factors():
        lax.fori_loop(0, 27, unpad, 0, unroll=3)
        all_gu_grads = gu_grads[...]
        gu_part = dot_tn(all_gu_grads[:, 0:32], inputs[:, :, 0:D].reshape(SEQ * ROWS, D))
        put(162, gu_part[0:16], early)
        put(171, gu_part[16:32], early)
        put(180, dot_tn(down_latents[:, 32:48], down_grads[:, :, 0:D].reshape(SEQ * ROWS, D)), early)
        for i in range(189, 192):
            early[i] = jnp.zeros((16, 128), bf16)
        e_line.start()

    backward_open(0, 1)
    backward_close(0, 1)
    mixed_grad[...] = total[0:ROWS, 0:D]
    m_plane.late()
    grad_moves[0].wait()
    grad_moves[4].start()
    grad_moves[1].wait()
    grad_moves[5].start()
    grad_moves[2].wait()
    grad_moves[3].wait()
    backward_open(1, 2)
    grad_moves[4].wait()
    grad_moves[5].wait()
    backward_open(3, 1)

    def all_factors():
        factors()
        spread_factors()

    scatter(6, backward_close, all_factors)
    m_plane.finish()
    own_sum = mixed_grad[...] + landed[0].astype(f32) + landed[1].astype(f32)
    mixed_grad[...] = out_grad[...].astype(f32) + norm_back(mixed[...], gain_third, own_sum)

    head_grads = [down_grads.at[3, :, 256 * h : 256 * h + 256] for h in range(4)]
    key_part, value_part = total.at[0:ROWS, 512:768], total.at[0:ROWS, 768:1024]
    kv_own = total.at[ROWS : 2 * ROWS, 512:1024]

    def query_part(h):
        row, lane = h // 2, lax.rem(h, 2)
        return total.at[pl.ds(pl.multiple_of(row * ROWS, ROWS), ROWS), pl.ds(pl.multiple_of(lane * 256, 256), 256)]

    def head_grad(h):
        return down_grads[3, :, pl.ds(pl.multiple_of(h * 256, 256), 256)]

    far[...] = norm_back(attn_proj[...], gain_second, mixed_grad[...]).astype(bf16)
    o_grad = dot_nt(far[...], second_o[...]).astype(bf16)

    for h in range(4):
        low = (dot_nt(far[...], got_o[h].reshape(256, D)) + dot(o_grad, first_o[h])).astype(bf16)
        head_grads[h][...] = low
        query_part(h)[...] = jnp.zeros((ROWS, 256), f32)

    def attend_back(chunk):
        keys, held = kv_all[chunk, :, 0:256], kv_all[chunk, :, 256:512]
        allowed = allowed_pairs(segment_rows, segment_column, me, chunk)
        key_part[...] = jnp.zeros_like(key_part)
        value_part[...] = jnp.zeros_like(value_part)

        def head(h, _):
            bent = jnp.tanh(dot_nt(queries[h], keys) * (SCORE / softcap))
            weight = jnp.where(allowed, jnp.exp(softcap * bent), 0.0).astype(bf16).astype(f32)
            probs = weight / total_of(h)
            grads = head_grad(h)
            centre = jnp.sum(grads.astype(f32) * context[h], -1, keepdims=True)
            prob_grad = dot_nt(grads, held)
            raw_grad = (probs * (prob_grad - centre) * ((1.0 - bent * bent) * SCORE)).astype(bf16)
            query_part(h)[...] += dot(raw_grad, keys)
            key_part[...] += dot_tn(raw_grad, queries[h])
            value_part[...] += dot_tn(probs.astype(bf16), grads)
            return 0

        lax.fori_loop(0, 4, head, 0)

    def back_copy(shift):
        peer = line[3 - shift]
        return remote(w_down.at[shift - 1, 2:4, :, :, 0:512], w_down.at[shift - 1, 0:2, :, :, 0:512], back_s.at[shift - 1], back_r.at[shift - 1], peer)

    for shift in (3, 2, 1):
        def earlier(shift=shift):
            attend_back(me - shift)
            w_down[shift - 1, 2:4, :, :, 0:256] = key_part[...].astype(bf16).reshape(2, 2, BLOCK, 256)
            w_down[shift - 1, 2:4, :, :, 256:512] = value_part[...].astype(bf16).reshape(2, 2, BLOCK, 256)
            back_copy(shift).start()

        pl.when(me >= shift)(earlier)

    e_line.finish()

    def add_early(i, _):
        for k in range(3):
            own = early_parts[me, 3 * i + k].astype(f32)
            for s in range(3):
                own = own + early_landed[s, 3 * i + k].astype(f32)
            early_sum[i // 4, lax.rem(i, 4), k] = own.astype(bf16)
        return 0

    lax.fori_loop(0, 16, add_early, 0)
    e_plane = PlaneExchange(early_sum, e2, e3, e4, plane_s.at[0], plane_r.at[0])
    e_plane.start()

    attend_back(me)
    for h in range(4):
        put(39 + 2 * h, dot_tn(o_grad, context[h].astype(bf16)), late)
    put(47, dot_tn(o_latent[...], far[...]), late)
    kv_own[:, 0:256] = key_part[...]
    kv_own[:, 256:512] = value_part[...]

    e_plane.middle()
    e_plane.late()
    e_plane.finish()
    e_plane.total(m_plane, early_total)
    early_line[me] = early_total[...].astype(bf16)
    e_spread = LineGather(early_line, spread_s.at[0], spread_r.at[0])
    e_spread.start()
    for shift in (1, 2, 3):
        def collect(shift=shift):
            back_copy(shift).wait_recv()
            kv_own[...] += w_down[shift - 1, 0:2, :, :, 0:512].reshape(ROWS, 512).astype(f32)

        pl.when(me + shift < SEQ)(collect)

    e_spread.finish()
    own_early = pltpu.make_async_copy(early_line, all_early.at[y, z, core], loc.at[0])
    own_early.start()
    e_out = PlaneGather(early_line, all_early, out_s.at[0], out_r.at[0])
    e_out.start()

    key_value = kv_own[...].astype(bf16)
    thin = dot_nt(key_value, second_kv[...])
    back = dot(key_value[:, 0:256], key_rows()) + dot(key_value[:, 256:512], value_rows())
    for h in range(4):
        low = query_part(h)[...].astype(bf16)
        back = back + dot(low, got_qkv[h, :, :, 0:32].reshape(256, D))
        thin = thin + dot_nt(low, second_q[h])
        put(27 + 2 * h, dot_tn(qkv_latent[...], low)[0:16], late)
    qkv_grad = thin.astype(bf16)
    back = back + dot(qkv_grad, first_qkv[...])
    in_grad = dot_tn(qkv_grad, first_norm[...])
    for i in range(3):
        put(9 * i, in_grad[16 * i : 16 * i + 16], late)
    kv_out_grad = dot_tn(qkv_latent[...], key_value)
    put(35, kv_out_grad[16:32, 0:256], late)
    put(37, kv_out_grad[32:48, 256:512], late)
    late_parts = late.reshape(SEQ, LATE, 16, 128)
    l_line = LineSum(late_parts, late_landed, line_s.at[1], line_r.at[1])
    l_line.start()
    near[0] = (mixed_grad[...] + norm_back(layer_input[...].astype(f32), gain_first, back)).astype(bf16)
    result = pltpu.make_async_copy(near.at[0], input_grad, loc.at[2])
    result.start()

    own_early.wait()
    e_out.middle()
    l_line.finish()
    for i in range(16):
        low = jnp.zeros((16, 128), bf16)
        if i < LATE:
            own = late_parts[me, i].astype(f32)
            for s in range(3):
                own = own + late_landed[s, i].astype(f32)
            low = own.astype(bf16)
        late_sum[i // 4, i % 4, 0] = low
    l_plane = PlaneExchange(late_sum, l2, l3, l4, plane_s.at[1], plane_r.at[1])
    l_plane.start()
    l_plane.middle()
    l_plane.late()
    l_plane.finish()
    l_plane.total(m_plane, late_total)
    late_line[me] = late_total[...].astype(bf16)
    l_spread = LineGather(late_line, spread_s.at[1], spread_r.at[1])
    l_spread.start()
    e_out.late()
    l_spread.finish()
    own_late = pltpu.make_async_copy(late_line, all_late.at[y, z, core], loc.at[1])
    own_late.start()
    l_out = PlaneGather(late_line, all_late, out_s.at[1], out_r.at[1])
    l_out.start()
    own_late.wait()
    l_out.middle()
    e_out.last()
    l_out.late()
    e_out.finish()
    l_out.last()
    l_out.finish()
    result.wait()
    for shift in (1, 2, 3):
        pl.when(me >= shift)(lambda shift=shift: back_copy(shift).wait_send())
    for shift in (1, 2, 3):
        pl.when(me + shift < SEQ)(lambda shift=shift: kv_copy(shift).wait_send())


def layer(*arrays):
    dma = pltpu.SemaphoreType.DMA
    vmem = pltpu.VMEM

    def reduction(slots):
        whole = vmem((4, 4, slots, 16, 128), bf16)
        return [
            whole, whole, whole,
            vmem((slots, 4, 16, 128), f32),
            vmem((SEQ, slots, 4, 16, 128), bf16),
        ]

    return staged_call(
        layer_kernel, "layer", arrays, "v" * 13 + "hhvvvv",
        [
            ((ROWS, D), bf16, "v"),
            ((ROWS, D), bf16, "h"),
            ((4, 4, 2, SEQ, 3, 4, 16, 128), bf16, "h"),
            ((4, 4, 2, SEQ, 1, 4, 16, 128), bf16, "h"),
        ],
        [
            vmem((4, ROWS, 256), bf16),
            vmem((ROWS, 128), f32),
            vmem((4, ROWS, 256), f32),
            vmem((ROWS, D), f32),
            vmem((ROWS, 48), bf16),
            vmem((ROWS, 16), bf16),
            vmem((ROWS, D), f32),
            vmem((4, 4, 3, 16, 128), bf16),
            vmem((4, 4, 2, 48, D), bf16),
            vmem((4, 4, 2, 32, D), bf16),
            vmem((ROWS, D), bf16),
            vmem((SEQ, ROWS, 512), bf16),
            vmem((ROWS, D), f32),
            vmem((4, 4, 2, 2 * BLOCK, WIDE), bf16),
            vmem((4, 4, 2, BLOCK, WIDE), bf16),
            vmem((SEQ, ROWS, WIDE), bf16),
            vmem((SEQ, ROWS, WIDE), bf16),
            vmem((SEQ, ROWS, HIDDEN), bf16),
            vmem((SEQ, ROWS, HIDDEN), bf16),
            vmem((SEQ, ROWS, HIDDEN), bf16),
            vmem((2 * ROWS, WIDE), f32),
            vmem((SEQ * ROWS, 128), bf16),
            vmem((SEQ * ROWS, 128), bf16),
            vmem((48, HIDDEN), bf16),
            vmem((SEQ * FF_BLOCKS, 16, 128), bf16),
            vmem((3, FF_BLOCKS, 16, 128), bf16),
            vmem((ROWS, D), bf16),
            vmem((2, HALF, D), bf16),
            vmem((2, ROWS, D), bf16),
            vmem((2, ROWS, D), bf16),
        ]
        + [vmem((4, 4, 1, 2, 8, 128), f32)] * 4
        + reduction(3)
        + [
            vmem((SEQ * LATE, 16, 128), bf16),
            vmem((3, LATE, 16, 128), bf16),
            vmem((4, 4, 1, 16, 128), bf16),
        ]
        + reduction(1)
        + [
            dma((4, 11)), dma((4, 11)), dma((3,)), dma((3,)), dma((6,)), dma((6,)),
            dma((12,)), dma((12,)), dma((6,)), dma((6,)), dma((2, 3)), dma((2, 3)), dma((6,)),
            dma((3,)), dma((3,)), dma((3, 7)), dma((3, 7)), dma((2, 3)), dma((2, 3)), dma((2, 11)), dma((2, 11)),
        ],
        collective_id=1,
    )


def tables_kernel(
    early, late, done_out, done_grad,
    qkv_in, q_out, kv_out, o_in, o_out, mlp_in, mlp_out, down_in, down_out, layer_out, input_grad,
):
    def copy(source, start, count, out):
        for i in range(count):
            x, place = divmod(start + i, FF_BLOCKS if source is early else LATE)
            owner, slot = divmod(place, 3 if source is early else 1)
            out[:, i * 128 : (i + 1) * 128] = source[owner // 4, owner % 4, 0, x, slot, 0].astype(f32)

    layer_out[...] = done_out[...]
    input_grad[...] = done_grad[...]
    for i in range(2):
        copy(early, 54 * i, 54, mlp_out.at[0, i])
        copy(early, 162 + 9 * i, 9, mlp_in.at[0, i])
        copy(late, 35 + 2 * i, 2, kv_out.at[0, i])
    copy(early, 108, 54, down_in.at[0])
    copy(early, 180, 9, down_out.at[0])
    for i in range(3):
        copy(late, 9 * i, 9, qkv_in.at[0, i])
    copy(late, 27, 8, q_out.at[0])
    copy(late, 39, 8, o_in.at[0])
    copy(late, 47, 9, o_out.at[0])


def put_tables(early, late, done_out, done_grad):
    shapes = (
        (3, 16, D), (16, 1024), (2, 16, 256), (16, 1024), (16, D),
        (2, 16, D), (2, 16, 6912), (16, 6912), (16, D),
    )

    def one(shape):
        rest = len(shape)
        return pl.BlockSpec((1,) + shape, lambda a, rest=rest: (a,) + (0,) * rest)

    rows = pl.BlockSpec((ROWS // 8, D), lambda a: (a, 0))

    def blocks(slots):
        return pl.BlockSpec(
            (4, 4, 1, SEQ, slots, 1, 16, 128), lambda a: (0, 0, a // 4, 0, 0, a % 4, 0, 0)
        )

    return pl.pallas_call(
        tables_kernel,
        grid=(8,),
        out_shape=[jax.ShapeDtypeStruct((8,) + shape, f32) for shape in shapes]
        + [jax.ShapeDtypeStruct((ROWS, D), bf16)] * 2,
        in_specs=[blocks(3), blocks(1), rows, rows],
        out_specs=[one(shape) for shape in shapes] + [rows, rows],
        compiler_params=pltpu.CompilerParams(vmem_limit_bytes=63 * MIB),
        name="tables",
    )(early, late, done_out, done_grad)


def prepare_kernel(
    arrive, leave, ids, place_x, segments, w_query, w_key, w_value, w_gate, w_up, w_down,
    qkv_adapt_in, q_adapt_out, kv_adapt_out, o_adapt_in, o_adapt_out,
    mlp_adapt_in, mlp_adapt_out, down_adapt_in, down_adapt_out,
    gain_one, gain_two, gain_three, gain_four,
    pack_qkv, pack_gu, pack_down, own_marks, segment_rows, segment_column,
    first_qkv, second_q, second_kv, first_o, second_o, first_gu, second_down, ext_gu, ext_down, gains,
    table, q_held, kv_held, o_held, in_held, out_held, sem,
):
    chosen, me = ids[0], place_x[0]
    mlp_out, down_in = mlp_adapt_out.at[chosen], down_adapt_in.at[chosen]
    moves = [
        (mlp_out.at[0], table.at[0:16]),
        (mlp_out.at[1], table.at[16:32]),
        (down_in, table.at[32:48]),
        (q_adapt_out.at[chosen], q_held),
        (kv_adapt_out.at[chosen], kv_held),
        (o_adapt_in.at[chosen], o_held),
        (o_adapt_out.at[chosen], second_o),
        (mlp_adapt_in.at[chosen], in_held),
        (down_adapt_out.at[chosen], out_held),
        (qkv_adapt_in.at[chosen], first_qkv),
    ]
    moves = [pltpu.make_async_copy(src, dst, sem.at[i]) for i, (src, dst) in enumerate(moves)]
    for moving in moves:
        moving.start()
    iota = lambda shape, axis: lax.broadcasted_iota(jnp.int32, shape, axis)
    ones = lambda where: jnp.where(where, 1.0, 0.0).astype(bf16)

    def placed(count, first):
        return ones(iota((48, count), 0) == iota((48, count), 1) + first)

    table[48:128] = jnp.zeros((80, 6912), bf16)
    arrive()
    rows = dot(placed(32, 0), w_query[...]) + dot(placed(8, 32), w_key[...])
    pack_qkv[...] = (rows + dot(placed(8, 40), w_value[...])).astype(bf16)
    row, unit = iota((BLOCK, 216), 0), iota((BLOCK, 216), 1)
    quarter = ones((unit == me * UNITS + row) & (row < UNITS))
    pack_gu[0:64] = dot(quarter, w_gate[...]).astype(bf16)
    pack_gu[64:128] = dot(quarter, w_up[...]).astype(bf16)
    pack_down[...] = dot(quarter, w_down[...]).astype(bf16)

    for i, gain in enumerate((gain_one, gain_two, gain_three, gain_four)):
        gains[i : i + 1] = gain[...].reshape(1, D)
    leave(0, 1, 2)
    adapter = iota((8, 128), 0)
    for half in (0, 1):
        own_marks[half] = jnp.where((adapter + 4 * half == chosen) & (adapter < 4), 1.0, 0.0)
    for i in range(SEQ):
        segment_rows[i] = segments[:, i * ROWS : (i + 1) * ROWS]
    square = iota((ROWS, ROWS), 0) == iota((ROWS, ROWS), 1)
    segment_column[...] = jnp.sum(jnp.where(square, segment_rows[me], 0), -1, keepdims=True)

    for moving in moves:
        moving.wait()
    second_q[...] = jnp.zeros_like(second_q)
    for h in range(4):
        second_q[h, 0:16] = q_held[:, h * 256 : (h + 1) * 256]
        first_o[h] = o_held[:, h * 256 : (h + 1) * 256]
    second_kv[...] = jnp.zeros_like(second_kv)
    second_kv[16:32, 0:256] = kv_held[0]
    second_kv[32:48, 256:512] = kv_held[1]
    first_gu[0:16] = in_held[0]
    first_gu[16:32] = in_held[1]
    first_gu[32:128] = jnp.zeros((96, D), bf16)
    second_down[0:32] = jnp.zeros((32, D), bf16)
    second_down[32:48] = out_held[...]
    second_down[48:128] = jnp.zeros((80, D), bf16)

    def spread(d, _):
        first = 216 * d + me * UNITS
        start = jnp.minimum(first // 128 * 128, 6912 - 256)
        row = iota((BLOCK, 256), 0)
        picked = ones((first + row == start + iota((BLOCK, 256), 1)) & (row < UNITS))
        held = dot_nt(picked, table[:, pl.ds(pl.multiple_of(start, 128), 256)])
        lane = iota((BLOCK, 128), 1)
        ext_gu[d, 0:64] = jnp.where(lane < 16, held, 0.0).astype(bf16)
        ext_gu[d, 64:128] = jnp.where((lane >= 16) & (lane < 32), held, 0.0).astype(bf16)
        ext_down[d] = jnp.where(lane >= 32, held, 0.0).astype(bf16)
        return 0

    lax.fori_loop(0, 32, spread, 0, unroll=4)


def prepare(*arrays):
    shapes = [
        ((48, D), bf16), ((128, D), bf16), ((64, D), bf16), ((2, 8, 128), f32),
        ((SEQ, 1, ROWS), jnp.int32), ((ROWS, 1), jnp.int32),
        ((3, 16, D), bf16), ((4, 48, 256), bf16), ((48, 512), bf16), ((4, 16, 256), bf16), ((16, D), bf16),
        ((128, D), bf16), ((128, D), bf16), ((32, 2 * BLOCK, 128), bf16), ((32, BLOCK, 128), bf16),
        ((4, D), f32),
    ]
    return staged_call(
        prepare_kernel, "prepare", arrays, "ss" + "v" * 7 + "h" * 9 + "v" * 4,
        [shape + ("v",) for shape in shapes],
        [
            pltpu.VMEM((128, 6912), bf16),
            pltpu.VMEM((16, 1024), bf16),
            pltpu.VMEM((2, 16, 256), bf16),
            pltpu.VMEM((16, 1024), bf16),
            pltpu.VMEM((2, 16, D), bf16),
            pltpu.VMEM((16, D), bf16),
            pltpu.SemaphoreType.DMA((10,)),
        ],
    )


def body(
    layer_input, out_grad, segment_ids, adapter_ids,
    gain_attn_in, gain_attn_out, gain_mlp_in, gain_mlp_out,
    w_query, w_key, w_value, w_out, w_gate, w_up, w_down,
    qkv_adapt_in, q_adapt_out, kv_adapt_out, o_adapt_in, o_adapt_out,
    mlp_adapt_in, mlp_adapt_out, down_adapt_in, down_adapt_out,
):
    me = lax.axis_index("seq").astype(jnp.int32)
    (
        pack_qkv, pack_gu, pack_down, own_marks, segment_rows, segment_column,
        first_qkv, second_q, second_kv, first_o, second_o, first_gu, second_down, ext_gu, ext_down, gains,
    ) = prepare(
        adapter_ids, me.reshape(1), segment_ids, w_query.T, w_key.T, w_value.T, w_gate.T, w_up.T, w_down,
        qkv_adapt_in, q_adapt_out, kv_adapt_out, o_adapt_in, o_adapt_out,
        mlp_adapt_in, mlp_adapt_out, down_adapt_in, down_adapt_out,
        gain_attn_in, gain_attn_out, gain_mlp_in, gain_mlp_out,
    )
    first_qkv = first_qkv.reshape(48, D)
    layer_out, input_grad, all_early, all_late = layer(
        layer_input[0], pack_qkv, w_out, pack_gu, pack_down, segment_rows, segment_column, gains,
        first_qkv, second_q, second_kv, first_o, second_o,
        ext_gu.reshape(4, 4, 2, 2 * BLOCK, 128), ext_down.reshape(4, 4, 2, BLOCK, 128),
        first_gu, second_down, out_grad[0], own_marks,
    )
    *tables, layer_out, input_grad = put_tables(all_early, all_late, layer_out, input_grad)
    return (layer_out[None], input_grad[None], *tables)


def solution(mesh):
    tokens = P("dp", "seq", None)
    columns, rows = P(None, "dp"), P("dp", None)
    placed = (
        (tokens, tokens, P("dp", None), P("dp"))
        + (P(),) * 4
        + (columns, columns, columns, rows, columns, columns, rows)
        + (P(),) * 9
    )
    return jax.shard_map(
        body,
        mesh=mesh,
        in_specs=placed,
        out_specs=(tokens, tokens) + (P(),) * 9,
        check_vma=False,
    )
```

time: 283 us -> 263 us (0.929)
  Pallas kernels: 276 us -> 261 us
  local copies, waits for them, and re-layouts: 4.44 us -> 0 us
    pallas_call x4 -> x2, Pallas kernels: 266 us -> 250 us  [staged_call(): pl.pallas_call(body, out_shape=[jax.ShapeDtypeStruct(shape, dtype) for sh...]
where the time goes in v4:
time: 263 us
  Pallas kernels  261 us (99%)
    pallas_call x2, Pallas kernels, staged_call(): pl.pallas_call(body, out_shape=[jax.ShapeDtypeStruct(shape, dtype) for sh...  250 us
    pallas_call x1, Pallas kernels, put_tables(): pl.pallas_call(tables_kernel, grid=(8,), out_shape=[jax.ShapeDtypeStruct(...  11 us

profile of v4, /device:TPU:1, one launch (start us, length us, event | category | flops | bytes accessed | tf_op | source)
XLA Modules:
  0.0 262.8 jit_solution(3445091363681336223)
XLA Ops:
  1.3 5.8 %prepare.1 = (bf16[48,1152]{1,0:T(8,128)(2,1)}, bf16[128,1152]{1,0:T(8,128)(2,1)}, bf16[64,1152]{1,0:T(8,128)(2,1)}, f32[2,8,128]{2,1,0:T(8,128)}, s32[4,1,256]{...) custom-call(s32[1]{0:T(128)S(6)} %copy.35.refs_0_, ...), custom_call_target="tpu_custom_call" | custom-call | tf_op jit(solution)/shard_map/prepare/pallas_call | solution.py:103
  7.1 244.5 %layer.1 = (bf16[256,1152]{1,0:T(8,128)(2,1)}, bf16[256,1152]{1,0:T(8,128)(2,1)}, bf16[4,4,2,4,3,4,16,128]{7,6,5,4,3,2,1,0:T(8,128)(2,1)}, bf16[4,4,2,4,1,4,16,128]{7,6,5,4,3,2,1,0:T(8,128)(2,1)}) custom-call(bf16[256,1152]{1,0:T(8,128)(2,1)} %bitcast.14, bf16[48,1152]{1,0:T(8,128)(2,1)} %get-tuple-element.42.refs_1_, bf16[32,1152]{1,0:T(8,128)(2,1)} %refs_2_.3, ...), custom_call_target="tpu_custom_call" | custom-call | tf_op jit(solution)/shard_map/layer/pallas_call | solution.py:103
  251.6 11.0 %tables.1 = (f32[8,3,16,1152]{3,2,1,0:T(8,128)}, f32[8,16,1024]{2,1,0:T(8,128)}, f32[8,2,16,256]{3,2,1,0:T(8,128)}, f32[8,16,1024]{2,1,0:T(8,128)}, f32[8,16,115...) custom-call(bf16[4,4,2,4,3,4,16,128]{7,6,5,4,3,2,1,0:T(8,128)(2,1)} , ...), custom_call_target="tpu_custom_call" | custom-call | tf_op jit(solution)/shard_map/tables/pallas_call | solution.py:973

commit v5 on v4

--- a/solution.py
+++ b/solution.py
@@ -128,6 +128,11 @@
     return [at(x, y + k, z, core) for k in (1, 2, 3)] + [at(x, y, z + k, core) for k in (1, 2, 3)]
 
 
+def far_siblings():
+    x, y, z, core = place()
+    return [at(x, y, z + k, 1 - core) for k in (1, 2, 3)]
+
+
 def sibling():
     x, y, z, core = place()
     return at(x, y, z, 1 - core)
@@ -141,9 +146,10 @@
 
 
 class PlaneGather:
-    def __init__(self, own, buffer, send_sem, recv_sem):
+    def __init__(self, own, buffer, send_sem, recv_sem, direct=False):
         self.x, self.y, self.z, self.core = place()
         self.own, self.buffer, self.send, self.recv = own, buffer, send_sem, recv_sem
+        self.direct = direct
 
     def _copy(self, src, dst, slot, peer):
         return remote(src, dst, self.send.at[slot], self.recv.at[slot], peer)
@@ -186,7 +192,7 @@
             self._first(k).wait()
 
         def act(core):
-            for k in (1, 3):
+            for k in (2, 1, 3) if self.direct else (1, 3):
                 self._second(core, k).start()
             self._swap(core, 0).start()
 
@@ -196,15 +202,19 @@
         def act(core):
             for half, k in ((0, 1), (1, 3)):
                 self._second(core, k).wait()
-                self._pass(core, half).start()
+                if not self.direct:
+                    self._pass(core, half).start()
                 self._swap(core, k).start()
 
         self._both(act)
 
     def last(self):
         def act(core):
-            for half in (0, 1):
-                self._pass(core, half).wait()
+            if self.direct:
+                self._second(core, 2).wait()
+            else:
+                for half in (0, 1):
+                    self._pass(core, half).wait()
             self._swap(core, 2).start()
 
         self._both(act)
@@ -254,8 +264,9 @@
         z = lax.rem(self.z + k, 4)
         return self._copy(self.second.at[:, z], self.third.at[k], 2 + k, at(self.x, self.y, z, self.core))
 
-    def _across(self):
-        return self._copy(self.third, self.fourth, 6, sibling())
+    def _other(self, k):
+        z = lax.rem(self.z + k, 4)
+        return self._copy(self.second.at[:, z], self.fourth.at[k], 6 + k, at(self.x, self.y, z, 1 - self.core))
 
     def start(self):
         for k in (2, 1, 3):
@@ -267,15 +278,15 @@
             self._along_y(k).wait()
         for k in (2, 1, 3):
             self._along_z(k).start()
+        for k in (2, 1, 3, 0):
+            self._other(k).start()
         self.third[0] = self.second[:, self.z]
 
     def late(self):
         for k in (1, 3, 2):
             self._along_z(k).wait()
-        self._across().start()
-
-    def finish(self):
-        self._across().wait()
+        for k in (0, 1, 3, 2):
+            self._other(k).wait()
 
     def total(self, marks, out):
         slots = self.first.shape[2]
@@ -347,7 +358,7 @@
     me, y, z, core = place()
     line = seq_peers()
     ahead, _, behind = line
-    greet(line + plane_peers() + [sibling()])
+    greet(line + plane_peers() + far_siblings() + [sibling()])
 
     all_gu, all_down = w_gu.at[:, :, :, :, 0:D], w_down.at[:, :, :, :, 0:D]
     gathers = [
@@ -481,6 +492,10 @@
     m_plane = PlaneExchange(m1, m2, m3, m4, plane_s.at[2], plane_r.at[2])
     g_down.late()
     g_gu.last()
+    token_moves[0].wait()
+    token_moves[4].start()
+    token_moves[1].wait()
+    token_moves[5].start()
     for moving in ext_copies:
         moving.wait()
     g_gu.finish()
@@ -519,7 +534,7 @@
             act_up[part, :, lanes(j)] = (upward * slope).astype(bf16).reshape(shape)
             return 0
 
-        lax.fori_loop(0, 8, step, 0, unroll=2)
+        lax.fori_loop(0, 8, step, 0, unroll=4)
 
     def forward_close(slot, many):
         size = many * ROWS
@@ -550,7 +565,7 @@
             act_gate[part, :, lanes(j)] = up_grad
             return 0
 
-        lax.fori_loop(0, 8, step, 0, unroll=2)
+        lax.fori_loop(0, 8, step, 0, unroll=4)
 
     def backward_close(slot, many):
         size = many * ROWS
@@ -624,14 +639,10 @@
 
     m_plane.start()
     forward_open(0, 1)
-    token_moves[0].wait()
-    token_moves[4].start()
-    token_moves[1].wait()
-    token_moves[5].start()
+    g_down.last()
     token_moves[2].wait()
     token_moves[3].wait()
     forward_open(1, 2)
-    g_down.last()
     token_moves[4].wait()
     token_moves[5].wait()
     forward_open(3, 1)
@@ -698,7 +709,6 @@
         spread_factors()
 
     scatter(6, backward_close, all_factors)
-    m_plane.finish()
     own_sum = mixed_grad[...] + landed[0].astype(f32) + landed[1].astype(f32)
     mixed_grad[...] = out_grad[...].astype(f32) + norm_back(mixed[...], gain_third, own_sum)
 
@@ -778,7 +788,6 @@
 
     e_plane.middle()
     e_plane.late()
-    e_plane.finish()
     e_plane.total(m_plane, early_total)
     early_line[me] = early_total[...].astype(bf16)
     e_spread = LineGather(early_line, spread_s.at[0], spread_r.at[0])
@@ -789,12 +798,6 @@
             kv_own[...] += w_down[shift - 1, 0:2, :, :, 0:512].reshape(ROWS, 512).astype(f32)
 
         pl.when(me + shift < SEQ)(collect)
-
-    e_spread.finish()
-    own_early = pltpu.make_async_copy(early_line, all_early.at[y, z, core], loc.at[0])
-    own_early.start()
-    e_out = PlaneGather(early_line, all_early, out_s.at[0], out_r.at[0])
-    e_out.start()
 
     key_value = kv_own[...].astype(bf16)
     thin = dot_nt(key_value, second_kv[...])
@@ -815,12 +818,15 @@
     late_parts = late.reshape(SEQ, LATE, 16, 128)
     l_line = LineSum(late_parts, late_landed, line_s.at[1], line_r.at[1])
     l_line.start()
+    e_spread.finish()
+    own_early = pltpu.make_async_copy(early_line, all_early.at[y, z, core], loc.at[0])
+    own_early.start()
+    e_out = PlaneGather(early_line, all_early, out_s.at[0], out_r.at[0])
+    e_out.start()
     near[0] = (mixed_grad[...] + norm_back(layer_input[...].astype(f32), gain_first, back)).astype(bf16)
     result = pltpu.make_async_copy(near.at[0], input_grad, loc.at[2])
     result.start()
 
-    own_early.wait()
-    e_out.middle()
     l_line.finish()
     for i in range(16):
         low = jnp.zeros((16, 128), bf16)
@@ -832,9 +838,10 @@
         late_sum[i // 4, i % 4, 0] = low
     l_plane = PlaneExchange(late_sum, l2, l3, l4, plane_s.at[1], plane_r.at[1])
     l_plane.start()
+    own_early.wait()
+    e_out.middle()
     l_plane.middle()
     l_plane.late()
-    l_plane.finish()
     l_plane.total(m_plane, late_total)
     late_line[me] = late_total[...].astype(bf16)
     l_spread = LineGather(late_line, spread_s.at[1], spread_r.at[1])
@@ -843,7 +850,7 @@
     l_spread.finish()
     own_late = pltpu.make_async_copy(late_line, all_late.at[y, z, core], loc.at[1])
     own_late.start()
-    l_out = PlaneGather(late_line, all_late, out_s.at[1], out_r.at[1])
+    l_out = PlaneGather(late_line, all_late, out_s.at[1], out_r.at[1], direct=True)
     l_out.start()
     own_late.wait()
     l_out.middle()
@@ -922,7 +929,7 @@
         + [
             dma((4, 11)), dma((4, 11)), dma((3,)), dma((3,)), dma((6,)), dma((6,)),
             dma((12,)), dma((12,)), dma((6,)), dma((6,)), dma((2, 3)), dma((2, 3)), dma((6,)),
-            dma((3,)), dma((3,)), dma((3, 7)), dma((3, 7)), dma((2, 3)), dma((2, 3)), dma((2, 11)), dma((2, 11)),
+            dma((3,)), dma((3,)), dma((3, 10)), dma((3, 10)), dma((2, 3)), dma((2, 3)), dma((2, 11)), dma((2, 11)),
         ],
         collective_id=1,
     )

time: 263 us -> 256 us (0.973)
  Pallas kernels: 261 us -> 254 us
    pallas_call x2, Pallas kernels: 250 us -> 243 us  [staged_call(): pl.pallas_call(body, out_shape=[jax.ShapeDtypeStruct(shape, dtype) for sh...]
where the time goes in v5:
time: 256 us
  Pallas kernels  254 us (99%)
    pallas_call x2, Pallas kernels, staged_call(): pl.pallas_call(body, out_shape=[jax.ShapeDtypeStruct(shape, dtype) for sh...  243 us
    pallas_call x1, Pallas kernels, put_tables(): pl.pallas_call(tables_kernel, grid=(8,), out_shape=[jax.ShapeDtypeStruct(...  11 us

profile of v5, /device:TPU:1, one launch (start us, length us, event | category | flops | bytes accessed | tf_op | source)
XLA Modules:
  0.0 255.8 jit_solution(12885888024258590425)
XLA Ops:
  1.3 5.8 %prepare.1 = (bf16[48,1152]{1,0:T(8,128)(2,1)}, bf16[128,1152]{1,0:T(8,128)(2,1)}, bf16[64,1152]{1,0:T(8,128)(2,1)}, f32[2,8,128]{2,1,0:T(8,128)}, s32[4,1,256]{...) custom-call(s32[1]{0:T(128)S(6)} %copy.35.refs_0_, ...), custom_call_target="tpu_custom_call" | custom-call | tf_op jit(solution)/shard_map/prepare/pallas_call | solution.py:103
  7.1 237.6 %layer.1 = (bf16[256,1152]{1,0:T(8,128)(2,1)}, bf16[256,1152]{1,0:T(8,128)(2,1)}, bf16[4,4,2,4,3,4,16,128]{7,6,5,4,3,2,1,0:T(8,128)(2,1)}, bf16[4,4,2,4,1,4,16,128]{7,6,5,4,3,2,1,0:T(8,128)(2,1)}) custom-call(bf16[256,1152]{1,0:T(8,128)(2,1)} %bitcast.14, bf16[48,1152]{1,0:T(8,128)(2,1)} %get-tuple-element.42.refs_1_, bf16[32,1152]{1,0:T(8,128)(2,1)} %refs_2_.3, ...), custom_call_target="tpu_custom_call" | custom-call | tf_op jit(solution)/shard_map/layer/pallas_call | solution.py:103
  244.6 11.0 %tables.1 = (f32[8,3,16,1152]{3,2,1,0:T(8,128)}, f32[8,16,1024]{2,1,0:T(8,128)}, f32[8,2,16,256]{3,2,1,0:T(8,128)}, f32[8,16,1024]{2,1,0:T(8,128)}, f32[8,16,115...) custom-call(bf16[4,4,2,4,3,4,16,128]{7,6,5,4,3,2,1,0:T(8,128)(2,1)} , ...), custom_call_target="tpu_custom_call" | custom-call | tf_op jit(solution)/shard_map/tables/pallas_call | solution.py:980

commit v6 on v5

--- a/solution.py
+++ b/solution.py
@@ -362,7 +362,7 @@
 
     all_gu, all_down = w_gu.at[:, :, :, :, 0:D], w_down.at[:, :, :, :, 0:D]
     gathers = [
-        PlaneGather(own, got, sem_s.at[i], sem_r.at[i])
+        PlaneGather(own, got, sem_s.at[i], sem_r.at[i], direct=i < 2)
         for i, (own, got) in enumerate(
             ((pack_qkv, got_qkv), (pack_o, got_o), (pack_gu, all_gu), (pack_down, all_down))
         )

time: 256 us -> 252 us (0.984)
  Pallas kernels: 254 us -> 250 us
    pallas_call x2, Pallas kernels: 243 us -> 239 us  [staged_call(): pl.pallas_call(body, out_shape=[jax.ShapeDtypeStruct(shape, dtype) for sh...]
where the time goes in v6:
time: 252 us; the launch traced here: 251 us
  Pallas kernels  250 us (99%)
    pallas_call x2, Pallas kernels, staged_call(): pl.pallas_call(body, out_shape=[jax.ShapeDtypeStruct(shape, dtype) for sh...  239 us
    pallas_call x1, Pallas kernels, put_tables(): pl.pallas_call(tables_kernel, grid=(8,), out_shape=[jax.ShapeDtypeStruct(...  11 us

profile of v6, /device:TPU:1, one launch (start us, length us, event | category | flops | bytes accessed | tf_op | source)
XLA Modules:
  0.0 251.3 jit_solution(1551111640397727451)
XLA Ops:
  1.3 5.8 %prepare.1 = (bf16[48,1152]{1,0:T(8,128)(2,1)}, bf16[128,1152]{1,0:T(8,128)(2,1)}, bf16[64,1152]{1,0:T(8,128)(2,1)}, f32[2,8,128]{2,1,0:T(8,128)}, s32[4,1,256]{...) custom-call(s32[1]{0:T(128)S(6)} %copy.35.refs_0_, ...), custom_call_target="tpu_custom_call" | custom-call | tf_op jit(solution)/shard_map/prepare/pallas_call | solution.py:103
  7.1 233.0 %layer.1 = (bf16[256,1152]{1,0:T(8,128)(2,1)}, bf16[256,1152]{1,0:T(8,128)(2,1)}, bf16[4,4,2,4,3,4,16,128]{7,6,5,4,3,2,1,0:T(8,128)(2,1)}, bf16[4,4,2,4,1,4,16,128]{7,6,5,4,3,2,1,0:T(8,128)(2,1)}) custom-call(bf16[256,1152]{1,0:T(8,128)(2,1)} %bitcast.14, bf16[48,1152]{1,0:T(8,128)(2,1)} %get-tuple-element.42.refs_1_, bf16[32,1152]{1,0:T(8,128)(2,1)} %refs_2_.3, ...), custom_call_target="tpu_custom_call" | custom-call | tf_op jit(solution)/shard_map/layer/pallas_call | solution.py:103
  240.1 11.0 %tables.1 = (f32[8,3,16,1152]{3,2,1,0:T(8,128)}, f32[8,16,1024]{2,1,0:T(8,128)}, f32[8,2,16,256]{3,2,1,0:T(8,128)}, f32[8,16,1024]{2,1,0:T(8,128)}, f32[8,16,115...) custom-call(bf16[4,4,2,4,3,4,16,128]{7,6,5,4,3,2,1,0:T(8,128)(2,1)} , ...), custom_call_target="tpu_custom_call" | custom-call | tf_op jit(solution)/shard_map/tables/pallas_call | solution.py:980
